TPU v7x, 32 devices: a whole 2x2x4 slice. The times are simulated.
32 devices in a mesh: dp: 8 (over y, x, core), tensor: 4 (over z).
Axes of the slice: x: 2, y: 2, z: 4, core: 2. Of those that a mesh axis runs over, the one named last changes fastest.
Arguments:
- tokens: bfloat16 [23328, 1152], P('dp'), may hold values from -6 to 6
- image_flags: int32 [32], P('dp'), may hold values 0 or 1
- cotangent: bfloat16 [23328, 1152], P('dp'), may hold values from -6 to 6
- gain_one: float32 [1152], replicated, may hold values from 0.25 to 1.75
- shift_one: float32 [1152], replicated, may hold values from -2 to 2
- w_query: float32 [1152, 1152], P('dp', 'tensor'), may hold values from -0.25 to 0.25
- b_query: float32 [1152], P('tensor'), may hold values from -3 to 3
- w_key: float32 [1152, 1152], P('dp', 'tensor'), may hold values from -0.25 to 0.25
- w_value: float32 [1152, 1152], P('dp', 'tensor'), may hold values from -0.1875 to 0.1875
- b_value: float32 [1152], P('tensor'), may hold values from -3 to 3
- w_out: float32 [1152, 1152], P('tensor', 'dp'), may hold values from -0.75 to 0.75
- b_out: float32 [1152], replicated, may hold values from -3 to 3
- gain_two: float32 [1152], replicated, may hold values from 0.25 to 1.75
- shift_two: float32 [1152], replicated, may hold values from -2 to 2
- w_up: float32 [1152, 4304], P('dp', 'tensor'), may hold values from -0.1875 to 0.1875
- b_up: float32 [4304], P('tensor'), may hold values from -3 to 3
- w_down: float32 [4304, 1152], P('tensor', 'dp'), may hold values from -0.125 to 0.125
- b_down: float32 [1152], replicated, may hold values from -3 to 3
Outputs:
- mixed: bfloat16 [23328, 1152], P(('dp', 'tensor'))
- tokens_grad: bfloat16 [23328, 1152], P(('dp', 'tensor'))
- grad_gain_one: float32 [1152], replicated
- grad_shift_one: float32 [1152], replicated
- grad_w_query: float32 [1152, 1152], P('dp', 'tensor')
- grad_b_query: float32 [1152], P('tensor')
- grad_w_key: float32 [1152, 1152], P('dp', 'tensor')
- grad_w_value: float32 [1152, 1152], P('dp', 'tensor')
- grad_b_value: float32 [1152], P('tensor')
- grad_w_out: float32 [1152, 1152], P('tensor', 'dp')
- grad_b_out: float32 [1152], replicated
- grad_gain_two: float32 [1152], replicated
- grad_shift_two: float32 [1152], replicated
- grad_w_up: float32 [1152, 4304], P('dp', 'tensor')
- grad_b_up: float32 [4304], P('tensor')
- grad_w_down: float32 [4304, 1152], P('tensor', 'dp')
- grad_b_down: float32 [1152], replicated
Inputs may be any that keep to these rules, and one draw needn't show every extreme that they name: `image_flags`: 1 marks a real image, 0 a padded empty one.
All inputs are finite; a program needn't handle non-finite values. No bound on the sum of `image_flags` on one device may be relied on, other than what follows from the above.
Results may differ from a plain program's by a relative error of at most 0.014.
The roundings to bfloat16 on the way count: a program that leaves them out, or rounds other values in their place, can miss the bound.
Values may be sent and summed in bfloat16 or wider, within the bound.
No kernel may reach another device: no remote copies, remote signals or barrier semaphores. Data moves between devices by JAX's collectives and lax.ppermute only.
A program may use at most 192 MiB of HBM per device.

v0:
```python
from functools import partial

import jax
import jax.numpy as jnp
from jax import lax
from jax.sharding import PartitionSpec as P

HD = 72


EPSILON = 1e-06


def matmul(left, right):
    return jnp.dot(left, right, preferred_element_type=jnp.float32)


def matmul_tn(left, right):
    return lax.dot_general(
        left, right, (((0,), (0,)), ((), ())), preferred_element_type=jnp.float32
    )


def matmul_nt(left, right):
    return lax.dot_general(
        left, right, (((1,), (1,)), ((), ())), preferred_element_type=jnp.float32
    )


def norm_rows(inputs, gain_vec, shift_vec):
    average = jnp.mean(inputs, axis=-1, keepdims=True)
    centred = inputs - average
    inverse = lax.rsqrt(jnp.mean(centred * centred, axis=-1, keepdims=True) + EPSILON)
    unit_rows = centred * inverse
    return (unit_rows * gain_vec + shift_vec, unit_rows, inverse)


def norm_back(grad_normed, unit_rows, inverse, gain_vec):
    scaled = grad_normed * gain_vec
    return inverse * (
        scaled
        - jnp.mean(scaled, axis=-1, keepdims=True)
        - unit_rows * jnp.mean(scaled * unit_rows, axis=-1, keepdims=True)
    )


def gelu_back(pre_act, grad_hidden):
    return jax.vjp(partial(jax.nn.gelu, approximate=True), pre_act)[1](grad_hidden)[0]


def split_heads(columns, images, head_count):
    seq_len = columns.shape[0] // images
    return (
        columns.reshape(images, seq_len, head_count, HD)
        .transpose(0, 2, 1, 3)
        .reshape(images * head_count, seq_len, HD)
    )


def merge_heads(stacked, images, head_count):
    seq_len = stacked.shape[1]
    return (
        stacked.reshape(images, head_count, seq_len, HD)
        .transpose(0, 2, 1, 3)
        .reshape(images * seq_len, head_count * HD)
    )


def attend(block):
    queries, key_rows, value_rows = block
    scores = matmul_nt(queries, key_rows) * HD ** (-0.5)
    highest = jnp.max(scores, axis=-1, keepdims=True)
    shifted = jnp.exp(scores - highest)
    row_total = jnp.sum(shifted, axis=-1, keepdims=True)
    softmax_rows = (shifted / row_total).astype(jnp.bfloat16)
    mixed_rows = matmul(softmax_rows, value_rows).astype(jnp.bfloat16)
    return (mixed_rows, (highest + jnp.log(row_total))[:, 0])


def attend_back(block):
    queries, key_rows, value_rows, grad_mixed, log_total = block
    score_scale = HD ** (-0.5)
    scores = matmul_nt(queries, key_rows) * score_scale
    softmax_rows = jnp.exp(scores - log_total[:, None])
    grad_values = matmul_tn(softmax_rows.astype(jnp.bfloat16), grad_mixed)
    grad_soft = matmul_nt(grad_mixed, value_rows)
    grad_scores = (
        softmax_rows * (grad_soft - jnp.sum(grad_soft * softmax_rows, axis=-1, keepdims=True))
    ).astype(jnp.bfloat16)
    grad_queries = matmul(grad_scores, key_rows) * score_scale
    grad_keys = matmul_tn(grad_scores, queries) * score_scale
    return (
        grad_queries.astype(jnp.bfloat16),
        grad_keys.astype(jnp.bfloat16),
        grad_values.astype(jnp.bfloat16),
    )


def on_device(
    tokens,
    image_flags,
    cotangent,
    gain_one,
    shift_one,
    w_query,
    b_query,
    w_key,
    w_value,
    b_value,
    w_out,
    b_out,
    gain_two,
    shift_two,
    w_up,
    b_up,
    w_down,
    b_down,
):
    images = image_flags.shape[0]
    head_count = w_query.shape[1] // HD
    all_rows = tokens.shape[0]
    share_rows = all_rows // lax.axis_size("tensor")
    share_start = lax.axis_index("tensor") * share_rows
    flag_rows = jnp.repeat(image_flags.astype(jnp.float32), all_rows // images)[:, None]
    flag_share = lax.dynamic_slice_in_dim(flag_rows, share_start, share_rows, 0)
    attn_full = (
        lax.all_gather(w_query.astype(jnp.bfloat16), "dp", axis=0, tiled=True),
        lax.all_gather(w_key.astype(jnp.bfloat16), "dp", axis=0, tiled=True),
        lax.all_gather(w_value.astype(jnp.bfloat16), "dp", axis=0, tiled=True),
        lax.all_gather(w_out.astype(jnp.bfloat16), "dp", axis=1, tiled=True),
    )
    inputs = tokens.astype(jnp.float32)
    normed_one, unit_one, inverse_one = norm_rows(inputs, gain_one, shift_one)
    normed_one = normed_one.astype(jnp.bfloat16)
    unit_one_share = lax.dynamic_slice_in_dim(unit_one, share_start, share_rows, 0)
    inverse_one_share = lax.dynamic_slice_in_dim(inverse_one, share_start, share_rows, 0)
    queries = (matmul(normed_one, attn_full[0]) + b_query).astype(jnp.bfloat16)
    key_rows = matmul(normed_one, attn_full[1]).astype(jnp.bfloat16)
    value_rows = (matmul(normed_one, attn_full[2]) + b_value).astype(jnp.bfloat16)
    head_queries = split_heads(queries, images, head_count)
    head_keys = split_heads(key_rows, images, head_count)
    head_values = split_heads(value_rows, images, head_count)
    head_mixed, log_total = lax.map(attend, (head_queries, head_keys, head_values))
    mixed_heads = merge_heads(head_mixed, images, head_count)
    mlp_full = (
        lax.all_gather(w_up.astype(jnp.bfloat16), "dp", axis=0, tiled=True),
        lax.all_gather(w_down.astype(jnp.bfloat16), "dp", axis=1, tiled=True),
    )
    attention = lax.psum_scatter(
        matmul(mixed_heads, attn_full[3]), "tensor", scatter_dimension=0, tiled=True
    )
    input_share = lax.dynamic_slice_in_dim(inputs, share_start, share_rows, 0)
    residual = input_share + attention + b_out
    normed_share, unit_two, inverse_two = norm_rows(residual, gain_two, shift_two)
    normed_two = lax.all_gather(normed_share.astype(jnp.bfloat16), "tensor", axis=0, tiled=True)
    pre_act = matmul(normed_two, mlp_full[0]) + b_up
    hidden = jax.nn.gelu(pre_act, approximate=True).astype(jnp.bfloat16)
    feed = lax.psum_scatter(
        matmul(hidden, mlp_full[1]).astype(jnp.bfloat16), "tensor", scatter_dimension=0, tiled=True
    ).astype(jnp.float32)
    mixed = ((residual + feed + b_down) * flag_share).astype(jnp.bfloat16)
    grad_out = cotangent.astype(jnp.float32) * flag_rows
    grad_out_share = lax.dynamic_slice_in_dim(grad_out, share_start, share_rows, 0)
    grad_feed = grad_out.astype(jnp.bfloat16)
    grad_b_down = jnp.sum(grad_out, axis=0)
    local_w_down = matmul_tn(hidden, grad_feed)
    grad_pre = gelu_back(pre_act, matmul_nt(grad_feed, mlp_full[1])).astype(jnp.bfloat16)
    grad_b_up = jnp.sum(grad_pre.astype(jnp.float32), axis=0)
    local_w_up = matmul_tn(normed_two, grad_pre)
    grad_w_up, grad_w_down = (local_w_up, local_w_down)
    grad_normed_two = lax.psum_scatter(
        matmul_nt(grad_pre, mlp_full[0]), "tensor", scatter_dimension=0, tiled=True
    )
    grad_gain_two = jnp.sum(grad_normed_two * unit_two, axis=0)
    grad_shift_two = jnp.sum(grad_normed_two, axis=0)
    grad_resid = grad_out_share + norm_back(grad_normed_two, unit_two, inverse_two, gain_two)
    grad_b_out = jnp.sum(grad_resid, axis=0)
    grad_attention = lax.all_gather(grad_resid.astype(jnp.bfloat16), "tensor", axis=0, tiled=True)
    local_w_out = matmul_tn(mixed_heads, grad_attention)
    grad_mixed = matmul_nt(grad_attention, attn_full[3]).astype(jnp.bfloat16)
    grad_q_heads, grad_k_heads, grad_v_heads = lax.map(
        attend_back,
        (
            head_queries,
            head_keys,
            head_values,
            split_heads(grad_mixed, images, head_count),
            log_total,
        ),
    )
    grad_queries = merge_heads(grad_q_heads, images, head_count)
    grad_keys = merge_heads(grad_k_heads, images, head_count)
    grad_values = merge_heads(grad_v_heads, images, head_count)
    grad_b_query = jnp.sum(grad_queries.astype(jnp.float32), axis=0)
    grad_b_value = jnp.sum(grad_values.astype(jnp.float32), axis=0)
    local_w_query = matmul_tn(normed_one, grad_queries)
    local_w_key = matmul_tn(normed_one, grad_keys)
    local_w_value = matmul_tn(normed_one, grad_values)
    partial_one = (
        matmul_nt(grad_queries, attn_full[0])
        + matmul_nt(grad_keys, attn_full[1])
        + matmul_nt(grad_values, attn_full[2])
    )
    grad_normed_one = lax.psum_scatter(partial_one, "tensor", scatter_dimension=0, tiled=True)
    grad_gain_one = jnp.sum(grad_normed_one * unit_one_share, axis=0)
    grad_shift_one = jnp.sum(grad_normed_one, axis=0)
    tokens_grad = (
        grad_resid + norm_back(grad_normed_one, unit_one_share, inverse_one_share, gain_one)
    ).astype(jnp.bfloat16)
    grad_w_query, grad_w_key, grad_w_value, grad_w_out, grad_w_up, grad_w_down = (
        lax.psum_scatter(local_w_query, "dp", scatter_dimension=0, tiled=True),
        lax.psum_scatter(local_w_key, "dp", scatter_dimension=0, tiled=True),
        lax.psum_scatter(local_w_value, "dp", scatter_dimension=0, tiled=True),
        lax.psum_scatter(local_w_out, "dp", scatter_dimension=1, tiled=True),
        lax.psum_scatter(local_w_up, "dp", scatter_dimension=0, tiled=True),
        lax.psum_scatter(local_w_down, "dp", scatter_dimension=1, tiled=True),
    )
    small_sums = lax.psum((grad_b_query, grad_b_value, grad_b_up, grad_b_down), "dp")
    row_sums = lax.psum(
        (grad_gain_one, grad_shift_one, grad_b_out, grad_gain_two, grad_shift_two), ("dp", "tensor")
    )
    return (
        mixed,
        tokens_grad,
        row_sums[0],
        row_sums[1],
        grad_w_query,
        small_sums[0],
        grad_w_key,
        grad_w_value,
        small_sums[1],
        grad_w_out,
        row_sums[2],
        row_sums[3],
        row_sums[4],
        grad_w_up,
        small_sums[2],
        grad_w_down,
        small_sums[3],
    )


def solution(mesh):
    return jax.shard_map(
        on_device,
        mesh=mesh,
        in_specs=(
            P("dp", None),
            P("dp"),
            P("dp", None),
            P(),
            P(),
            P("dp", "tensor"),
            P("tensor"),
            P("dp", "tensor"),
            P("dp", "tensor"),
            P("tensor"),
            P("tensor", "dp"),
            P(),
            P(),
            P(),
            P("dp", "tensor"),
            P("tensor"),
            P("tensor", "dp"),
            P(),
        ),
        out_specs=(
            P(("dp", "tensor"), None),
            P(("dp", "tensor"), None),
            P(),
            P(),
            P("dp", "tensor"),
            P("tensor"),
            P("dp", "tensor"),
            P("dp", "tensor"),
            P("tensor"),
            P("tensor", "dp"),
            P(),
            P(),
            P(),
            P("dp", "tensor"),
            P("tensor"),
            P("tensor", "dp"),
            P(),
        ),
        check_vma=False,
    )
```

profile of v0, /device:TPU:0, one launch (start us, length us, event | category | flops | bytes accessed | tf_op | source)
XLA Modules:
  0.0 1818.1 jit_solution(7127341817444744375)
XLA Ops:
  14.0 12.1 all_gather.24
  44.1 10.9 all_gather.25
  67.8 9.7 all_gather.26
  91.7 87.4 %while.26 = (s32[]{:T(128)}, bf16[16,729,72]{1,2,0:T(8,128)(2,1)}, f32[16,729]{1,0:T(8,128)}, bf16[16,729,72]{2,1,0:T(8,128)(2,1)}, bf16[16,729,72]{2,1,0:T(8,12...) while((s32[]{:T(128)}, bf16[16,729,72]{1,2,0:T(8,128)(2,1)}, f32[16,729]{1,0:T(8,128)}, ...), condition=%wide.region_5.6_spmd, body=%wide.region_2.5_spmd.sunk | while | flops 157889728 | bytes 7090261 | solution.py:143
  184.6 10.7 all_gather.27
  203.3 232.5 %fusion = f32[736,1152]{1,0:T(8,128)S(1)} fusion(f32[2916,1152]{1,0:T(8,128)} %fusion.67), kind=kCustom, calls=%all-reduce-scatter | all-reduce-scatter fusion | flops 3391489 | bytes 16828928
  435.8 13.4 collective-permute-start
  449.3 8.6 convert_element_type.101
  459.2 9.7 concatenate
  479.4 116.7 %all-gather.11.cloned.1.call-done = bf16[4,729,1152]{2,1,0:T(8,128)(2,1)} async-done(((bf16[1,729,1152]{2,1,0:T(8,128)(2,1)}), bf16[4,729,1152]{2,1,0:T(8,128)(2,1)}) %all-gather.11.cloned.1.call-update) | async-done | bytes 6718480 | tf_op jit(solution)/shard_map/all_gather | solution.py:155
  603.4 23.6 %all-gather.7.cloned.1.call-done = bf16[1152,1076]{1,0:T(8,128)(2,1)} async-done(((bf16[144,1076]{1,0:T(8,128)(2,1)}), bf16[1152,1076]{1,0:T(8,128)(2,1)}) %all-gather.7.cloned.1.call-update) | async-done | bytes 2479120 | tf_op jit(solution)/shard_map/all_gather | solution.py:146
  627.0 14.5 convolution_add_fusion.2
  641.5 18.3 %all-gather.9.cloned.1.call-done = bf16[1076,1152]{0,1:T(8,128)(2,1)} async-done(((bf16[1076,144]{0,1:T(8,128)(2,1)}), bf16[1076,1152]{0,1:T(8,128)(2,1)}) %all-gather.9.cloned.1.call-update) | async-done | bytes 2479120 | tf_op jit(solution)/shard_map/all_gather | solution.py:147
  659.8 18.8 %convolution_convert_fusion.2 = bf16[2916,1152]{1,0:T(8,128)(2,1)} fusion(bf16[1076,1152]{0,1:T(8,128)(2,1)} %all-gather.9.cloned.1.call-done, f32[2916,1076]{0,1:T(8,128)} %convolution_add_fusion.2), kind=kOutput, calls=%fused_computation.72 | convolution fusion | flops 7260664832 | bytes 21748032 | tf_op jit(solution)/shard_map/dot_general | solution.py:15
  678.6 121.6 %fusion.1 = bf16[736,1152]{1,0:T(8,128)(2,1)} fusion(bf16[2916,1152]{1,0:T(8,128)(2,1)} %convolution_convert_fusion.2), kind=kCustom, calls=%all-reduce-scatter.1 | all-reduce-scatter fusion | flops 3391489 | bytes 8414720
  803.8 23.0 %convert_reduce_fusion = (f32[1076]{0:T(1024)}, bf16[2916,1076]{0,1:T(8,128)(2,1)S(1)}) fusion(f32[2916,1076]{0,1:T(8,128)} %convolution_add_fusion.2, bf16[1076,1152]{0,1:T(8,128)(2,1)} %all-gather.9.cloned.1.call-done, f32[2916]{0:T(1024)S(1)} %mul.200, bf16[2916,1152]{1,0:T(8,128)(2,1)} %param.24), kind=kOutput, calls=%fused_computation.69 | convolution fusion | flops 7308169728 | bytes 28039232 | tf_op jit(solution)/shard_map/dot_general | solution.py:25
  829.5 12.9 fusion.68
  842.4 227.4 %fusion.2 = f32[736,1152]{1,0:T(8,128)} fusion(f32[2916,1152]{1,0:T(8,128)} %fusion.68), kind=kCustom, calls=%all-reduce-scatter.2 | all-reduce-scatter fusion | flops 3391489 | bytes 16828928
  1072.7 9.7 fusion.63
  1082.6 10.9 concatenate.1
  1093.6 11.3 concatenate.2
  1118.3 14.5 fusion.74
  1133.7 18.7 %fusion.56 = f32[1076,1152]{0,1:T(8,128)} fusion(bf16[2916,1152]{1,0:T(8,128)(2,1)} %param.24, f32[2916]{0:T(1024)S(1)} %mul.200, f32[2916,1076]{0,1:T(8,128)} %convolution_add_fusion.2), kind=kOutput, calls=%fused_computation.93 | convolution fusion | flops 7267383296 | bytes 24238800 | tf_op jit(solution)/shard_map/dot_general | solution.py:19
  1152.5 86.6 %all-gather.13.cloned.1.call-done = bf16[4,729,1152]{2,1,0:T(8,128)(2,1)} async-done(((bf16[1,729,1152]{2,1,0:T(8,128)(2,1)}), bf16[4,729,1152]{2,1,0:T(8,128)(2,1)}) %all-gather.13.cloned.1.call-update) | async-done | bytes 6718480 | tf_op jit(solution)/shard_map/all_gather | solution.py:178
  1260.7 143.6 %while.27 = (s32[]{:T(128)}, bf16[16,729,72]{1,2,0:T(8,128)(2,1)S(1)}, bf16[16,729,72]{1,2,0:T(8,128)(2,1)}, bf16[16,729,72]{1,2,0:T(8,128)(2,1)S(1)}, bf16[16,7...) while((s32[]{:T(128)}, ...), condition=%wide.region_15.16_spmd, body=%wide.region_13.15_spmd.sunk | while | flops 387150720 | bytes 17816564 | solution.py:181
  1426.9 8.5 fusion.73
  1435.5 10.9 fusion.69
  1462.6 10.0 convolution_add_fusion.1
  1480.1 229.1 %fusion.3 = f32[736,1152]{1,0:T(8,128)} fusion(f32[2916,1152]{1,0:T(8,128)} %convolution_add_fusion), kind=kCustom, calls=%all-reduce-scatter.3 | all-reduce-scatter fusion | flops 3391489 | bytes 16828928
  1727.2 23.3 %all-reduce.9 = (f32[288]{0:T(512)}, f32[288]{0:T(512)}, f32[1076]{0:T(1024)}, f32[1152]{0:T(1024)}) all-reduce(f32[288]{0:T(512)S(1)} %reduce_sum.186, f32[288]{0:T(512)S(1)} %reduce_sum.188, f32[1076]{0:T(1024)} %get-tuple-element.164, f32[1152]{0:T(1024)S(1)} %copy-done.25), channel_id=1, replica_groups=mesh['dp'=8,'tensor'=4] {'dp'}, use_global_device_ids=true, to_apply=%region_25.26 | all-reduce | flops 2804 | bytes 22432 | tf_op jit(solution)/shard_map/psum | solution.py:218
  1750.5 11.4 concatenate.3
  1766.6 38.7 %all-reduce.8 = (f32[1152]{0:T(1024)}, f32[1152]{0:T(1024)}, f32[1152]{0:T(1024)}, f32[1152]{0:T(1024)}, f32[1152]{0:T(1024)}) all-reduce(f32[1152]{0:T(1024)S(1)} %get-tuple-element.104, f32[1152]{0:T(1024)S(1)} %get-tuple-element.111, f32[1152]{0:T(1024)S(1)} %copy-done.22, ...), channel_id=1, replica_groups=mesh['dp'=8,'tensor'=4] {'dp','tensor'}, use_global_device_ids=true, to_apply=%region_20.21 | all-reduce | flops 5760 | bytes 46080 | tf_op jit(solution)/shard_map/psum | solution.py:219
  (386 shorter events, 432.9 us)
Async XLA Ops:
  7.2 588.9 %all-gather.11.cloned.1.call-start = ((), (), s32[]{:S(2)}) async-start(), calls=%async_computation.14 | async-start | bytes 8478720 | tf_op jit(solution)/shard_map/all_gather | solution.py:155
  7.2 4.8 copy-start
  12.1 14.1 copy-start.19
  12.1 14.1 copy-start.27
  14.0 18.4 %copy-start.21 = (f32[2916]{0:T(1024)}, f32[2916]{0:T(1024)S(1)}, u32[]{:S(2)}) copy-start(f32[2916]{0:T(1024)S(1)} %add_rsqrt_fusion) | copy-start | bytes 34996
  26.2 6.2 copy-start.12
  26.2 8.9 copy-start.33
  64.0 14.5 copy-start.34
  183.4 11.9 copy-start.5
  435.8 23.3 %collective-permute-start = (f32[21,1152]{1,0:T(8,128)S(1)}, f32[21,1152]{1,0:T(8,128)}, u32[]{:S(2)}, u32[]{:S(2)}) collective-permute-start(f32[21,1152]{1,0:T(8,128)S(1)} %slice), channel_id=1, source_target_pairs={{0,1},{1,2},{2,3},{4,5},{5,6},{6,7},{8,9},{9,10},{10,11},{12,13},{... | collective-permute-start | bytes 290312
  449.3 8.6 copy-start.30
  459.1 9.7 copy-start.28
  475.3 151.7 %all-gather.7.cloned.1.call-start = ((), (), s32[]{:S(2)}) async-start(), calls=%async_computation.6 | async-start | bytes 2985984 | tf_op jit(solution)/shard_map/all_gather | solution.py:146
  477.2 182.6 %all-gather.9.cloned.1.call-start = ((), (), s32[]{:S(2)}) async-start(), calls=%async_computation.7 | async-start | bytes 2985984 | tf_op jit(solution)/shard_map/all_gather | solution.py:147
  479.2 759.9 %all-gather.13.cloned.1.call-start = ((), (), s32[]{:S(2)}) async-start(), calls=%async_computation.15 | async-start | bytes 8478720 | tf_op jit(solution)/shard_map/all_gather | solution.py:178
  479.4 147.7 %copy-start.32 = (f32[1076]{0:T(1024)S(1)}, f32[1076]{0:T(1024)}, u32[]{:S(2)}) copy-start(f32[1076]{0:T(1024)} %param.37) | copy-start | bytes 12916
  801.7 27.8 %copy-start.31 = (bf16[1152,1076]{1,0:T(8,128)(2,1)S(1)}, bf16[1152,1076]{1,0:T(8,128)(2,1)}, u32[]{:S(2)}) copy-start(bf16[1152,1076]{1,0:T(8,128)(2,1)} %all-gather.7.cloned.1.call-done) | copy-start | bytes 7437316
  801.7 280.9 %collective-permute-start.1 = (bf16[21,1152]{1,0:T(8,128)(2,1)}, bf16[21,1152]{1,0:T(8,128)(2,1)}, u32[]{:S(2)}, u32[]{:S(2)}) collective-permute-start(bf16[21,1152]{1,0:T(8,128)(2,1)} %slice.1), channel_id=1, source_target_pairs={{0,1},{1,2},{2,3},{4,5},{5,6},{6,7},{8,9},{9,10},{10,11},{12,13},{... | collective-permute-start | bytes 145160
  1070.7 22.9 %collective-permute-start.2 = (f32[21,1152]{1,0:T(8,128)S(1)}, f32[21,1152]{1,0:T(8,128)}, u32[]{:S(2)}, u32[]{:S(2)}) collective-permute-start(f32[21,1152]{1,0:T(8,128)S(1)} %slice.2), channel_id=1, source_target_pairs={{0,1},{1,2},{2,3},{4,5},{5,6},{6,7},{8,9},{9,10},{10,11},{12,13},{... | collective-permute-start | bytes 290312
  1118.3 692.4 %reduce-scatter.23.cloned.1.call-start = ((), (), s32[]{:S(2)}) async-start(), calls=%async_computation.12 | async-start | bytes 5971968 | tf_op jit(solution)/shard_map/reduce_scatter | solution.py:215
  1132.9 677.8 %reduce-scatter.25.cloned.1.call-start = ((), (), s32[]{:S(2)}) async-start(), calls=%async_computation.13 | async-start | bytes 5971968 | tf_op jit(solution)/shard_map/reduce_scatter | solution.py:216
  1152.4 94.1 %copy-start.14 = (bf16[288,1152]{0,1:T(8,128)(2,1)S(1)}, bf16[288,1152]{0,1:T(8,128)(2,1)}, u32[]{:S(2)}) copy-start(bf16[288,1152]{0,1:T(8,128)(2,1)} %copy-done.13) | copy-start | bytes 1990660
  1152.4 658.3 %reduce-scatter.21.cloned.1.call-start = ((), (), s32[]{:S(2)}) async-start(), calls=%async_computation.11 | async-start | bytes 1990656 | tf_op jit(solution)/shard_map/reduce_scatter | solution.py:214
  1435.4 375.3 %reduce-scatter.15.cloned.1.call-start = ((), (), s32[]{:S(2)}) async-start(), calls=%async_computation.8 | async-start | bytes 1990656 | tf_op jit(solution)/shard_map/reduce_scatter | solution.py:211
  1435.5 10.9 copy-start.6
  1462.5 348.2 %reduce-scatter.17.cloned.1.call-start = ((), (), s32[]{:S(2)}) async-start(), calls=%async_computation.9 | async-start | bytes 1990656 | tf_op jit(solution)/shard_map/reduce_scatter | solution.py:212
  1462.5 10.0 copy-start.4
  1462.6 10.0 copy-start.11
  1480.1 330.7 %reduce-scatter.19.cloned.1.call-start = ((), (), s32[]{:S(2)}) async-start(), calls=%async_computation.10 | async-start | bytes 1990656 | tf_op jit(solution)/shard_map/reduce_scatter | solution.py:213
  1710.8 39.7 %collective-permute-start.3 = (f32[21,1152]{1,0:T(8,128)}, f32[21,1152]{1,0:T(8,128)}, u32[]{:S(2)}, u32[]{:S(2)}) collective-permute-start(f32[21,1152]{1,0:T(8,128)} %slice.3), channel_id=1, source_target_pairs={{0,1},{1,2},{2,3},{4,5},{5,6},{6,7},{8,9},{9,10},{10,11},{12,13},{... | collective-permute-start | bytes 290312
  1750.5 11.4 copy-start.20
  1761.9 43.4 %copy-start.2 = (f32[729,1152]{1,0:T(8,128)S(1)}, f32[729,1152]{1,0:T(8,128)}, u32[]{:S(2)}) copy-start(f32[729,1152]{1,0:T(8,128)} %copy-done.1) | copy-start | bytes 10077700
  (19 other events, 55.0 us)
Sparse Core Ops, SparseCore 0:
  475.4 120.6 all-gather.10
  598.5 28.4 all-gather.6
  629.5 30.2 all-gather.8
  1118.4 120.6 all-gather.12
  1242.9 55.1 reduce-scatter.22
  1302.3 56.9 reduce-scatter.24
  1435.5 37.6 reduce-scatter.20
  1477.1 39.4 reduce-scatter.14
  1520.5 39.3 reduce-scatter.16
  1724.1 37.4 reduce-scatter.18
where the time goes:
time: 1830 us; the launch traced here: 1820 us
  blocking collectives  916 us (50%)
  matrix products  374 us (20%)
  waiting for transfers between devices  245 us (13%)
  local copies, waits for them, and re-layouts  165 us (9%)
  other arithmetic  78.4 us (4%)
  starting transfers between devices  22.8 us (1%)
    unnamed x4, blocking collectives  811 us
    dot_general x54, matrix products, matmul_nt(): lax.dot_general(left, right, (((1,), (1,)), ((), ())), preferred_element_...  142 us
    dot_general x38, matrix products, matmul_tn(): lax.dot_general(left, right, (((0,), (0,)), ((), ())), preferred_element_...  123 us
    all_gather x1, waiting for transfers between devices, on_device(): lax.all_gather(normed_share.astype(jnp.bfloat16), 'tensor', axis=0, tiled...  117 us
    dot_general x38, matrix products, matmul(): return jnp.dot(left, right, preferred_element_type=jnp.float32)  109 us
    all_gather x1, waiting for transfers between devices, on_device(): lax.all_gather(grad_resid.astype(jnp.bfloat16), 'tensor', axis=0, tiled=T...  86.6 us
    unnamed x85, local copies, waits for them, and re-layouts  73.8 us
    psum x1, blocking collectives, on_device(): lax.psum((grad_gain_one, grad_shift_one, grad_b_out, grad_gain_two, grad_...  38.7 us
  transfers between devices with their start and end apart: 14, of which 4 were waited for; matrix products, arithmetic and copies ran while one was open for 47% of the time, Pallas kernels for 0%

commit v1 on v0

v1 whole, which is shorter than its diff:
```python
from functools import partial

import jax
import jax.numpy as jnp
from jax import lax
from jax.experimental import pallas as pl
from jax.experimental.pallas import tpu as pltpu
from jax.sharding import PartitionSpec as P

HD = 72
LANES = 128
EPSILON = 1e-06
SCALE = HD**-0.5
SHARP = SCALE * 1.4426950408889634
GELU_A = 0.7978845608028654
GELU_B = 0.044715
BF = jnp.bfloat16
F32 = jnp.float32
VMEM_BYTES = 40 * 2**20
ANY = pl.BlockSpec(memory_space=pl.ANY)
SMEM = pl.BlockSpec(memory_space=pltpu.SMEM)
VMEM = pl.BlockSpec(memory_space=pltpu.VMEM)


def up(value, step):
    return -(-value // step) * step


def nn(left, right):
    return lax.dot_general(left, right, (((1,), (0,)), ((), ())), preferred_element_type=F32)


def nt(left, right):
    return lax.dot_general(left, right, (((1,), (1,)), ((), ())), preferred_element_type=F32)


def call(kernel, name, us, place, weights, after, ins, outs, scratch, aliases=()):
    weights, after = list(weights), list(after)
    lead = 1 + len(weights) + len(after)

    def body(*refs):
        kernel(refs[0], refs[1 : 1 + len(weights)], *refs[lead:])

    return pl.pallas_call(
        body,
        in_specs=[SMEM] + [ANY] * (lead - 1) + [VMEM] * len(ins),
        out_specs=[VMEM] * len(outs),
        out_shape=[jax.ShapeDtypeStruct(*out) for out in outs],
        scratch_shapes=scratch,
        input_output_aliases={lead + i: o for i, o in aliases},
        compiler_params=pltpu.CompilerParams(vmem_limit_bytes=VMEM_BYTES),
        cost_estimate=pl.CostEstimate(
            flops=int(us * 1.15e9), bytes_accessed=int(us * 1e5), transcendentals=0
        ),
        name=name,
    )(place, *weights, *after, *ins)


class Piece:
    def __init__(self, arrays, blocks):
        self.arrays, self.blocks = arrays, blocks

    def fetch(self, refs, place_ref, buffer, sem):
        for array, lead, first, rows in self.blocks(place_ref[0], place_ref[1]):
            pltpu.make_async_copy(
                refs[array].at[lead], buffer.at[pl.ds(first, rows), :], sem
            ).start()


def landed(buffer, sem):
    pltpu.make_async_copy(buffer, buffer, sem).wait()


def turn(cfg, d, value, out_ref, scratch):
    rows, order = cfg["rows"], cfg["order"]
    if order is None:
        out_ref[...] = value.T
        return
    scratch[...] = value.T
    for place, offset in enumerate(order):
        first = pl.multiple_of(jnp.bitwise_xor(d, offset) * rows, 16)
        out_ref[place * rows : (place + 1) * rows, :] = scratch[pl.ds(first, rows), :]


STEP = 32


def over_rows(total, body, carry):
    def step(t, carry):
        return body(pl.ds(pl.multiple_of(t * STEP, STEP), STEP), carry)

    return lax.fori_loop(0, total // STEP, step, carry)


def norm_stats(rows):
    average = jnp.mean(rows, axis=-1, keepdims=True)
    centred = rows - average
    inverse = lax.rsqrt(jnp.mean(centred * centred, axis=-1, keepdims=True) + EPSILON)
    return centred * inverse, inverse


def fold(value):
    return jnp.sum(value.reshape(STEP // 8, 8, value.shape[1]), axis=0)


def total_of(partial_sums):
    return jnp.sum(partial_sums, axis=0, keepdims=True)


def norm_one_kernel(
    cfg, place_ref, _, x_ref, eb_ref, gain_ref, shift_ref, a_ref, at_ref, et_ref, sum_ref, scratch
):
    def rows_of(rows, carry):
        unit, _ = norm_stats(x_ref[rows, :].astype(F32))
        a_ref[rows, :] = (unit * gain_ref[...] + shift_ref[...]).astype(BF)
        return carry + fold(eb_ref[rows, :].astype(F32))

    m, dim = x_ref.shape
    sum_ref[...] = total_of(over_rows(m, rows_of, jnp.zeros((8, dim), F32)))
    turn(cfg, place_ref[0], a_ref[...], at_ref, scratch)
    turn(cfg, place_ref[0], eb_ref[...], et_ref, scratch)


def norm_one(cfg, place, x, eb, gain, shift):
    m, d = x.shape
    outs = [((m, d), BF), ((d, m), BF), ((d, m), BF), ((1, d), F32)]
    return call(
        partial(norm_one_kernel, cfg), "norm_one", 6, place, [], [], [x, eb, gain, shift], outs,
        [pltpu.VMEM((d, m), BF)],
    )


def norm_two_kernel(
    cfg, place_ref, _, x_ref, att_ref, b_out, gain, shift, h_ref, a_ref, at_ref, scratch
):
    def rows_of(rows, carry):
        h = x_ref[rows, :].astype(F32) + att_ref[rows, :] + b_out[...]
        h_ref[rows, :] = h
        unit, _ = norm_stats(h)
        a_ref[rows, :] = (unit * gain[...] + shift[...]).astype(BF)
        return carry

    over_rows(x_ref.shape[0], rows_of, 0)
    turn(cfg, place_ref[0], a_ref[...], at_ref, scratch)


def norm_two(cfg, place, after, x, att, b_out, gain, shift):
    m, d = x.shape
    outs = [((m, d), F32), ((m, d), BF), ((d, m), BF)]
    return call(
        partial(norm_two_kernel, cfg), "norm_two", 6, place, [], after,
        [x, att, b_out, gain, shift], outs, [pltpu.VMEM((d, m), BF)],
    )


def norm_two_back_kernel(
    cfg, place_ref, _, h_ref, feed_ref, dn_ref, eb_ref, b_down, gain,
    mixed_ref, dh_ref, dhb_ref, dht_ref, vec_ref, scratch,
):
    flag = place_ref[2].astype(F32)

    def rows_of(rows, carry):
        h = h_ref[rows, :]
        mixed_ref[rows, :] = ((h + feed_ref[rows, :] + b_down[...]) * flag).astype(BF)
        unit, inverse = norm_stats(h)
        grad = dn_ref[rows, :]
        scaled = grad * gain[...]
        dh = eb_ref[rows, :].astype(F32) + inverse * (
            scaled
            - jnp.mean(scaled, axis=-1, keepdims=True)
            - unit * jnp.mean(scaled * unit, axis=-1, keepdims=True)
        )
        dh_ref[rows, :] = dh
        dhb_ref[rows, :] = dh.astype(BF)
        return carry[0] + fold(grad * unit), carry[1] + fold(grad), carry[2] + fold(dh)

    m, dim = h_ref.shape
    zero = jnp.zeros((8, dim), F32)
    sums = over_rows(m, rows_of, (zero, zero, zero))
    for i, value in enumerate(sums):
        vec_ref[i : i + 1, :] = total_of(value)
    turn(cfg, place_ref[0], dhb_ref[...], dht_ref, scratch)


def norm_two_back(cfg, place, after, h, feed, dn, eb, b_down, gain):
    m, d = h.shape
    outs = [((m, d), BF), ((m, d), F32), ((m, d), BF), ((d, m), BF), ((3, d), F32)]
    return call(
        partial(norm_two_back_kernel, cfg), "norm_two_back", 10, place, [], after,
        [h, feed, dn, eb, b_down, gain], outs, [pltpu.VMEM((d, m), BF)],
    )


def norm_back_kernel(place_ref, _, x_ref, dn_ref, dh_ref, gain, out_ref, vec_ref):
    def rows_of(rows, carry):
        unit, inverse = norm_stats(x_ref[rows, :].astype(F32))
        grad = dn_ref[rows, :]
        scaled = grad * gain[...]
        out = dh_ref[rows, :] + inverse * (
            scaled
            - jnp.mean(scaled, axis=-1, keepdims=True)
            - unit * jnp.mean(scaled * unit, axis=-1, keepdims=True)
        )
        out_ref[rows, :] = out.astype(BF)
        return carry[0] + fold(grad * unit), carry[1] + fold(grad)

    m, dim = x_ref.shape
    zero = jnp.zeros((8, dim), F32)
    for i, value in enumerate(over_rows(m, rows_of, (zero, zero))):
        vec_ref[i : i + 1, :] = total_of(value)


def norm_back(place, after, x, dn, dh, gain):
    m, d = x.shape
    outs = [((m, d), BF), ((2, d), F32)]
    return call(
        norm_back_kernel, "norm_back", 8, place, [], after, [x, dn, dh, gain], outs, []
    )


def pad_heads(cfg, refs):
    m, seq = cfg["m"], cfg["seq"]
    lane = lax.broadcasted_iota(jnp.int32, (m, LANES - HD), 1)
    row = lax.broadcasted_iota(jnp.int32, (m, LANES - HD), 0)
    one = jnp.where(lane == 0, 1.0, 0.0).astype(BF)
    past = jnp.where((lane == 0) & (row >= seq), -1e30, 0.0).astype(BF)
    for h in range(cfg["heads"]):
        for ref, fill in zip(refs, (one, past, one)):
            ref[h, :, HD:] = fill


def attn_fwd_kernel(cfg, piece, begin, place_ref, w_refs, a_ref, bias_ref, *refs):
    if not begin:
        acc_in, *refs = refs
    qkv_ref, o_ref, lse_ref, acc_ref, w, q_s, k_s, v_s, vt, ot, sem = refs
    m, heads, base, wide = cfg["m"], cfg["heads"], cfg["base"], cfg["wide"]
    piece.fetch(w_refs, place_ref, w, sem)
    pad_heads(cfg, (q_s, k_s, v_s))
    ot[...] = jnp.zeros_like(ot)
    lse_ref[...] = jnp.zeros_like(lse_ref)
    landed(w, sem)
    qkv_ref[...] = (nn(a_ref[...], w[:, base:]) + bias_ref[...]).astype(BF)
    span = heads * HD
    skip = span - base
    for h in range(heads):
        for n, s in enumerate((q_s, k_s, v_s)):
            at = skip + n * span + h * HD
            s[h, :, :HD] = qkv_ref[:, at : at + HD]
        vt[h] = v_s[h].T
        s = nt(k_s[h], q_s[h])
        highest = jnp.max(s, axis=0, keepdims=True) * SHARP
        p = jnp.exp2(s * SHARP - highest).astype(BF)
        mixed = nn(vt[h], p)
        total = mixed[HD : HD + 1, :]
        ot[h * HD : (h + 1) * HD, :] = mixed[:HD, :] * (1.0 / total)
        lse_ref[h : h + 1, :] = highest + jnp.log2(total)
    o_ref[...] = ot[...].T.astype(BF)
    part = nt(o_ref[...], w[:, :wide])
    acc_ref[...] = part if begin else acc_in[...] + part


def attn_fwd(cfg, place, after, piece, a, bias, acc):
    m, dim = a.shape
    qw, wide, heads, width = cfg["qw"], cfg["wide"], cfg["heads"], cfg["width"]
    begin = acc is None
    outs = [((m, qw), BF), ((m, wide), BF), ((8, m), F32), ((m, dim), F32)]
    scratch = (
        [pltpu.VMEM((dim, width), BF)]
        + [pltpu.VMEM((heads, m, LANES), BF)] * 3
        + [
            pltpu.VMEM((heads, LANES, m), BF),
            pltpu.VMEM((wide, m), F32),
            pltpu.SemaphoreType.DMA,
        ]
    )
    return call(
        partial(attn_fwd_kernel, cfg, piece, begin), "attn_fwd", 10, place, piece.arrays, after,
        [a, bias] + ([] if begin else [acc]), outs, scratch, () if begin else ((2, 3),),
    )


def attn_bwd_kernel(cfg, piece, begin, place_ref, w_refs, *refs):
    at_ref, dh_ref, dht_ref, qkv_ref, o_ref, lse_ref, *refs = refs
    if not begin:
        acc_in, *refs = refs
    ga_ref, gb_ref, sum_ref, acc_ref, *refs = refs
    w, q_s, k_s, v_s, do_s, kt, do_all, dqkv, dqt, p_s, ds_s, sem = refs
    m, heads, base, wide = cfg["m"], cfg["heads"], cfg["base"], cfg["wide"]
    tile = m // 2
    piece.fetch(w_refs, place_ref, w, sem)
    span = heads * HD
    skip = span - base
    pad_heads(cfg, (q_s, k_s))
    dqt[...] = jnp.zeros_like(dqt)
    dqkv[:, :LANES] = jnp.zeros((m, LANES), BF)
    for h in range(heads):
        v_s[h, :, HD:] = jnp.zeros((m, LANES - HD), BF)
        do_s[h, :, HD:] = jnp.zeros((m, LANES - HD), BF)
        for n, s in enumerate((q_s, k_s, v_s)):
            at = skip + n * span + h * HD
            s[h, :, :HD] = qkv_ref[:, at : at + HD]
        kt[h] = k_s[h].T
    landed(w, sem)
    do_all[...] = nn(dh_ref[...], w[:, :wide]).astype(BF)
    for h in range(heads):
        do_s[h, :, :HD] = do_all[:, h * HD : (h + 1) * HD]
        for t in range(m // tile):
            cols = slice(t * tile, (t + 1) * tile)
            p = jnp.exp2(nt(k_s[h], q_s[h, cols, :]) * SHARP - lse_ref[h : h + 1, cols])
            dp = nt(v_s[h], do_s[h, cols, :])
            ds = (p * (dp - jnp.sum(dp * p, axis=0, keepdims=True))).astype(BF)
            p_s[h % 2, :, cols] = p.astype(BF)
            ds_s[h % 2, :, cols] = ds
            dqt[h * HD : (h + 1) * HD, cols] = nn(kt[h], ds)[:HD] * SCALE
        dk = (nn(ds_s[h % 2], q_s[h]) * SCALE).astype(BF)
        dv = nn(p_s[h % 2], do_s[h]).astype(BF)
        at = skip + span + h * HD
        dqkv[:, at : at + HD] = dk[:, :HD]
        at = skip + 2 * span + h * HD
        dqkv[:, at : at + HD] = dv[:, :HD]
    dqkv[:, skip : skip + span] = dqt[...].T.astype(BF)[:, :span]
    grads = dqkv[...]
    sum_ref[...] = jnp.sum(grads.astype(F32), axis=0, keepdims=True)
    half = at_ref.shape[0] // 2
    for n, g_ref in ((1, gb_ref), (0, ga_ref)):
        rows = slice(n * half, (n + 1) * half)
        left = nn(dht_ref[rows, :], o_ref[...])
        right = nn(at_ref[rows, :], grads)
        g_ref[:, :base] = left[:, :base].astype(BF)
        g_ref[:, base:wide] = (left[:, base:] + right[:, : wide - base]).astype(BF)
        g_ref[:, wide:] = right[:, wide - base :].astype(BF)
    part = nt(grads, w[:, base:])
    acc_ref[...] = part if begin else acc_in[...] + part


def attn_bwd(cfg, place, after, piece, at, dh, dht, qkv, o, lse, acc):
    dim, m = at.shape
    qw, wide, heads, width = cfg["qw"], cfg["wide"], cfg["heads"], cfg["width"]
    begin = acc is None
    outs = [((dim // 2, width), BF), ((dim // 2, width), BF), ((1, qw), F32), ((m, dim), F32)]
    scratch = (
        [pltpu.VMEM((dim, width), BF)]
        + [pltpu.VMEM((heads, m, LANES), BF)] * 4
        + [
            pltpu.VMEM((heads, LANES, m), BF),
            pltpu.VMEM((m, wide), BF),
            pltpu.VMEM((m, qw), BF),
            pltpu.VMEM((wide, m), F32),
            pltpu.VMEM((2, m, m), BF),
            pltpu.VMEM((2, m, m), BF),
            pltpu.SemaphoreType.DMA,
        ]
    )
    return call(
        partial(attn_bwd_kernel, cfg, piece, begin), "attn_bwd", 20, place, piece.arrays, after,
        [at, dh, dht, qkv, o, lse] + ([] if begin else [acc]), outs, scratch,
        () if begin else ((6, 3),),
    )


def ffn_one_kernel(cfg, piece, place_ref, w_refs, a_ref, bias_ref, et_ref, *refs):
    g_ref, gp_ref, ga_ref, gb_ref, w, sem = refs
    piece.fetch(w_refs, place_ref, w, sem)
    landed(w, sem)
    width = g_ref.shape[1]
    for n in range(0, width, 256):
        cols = slice(n, min(n + 256, width))
        pre = nn(a_ref[...], w[:, cols]) + bias_ref[:, cols]
        square = pre * pre
        bent = jnp.tanh(pre * (GELU_A + GELU_A * GELU_B * square))
        half = 0.5 + 0.5 * bent
        g_ref[:, cols] = (pre * half).astype(BF)
        slope = half + 0.5 * pre * (1.0 - bent * bent) * (GELU_A + 3 * GELU_A * GELU_B * square)
        gp_ref[:, cols] = slope.astype(BF)
    middle = et_ref.shape[0] // 2
    gb_ref[...] = nn(et_ref[middle:, :], g_ref[...]).astype(BF)
    ga_ref[...] = nn(et_ref[:middle, :], g_ref[...]).astype(BF)


def ffn_one(cfg, place, after, piece, a, bias, et):
    dim, m = et.shape
    width = bias.shape[1]
    outs = [((m, width), BF), ((m, width), BF), ((dim // 2, width), BF), ((dim // 2, width), BF)]
    return call(
        partial(ffn_one_kernel, cfg, piece), "ffn_one", 9, place, piece.arrays, after,
        [a, bias, et], outs, [pltpu.VMEM((dim, width), BF), pltpu.SemaphoreType.DMA],
    )


def ffn_two_kernel(cfg, ups, downs, begin, place_ref, w_refs, eb_ref, at_ref, g_ref, gp_ref, *refs):
    if not begin:
        feed_in, dn_in, *refs = refs
    ga_ref, gb_ref, sum_ref, feed_ref, dn_ref, wu, wd, dz, sems = refs
    count = len(ups.arrays)
    downs.fetch(w_refs[count:], place_ref, wd, sems.at[1])
    ups.fetch(w_refs[:count], place_ref, wu, sems.at[0])
    landed(wd, sems.at[1])
    width = g_ref.shape[1]
    for n in range(0, width, 256):
        cols = slice(n, min(n + 256, width))
        grad = (nn(eb_ref[...], wd[:, cols]) * gp_ref[:, cols].astype(F32)).astype(BF)
        dz[:, cols] = grad
        sum_ref[:, cols] = jnp.sum(grad.astype(F32), axis=0, keepdims=True)
    middle = at_ref.shape[0] // 2
    gb_ref[...] = nn(at_ref[middle:, :], dz[...]).astype(BF)
    ga_ref[...] = nn(at_ref[:middle, :], dz[...]).astype(BF)
    landed(wu, sems.at[0])
    part = nt(g_ref[...], wd[...])
    feed_ref[...] = part if begin else feed_in[...] + part
    part = nt(dz[...], wu[...])
    dn_ref[...] = part if begin else dn_in[...] + part


def ffn_two(cfg, place, after, ups, downs, eb, at, g, gp, feed, dn):
    dim, m = at.shape
    width = g.shape[1]
    begin = feed is None
    outs = [
        ((dim // 2, width), BF), ((dim // 2, width), BF), ((1, width), F32), ((m, dim), F32),
        ((m, dim), F32),
    ]
    return call(
        partial(ffn_two_kernel, cfg, ups, downs, begin), "ffn_two", 14, place,
        ups.arrays + downs.arrays, after,
        [eb, at, g, gp] + ([] if begin else [feed, dn]), outs,
        [
            pltpu.VMEM((dim, width), BF),
            pltpu.VMEM((dim, width), BF),
            pltpu.VMEM((m, width), BF),
            pltpu.SemaphoreType.DMA((2,)),
        ],
        () if begin else ((4, 3), (5, 4)),
    )


CORE, ACROSS, ALONG = 1, 2, 4
CUBE = 8
ORDER = (0, ACROSS, ALONG, ACROSS + ALONG, CORE, CORE + ACROSS, CORE + ALONG, CORE + ACROSS + ALONG)


def ring(value, by, size):
    return lax.ppermute(value, "tensor", [(i, (i + by) % size) for i in range(size)])


def swap(value, offset):
    return lax.ppermute(value, "dp", [(i, i ^ offset) for i in range(lax.axis_size("dp"))])


def tie(value, *others):
    return lax.optimization_barrier((value, *others))[0]


def gather_all(own, split):
    dp, size = lax.axis_size("dp"), lax.axis_size("tensor")
    rows = own.shape[0]
    full = lax.all_gather(own, ("dp", "tensor"), axis=0, tiled=False)
    if split:

        def blocks(k, d, z):
            t = lax.rem(z - k + size, size)
            return [(0, i * size + t, i * rows, rows) for i in range(dp)]
    else:
        full = full.reshape(dp, size, rows, -1).transpose(1, 0, 2, 3)
        full = full.reshape(size, dp * rows, -1)

        def blocks(k, d, z):
            return [(0, lax.rem(z - k + size, size), 0, dp * rows)]

    return [Piece([full], partial(blocks, k)) for k in range(size)]


def gather_ring(own):
    size = lax.axis_size("tensor")
    held = [own]
    for _ in range(size - 1):
        held.append(ring(held[-1], 1, size))
    return held


def gather_near(held, group):
    mine = jnp.stack(held[2 * group : 2 * group + 2])
    return jnp.stack([mine, swap(mine, (ACROSS, ALONG)[group])])


def gather_far(both, group):
    return swap(both, (ALONG, ACROSS)[group])


def gather_core(both, far, group, rows):
    first, second = ((ACROSS, ALONG), (ALONG, ACROSS))[group]
    arrays = [both, far, swap(both, CORE), swap(far, CORE)]

    def blocks(n, d, z):
        return [
            (
                index,
                (other, n),
                pl.multiple_of(jnp.bitwise_xor(d, offset + other * first) * rows, 16),
                rows,
            )
            for index, offset in enumerate((0, second, CORE, CORE + second))
            for other in range(2)
        ]

    return [Piece(arrays, partial(blocks, n)) for n in range(2)]


def scatter_all(near, far, cube):
    size, dp = lax.axis_size("tensor"), lax.axis_size("dp")
    d, z = lax.axis_index("dp"), lax.axis_index("tensor")
    pieces = jnp.stack([jnp.concatenate(halves) for halves in zip(near, far)])
    dim, width = pieces.shape[1:]
    rows = dim // dp
    pieces = pieces.reshape(size, dp, rows, width).transpose(1, 0, 2, 3)
    order = jnp.stack([lax.rem(z - t + size, size) for t in range(size)])
    index = (jnp.arange(dp)[:, None] * size + order[None]).reshape(-1)
    absolute = jnp.take(pieces.reshape(dp * size, rows, width), index, axis=0)
    return lax.psum_scatter(absolute, ("dp", "tensor"), scatter_dimension=0, tiled=True)[0].astype(F32)


def add(*terms):
    total = terms[0].astype(F32)
    for term in terms[1:]:
        total = total + term.astype(F32)
    return total


class Scatter:
    def __init__(self, near, far, first, second):
        half, self.width = near[0].shape
        self.quarter = half // 4
        self.near = [self.shaped(v) for v in near]
        self.far = far
        self.first, self.second = first, second

    def shaped(self, value):
        return value.reshape(2, 2, self.quarter, self.width)

    def pick(self, value, i, j):
        return value[j, i] if self.first == ACROSS else value[i, j]

    def step_core(self):
        self.core = [self.shaped(swap(v, CORE)) for v in self.far]
        return self.core

    def step_first(self):
        out = [
            add(self.pick(a, 1, j), self.pick(b, 1, j)).astype(BF)
            for j in range(2)
            for a, b in zip(self.near, self.core)
        ]
        self.one = swap(jnp.stack(out), self.first)
        return [self.one]

    def step_second(self):
        count = len(self.near)
        out = [
            add(self.pick(a, 0, 1), self.pick(b, 0, 1), self.one[count + i]).astype(BF)
            for i, (a, b) in enumerate(zip(self.near, self.core))
        ]
        self.two = swap(jnp.stack(out), self.second)
        return [self.two]

    def terms(self, i):
        return [
            self.pick(self.near[i], 0, 0), self.pick(self.core[i], 0, 0), self.one[i], self.two[i]
        ]


def sum_all(vector, cube):
    if not cube:
        return lax.psum(vector, ("dp", "tensor"))
    size = lax.axis_size("tensor")
    for offset in (CORE, ACROSS, ALONG):
        vector = vector + swap(vector, offset)
    offset = 1
    while offset < size:
        vector = vector + lax.ppermute(vector, "tensor", [(i, i ^ offset) for i in range(size)])
        offset *= 2
    return vector


def on_device(
    tokens, image_flags, cotangent, gain_one, shift_one, w_query, b_query, w_key, w_value, b_value,
    w_out, b_out, gain_two, shift_two, w_up, b_up, w_down, b_down,
):
    dp, size = lax.axis_size("dp"), lax.axis_size("tensor")
    d, z = lax.axis_index("dp"), lax.axis_index("tensor")
    images = image_flags.shape[0]
    all_rows, dim = tokens.shape
    seq = all_rows // images
    assert images == size
    m = up(seq, 256)
    rows = dim // dp
    split = rows % 16 == 0
    span = w_query.shape[1]
    units = w_up.shape[1]
    hidden = up(units, LANES)
    width = 4 * span
    base, wide = span // LANES * LANES, up(span, LANES)
    qw = width - base
    cube = dp == CUBE and split and size == 4
    cfg = dict(m=m, seq=seq, heads=span // HD, base=base, wide=wide, width=width, qw=qw)
    cfg.update(rows=rows, order=ORDER if cube else None)

    own_attn = jnp.concatenate([w_out.T, w_query, w_key, w_value], axis=1).astype(BF)
    own_up = jnp.pad(w_up.astype(BF), ((0, 0), (0, hidden - units)))
    own_down = jnp.pad(w_down.T.astype(BF), ((0, 0), (0, hidden - units)))
    skip = jnp.zeros((span - base,), F32)
    own_bias = jnp.concatenate(
        [skip, b_query, jnp.zeros((span,), F32), b_value, b_up, jnp.zeros((hidden - units,), F32)]
    )[None]
    bias = [own_bias] + [ring(own_bias, k, size) for k in range(1, size)]
    flag = lax.dynamic_index_in_dim(image_flags, z, 0, keepdims=False)
    place = jnp.stack([d, z, flag]).astype(jnp.int32)

    pad_rows = ((0, m - seq), (0, 0))
    x = jnp.pad(lax.dynamic_slice_in_dim(tokens, z * seq, seq, 0), pad_rows)
    eb = jnp.pad(lax.dynamic_slice_in_dim(cotangent, z * seq, seq, 0) * flag.astype(BF), pad_rows)
    a1, a1t, et, sum_e = norm_one(cfg, place, x, eb, gain_one[None], shift_one[None])

    pins = [[] for _ in range(2 * size)]
    if cube:
        held = gather_ring(own_attn)
        both = [gather_near(held, 0), gather_near(held, 1)]
        far = [gather_far(both[0], 0), gather_far(both[1], 1)]
        attn_w = gather_core(both[0], far[0], 0, rows) + gather_core(both[1], far[1], 1, rows)
        up_held = gather_ring(tie(own_up, held[-1]))
        down_held = gather_ring(tie(own_down, up_held[-1]))
        up_held = [tie(v, far[0]) for v in up_held]
        both_up = [gather_near(up_held, 0), gather_near(up_held, 1)]
        far_up = [gather_far(tie(both_up[i], far[1]), i) for i in range(2)]
        up_w = gather_core(both_up[0], far_up[0], 0, rows) + gather_core(both_up[1], far_up[1], 1, rows)
        down_held = [tie(v, far_up[0]) for v in down_held]
        both_down = [gather_near(down_held, 0), gather_near(down_held, 1)]
        far_down = [gather_far(tie(both_down[i], far_up[1]), i) for i in range(2)]
        down_w = gather_core(both_down[0], far_down[0], 0, rows) + gather_core(
            both_down[1], far_down[1], 1, rows
        )
        pins[0] = [up_held[-1]]
        pins[2] = [*both_up]
        pins[3] = []
    else:
        attn_w, up_w, down_w = (gather_all(w, split) for w in (own_attn, own_up, own_down))
    every = list(range(size))
    att, kept = None, []
    for k in every:
        *saved, att = attn_fwd(cfg, place, pins[k], attn_w[k], a1, bias[k][:, :qw], att)
        kept.append(saved)
    h, a2, a2t = norm_two(cfg, place, [], x, att, b_out[None], gain_two[None], shift_two[None])
    hidden_of, down_near, down_far = [], [], []
    for k in every:
        g, gp, near, far_half = ffn_one(cfg, place, pins[size + k], up_w[k], a2, bias[k][:, qw:], et)
        hidden_of.append((g, gp))
        down_near.append(near)
        down_far.append(far_half)

    feed = dn2 = dn1 = None
    sum_dz, up_near, up_far = [None] * size, [None] * size, [None] * size
    sum_qkv, attn_near, attn_far = [None] * size, [None] * size, [None] * size
    back = list(reversed(every))
    after = {}
    if cube:
        down_out = [
            Scatter([down_near[3], down_near[2]], [down_far[3], down_far[2]], ACROSS, ALONG),
            Scatter([down_near[1], down_near[0]], [down_far[1], down_far[0]], ALONG, ACROSS),
        ]
        after["f2"] = down_out[0].step_core() + down_out[1].step_core()
        after["f0"] = down_out[0].step_first() + down_out[1].step_first()
        after["a3"] = down_out[0].step_second() + down_out[1].step_second()
    for k in back:
        up_near[k], up_far[k], sum_dz[k], feed, dn2 = ffn_two(
            cfg, place, after.get(f"f{k}", []), up_w[k], down_w[k], eb, a2t, *hidden_of[k], feed, dn2
        )
    if cube:
        up_out = [
            Scatter([up_near[3], up_near[2]], [up_far[3], up_far[2]], ACROSS, ALONG),
            Scatter([up_near[1], up_near[0]], [up_far[1], up_far[0]], ALONG, ACROSS),
        ]
        after["b"] = up_out[0].step_core()
        after["a3"] += up_out[1].step_core()
        after["a1"] = up_out[0].step_first() + up_out[1].step_first()
        after["a0"] = up_out[0].step_second() + up_out[1].step_second()
    mixed, dh, dhb, dht, vec_two = norm_two_back(
        cfg, place, after.get("b", []), h, feed, dn2, eb, b_down[None], gain_two[None]
    )
    attn_out = {}
    for k in back:
        attn_near[k], attn_far[k], sum_qkv[k], dn1 = attn_bwd(
            cfg, place, after.get(f"a{k}", []), attn_w[k], a1t, dhb, dht, *kept[k], dn1
        )
        if cube:
            links = (ACROSS, ALONG) if k % 2 else (ALONG, ACROSS)
            attn_out[k] = Scatter([attn_near[k]], [attn_far[k]], *links)
            if k > 1:
                after[f"a{k - 2}"] = after.get(f"a{k - 2}", []) + attn_out[k].step_core()
            if k == 3:
                after["a0"] += attn_out[k].step_first()
            if k == 1:
                after["n"] = attn_out[3].step_second() + attn_out[2].step_first()
                after["n"] += attn_out[1].step_core()
    tokens_grad, vec_one = norm_back(place, after.get("n", []), x, dn1, dh, gain_one[None])

    if cube:
        attn_out[0].step_core()
        attn_out[1].step_first()
        attn_out[2].step_second()
        attn_out[0].step_first()
        attn_out[1].step_second()
        attn_out[0].step_second()

        def along_z(terms):
            total = add(*terms(size - 1))
            for k in range(size - 2, -1, -1):
                total = add(*terms(k), ring(total.astype(BF), -1, size))
            return total

        grad_down = along_z(lambda k: down_out[k < 2].terms((3 - k) % 2))
        grad_up = along_z(lambda k: up_out[k < 2].terms((3 - k) % 2))
        grad_attn = along_z(lambda k: attn_out[k].terms(0))
    else:
        grad_down = scatter_all(down_near, down_far, cube)
        grad_up = scatter_all(up_near, up_far, cube)
        grad_attn = scatter_all(attn_near, attn_far, cube)
    grad_down = grad_down[:, :units].T
    grad_up = grad_up[:, :units]
    pieces = jnp.concatenate([jnp.concatenate(sum_qkv), jnp.concatenate(sum_dz)], axis=1)
    order = jnp.stack([lax.rem(z - t + size, size) for t in range(size)])
    pieces = jnp.take(pieces, order, axis=0)
    sums = sum_all(
        jnp.concatenate([pieces.reshape(-1), vec_one.reshape(-1), vec_two.reshape(-1), sum_e[0]]),
        cube,
    )
    per = qw + hidden
    mine = lax.dynamic_index_in_dim(sums[: size * per].reshape(size, per), z, 0, keepdims=False)
    rest = sums[size * per :].reshape(6, dim)
    at = span - base
    return (
        mixed[:seq],
        tokens_grad[:seq],
        rest[0],
        rest[1],
        grad_attn[:, span : 2 * span],
        mine[at : at + span],
        grad_attn[:, 2 * span : 3 * span],
        grad_attn[:, 3 * span :],
        mine[at + 2 * span : at + 3 * span],
        grad_attn[:, :span].T,
        rest[4],
        rest[2],
        rest[3],
        grad_up,
        mine[qw : qw + units],
        grad_down,
        rest[5],
    )


SPECS_IN = (
    P("dp", None), P("dp"), P("dp", None), P(), P(), P("dp", "tensor"), P("tensor"),
    P("dp", "tensor"), P("dp", "tensor"), P("tensor"), P("tensor", "dp"), P(), P(), P(),
    P("dp", "tensor"), P("tensor"), P("tensor", "dp"), P(),
)
SPECS_OUT = (
    P(("dp", "tensor"), None), P(("dp", "tensor"), None), P(), P(), P("dp", "tensor"), P("tensor"),
    P("dp", "tensor"), P("dp", "tensor"), P("tensor"), P("tensor", "dp"), P(), P(), P(),
    P("dp", "tensor"), P("tensor"), P("tensor", "dp"), P(),
)


def solution(mesh):
    return jax.shard_map(
        on_device, mesh=mesh, in_specs=SPECS_IN, out_specs=SPECS_OUT, check_vma=False
    )
```

time: 1830 us -> 635 us (0.35)
  blocking collectives: 916 us -> 0 us
  matrix products: 374 us -> 0 us
  Pallas kernels: 0 us -> 274 us
  waiting for transfers between devices: 245 us -> 127 us
  local copies, waits for them, and re-layouts: 165 us -> 75.6 us
  starting transfers between devices: 22.8 us -> 65 us
    unnamed x4 -> x0, blocking collectives: 811 us -> none
    dot_general x130 -> x0, matrix products: 374 us -> none  [the longest x54 142 us: matmul_nt(): lax.dot_general(left, right, (((1,), (1,)), ((), ())), preferred_element_...]
    pallas_call x0 -> x20, Pallas kernels: none -> 274 us  [call(): pl.pallas_call(body, in_specs=[SMEM] + [ANY] * (lead - 1) + [VMEM] * len(...]
    all_gather x4 -> x0, waiting for transfers between devices: 245 us -> none  [the longest x1 117 us: on_device(): lax.all_gather(normed_share.astype(jnp.bfloat16), 'tensor', axis=0, tiled...]
    ppermute x0 -> x78, waiting for transfers between devices: none -> 127 us  [the longest x55 66.9 us: swap(): lax.ppermute(value, 'dp', [(i, i ^ offset) for i in range(lax.axis_size('...]
    ppermute x0 -> x78, starting transfers between devices: none -> 65 us  [the longest x55 37.8 us: swap(): lax.ppermute(value, 'dp', [(i, i ^ offset) for i in range(lax.axis_size('...]
    psum x2 -> x0, blocking collectives: 62 us -> none  [the longest x1 38.7 us: on_device(): lax.psum((grad_gain_one, grad_shift_one, grad_b_out, grad_gain_two, grad_...]
    reduce_sum x26 -> x0, other arithmetic: 44.5 us -> none  [the longest x1 9.71 us: on_device(): grad_b_down = jnp.sum(grad_out, axis=0)]
  transfers between devices with their start and end apart: 14 -> 78, of which waited for: 4 -> 17; matrix products, arithmetic and copies ran while one was open for 47% -> 15% of each run, Pallas kernels for 0% -> 44%
where the time goes in v1:
time: 635 us; the launch traced here: 627 us
  Pallas kernels  274 us (43%)
  waiting for transfers between devices  127 us (20%)
  other arithmetic  82.4 us (13%)
  local copies, waits for them, and re-layouts  75.6 us (12%)
  starting transfers between devices  65 us (10%)
    pallas_call x20, Pallas kernels, call(): pl.pallas_call(body, in_specs=[SMEM] + [ANY] * (lead - 1) + [VMEM] * len(...  274 us
    ppermute x55, waiting for transfers between devices, swap(): lax.ppermute(value, 'dp', [(i, i ^ offset) for i in range(lax.axis_size('...  66.9 us
    unnamed x313, local copies, waits for them, and re-layouts  62.6 us
    ppermute x21, waiting for transfers between devices, ring(): lax.ppermute(value, 'tensor', [(i, (i + by) % size) for i in range(size)])  59.9 us
    ppermute x55, starting transfers between devices, swap(): lax.ppermute(value, 'dp', [(i, i ^ offset) for i in range(lax.axis_size('...  37.8 us
    ppermute x21, starting transfers between devices, ring(): lax.ppermute(value, 'tensor', [(i, (i + by) % size) for i in range(size)])  24.7 us
    another operation x12, other arithmetic, gather_near(): return jnp.stack([mine, swap(mine, (ACROSS, ALONG)[group])])  17.3 us
    convert_element_type x9, other arithmetic, along_z(): total = add(*terms(k), ring(total.astype(BF), -1, size))  17 us
  transfers between devices with their start and end apart: 78, of which 17 were waited for; matrix products, arithmetic and copies ran while one was open for 15% of the time, Pallas kernels for 44%

profile of v1, /device:TPU:0, one launch (start us, length us, event | category | flops | bytes accessed | tf_op | source)
XLA Modules:
  0.0 627.0 jit_solution(1329320583216302561)
XLA Ops:
  8.4 9.4 %collective-permute-done = bf16[144,1152]{1,0:T(8,128)(2,1)S(1)} collective-permute-done((bf16[144,1152]{1,0:T(8,128)(2,1)S(1)}, bf16[144,1152]{1,0:T(8,128)(2,1)S(1)}, u32[]{:S(2)}, u32[]{:S(2)}) %collective-permute-start) | collective-permute-done | bytes 331808 | tf_op jit(solution)/shard_map/ppermute | solution.py:442
  20.0 10.5 %collective-permute-done.1 = bf16[144,1152]{1,0:T(8,128)(2,1)S(1)} collective-permute-done((bf16[144,1152]{1,0:T(8,128)(2,1)}, bf16[144,1152]{1,0:T(8,128)(2,1)S(1)}, u32[]{:S(2)}, u32[]{:S(2)}) %collective-permute-start.1) | collective-permute-done | bytes 331808 | tf_op jit(solution)/shard_map/ppermute | solution.py:442
  43.7 5.4 collective-permute-done.3
  61.9 17.9 %collective-permute-done.9 = bf16[2,144,1152]{2,1,0:T(8,128)(2,1)} collective-permute-done((bf16[2,144,1152]{2,1,0:T(8,128)(2,1)}, bf16[2,144,1152]{2,1,0:T(8,128)(2,1)}, u32[]{:S(2)}, u32[]{:S(2)}) %collective-permute-start.9) | collective-permute-done | bytes 663584 | tf_op jit(solution)/shard_map/ppermute | solution.py:446
  96.0 6.8 %norm_one.1 = (bf16[768,1152]{1,0:T(8,128)(2,1)S(1)}, bf16[1152,768]{1,0:T(8,128)(2,1)S(1)}, bf16[1152,768]{1,0:T(8,128)(2,1)S(1)}, f32[1,1152]{1,0:T(1,128)S(1)}) custom-call(s32[3]{0:T(128)S(1)} %pad_add_fusion.refs_0_, bf16[768,1152]{1,0:T(8,128)(2,1)S(1)} %pad.17.refs_1_.refs_4_, bf16[768,1152]{1,0:T(8,128)(2,1)S(1)} %pad.16.refs_2_.refs_9_.refs_13_.refs_11_.refs_6_, ...), custom_call_target="tpu_custom_call" | custom-call | flops 6899999744 | bytes 600000 | tf_op jit(solution)/shard_map/norm_one/pallas_call | solution.py:44
  110.7 8.9 %collective-permute-done.15 = bf16[144,1152]{1,0:T(8,128)(2,1)} collective-permute-done((bf16[144,1152]{1,0:T(8,128)(2,1)}, bf16[144,1152]{1,0:T(8,128)(2,1)}, u32[]{:S(2)}, u32[]{:S(2)}) %collective-permute-start.15) | collective-permute-done | bytes 331808 | tf_op jit(solution)/shard_map/ppermute | solution.py:442
  119.5 13.5 %collective-permute-done.16 = bf16[2,144,1152]{2,1,0:T(8,128)(2,1)} collective-permute-done((bf16[2,144,1152]{2,1,0:T(8,128)(2,1)}, bf16[2,144,1152]{2,1,0:T(8,128)(2,1)}, u32[]{:S(2)}, u32[]{:S(2)}) %collective-permute-start.16) | collective-permute-done | bytes 663584 | tf_op jit(solution)/shard_map/ppermute | solution.py:446
  137.4 8.8 %attn_fwd.4 = (bf16[768,896]{1,0:T(8,128)(2,1)S(1)}, bf16[768,384]{1,0:T(8,128)(2,1)S(1)}, f32[8,768]{1,0:T(8,128)S(1)}, f32[768,1152]{1,0:T(8,128)S(1)}) custom-call(s32[3]{0:T(128)S(1)} %pad_add_fusion.refs_0_, bf16[2,2,144,1152]{3,2,1,0:T(8,128)(2,1)} %pad_maximum_fusion.refs_1_, bf16[2,2,144,1152]{3,2,1,0:T(8,128)(2,1)} %collective-permute-done.6.refs_2_, ...), custom_call_target="tpu_custom_call" | custom-call | flops 11500000256 | bytes 1000000 | tf_op jit(solution)/shard_map/attn_fwd/pallas_call | solution.py:44
  148.7 9.6 %attn_fwd.5 = (bf16[768,896]{1,0:T(8,128)(2,1)S(1)}, bf16[768,384]{1,0:T(8,128)(2,1)S(1)}, f32[8,768]{1,0:T(8,128)S(1)}, f32[768,1152]{1,0:T(8,128)S(1)}) custom-call(s32[3]{0:T(128)S(1)} %pad_add_fusion.refs_0_, bf16[2,2,144,1152]{3,2,1,0:T(8,128)(2,1)} %pad_maximum_fusion.refs_1_, ...), custom_call_target="tpu_custom_call", output_to_operand_aliasing={{3}: (7, {})} | custom-call | flops 11500000256 | bytes 1000000 | tf_op jit(solution)/shard_map/attn_fwd/pallas_call | solution.py:44
  160.2 5.8 collective-permute-done.17.refs_2_
  171.6 12.1 %attn_fwd.6 = (bf16[768,896]{1,0:T(8,128)(2,1)S(1)}, bf16[768,384]{1,0:T(8,128)(2,1)S(1)}, f32[8,768]{1,0:T(8,128)S(1)}, f32[768,1152]{1,0:T(8,128)}) custom-call(s32[3]{0:T(128)S(1)} %pad_add_fusion.refs_0_, bf16[2,2,144,1152]{3,2,1,0:T(8,128)(2,1)} %pad_maximum_fusion.2.refs_1_, ...), custom_call_target="tpu_custom_call", output_to_operand_aliasing={{3}: (9, {})} | custom-call | flops 11500000256 | bytes 1000000 | tf_op jit(solution)/shard_map/attn_fwd/pallas_call | solution.py:44
  188.5 9.0 %attn_fwd.7 = (bf16[768,896]{1,0:T(8,128)(2,1)S(1)}, bf16[768,384]{1,0:T(8,128)(2,1)S(1)}, f32[8,768]{1,0:T(8,128)S(1)}, f32[768,1152]{1,0:T(8,128)S(1)}) custom-call(s32[3]{0:T(128)S(1)} %pad_add_fusion.refs_0_, bf16[2,2,144,1152]{3,2,1,0:T(8,128)(2,1)} %pad_maximum_fusion.2.refs_1_, ...), custom_call_target="tpu_custom_call", output_to_operand_aliasing={{3}: (7, {})} | custom-call | flops 11500000256 | bytes 1000000 | tf_op jit(solution)/shard_map/attn_fwd/pallas_call | solution.py:44
  198.6 6.3 norm_two.1
  213.2 9.6 %ffn_one.4 = (bf16[768,1152]{1,0:T(8,128)(2,1)S(1)}, bf16[768,1152]{1,0:T(8,128)(2,1)S(1)}, bf16[576,1152]{1,0:T(8,128)(2,1)S(1)}, bf16[576,1152]{1,0:T(8,128)(2,1)}) custom-call(s32[3]{0:T(128)S(1)} %pad_add_fusion.refs_0_, bf16[2,2,144,1152]{3,2,1,0:T(8,128)(2,1)S(1)} %pad_maximum_fusion.1.refs_6_.refs_1_, ...), custom_call_target="tpu_custom_call" | custom-call | flops 10350000128 | bytes 900000 | tf_op jit(solution)/shard_map/ffn_one/pallas_call | solution.py:44
  227.9 9.4 %ffn_one.5 = (bf16[768,1152]{1,0:T(8,128)(2,1)S(1)}, bf16[768,1152]{1,0:T(8,128)(2,1)S(1)}, bf16[576,1152]{1,0:T(8,128)(2,1)S(1)}, bf16[576,1152]{1,0:T(8,128)(2,1)}) custom-call(s32[3]{0:T(128)S(1)} %pad_add_fusion.refs_0_, bf16[2,2,144,1152]{3,2,1,0:T(8,128)(2,1)S(1)} %pad_maximum_fusion.1.refs_6_.refs_1_, bf16[2,2,144,1152]{3,2,1,0:T(8,128)(2,1)S(1)} %copy-done.55, ...), custom_call_target="tpu_custom_call" | custom-call | flops 10350000128 | bytes 900000 | tf_op jit(solution)/shard_map/ffn_one/pallas_call | solution.py:44
  241.8 9.6 %ffn_one.6 = (bf16[768,1152]{1,0:T(8,128)(2,1)S(1)}, bf16[768,1152]{1,0:T(8,128)(2,1)S(1)}, bf16[576,1152]{1,0:T(8,128)(2,1)S(1)}, bf16[576,1152]{1,0:T(8,128)(2,1)}) custom-call(s32[3]{0:T(128)S(1)} %pad_add_fusion.refs_0_, bf16[2,2,144,1152]{3,2,1,0:T(8,128)(2,1)S(1)} %pad_maximum_fusion.3.refs_5_.refs_1_, ...), custom_call_target="tpu_custom_call" | custom-call | flops 10350000128 | bytes 900000 | tf_op jit(solution)/shard_map/ffn_one/pallas_call | solution.py:44
  255.8 9.0 %ffn_one.7 = (bf16[768,1152]{1,0:T(8,128)(2,1)S(1)}, bf16[768,1152]{1,0:T(8,128)(2,1)S(1)}, bf16[576,1152]{1,0:T(8,128)(2,1)S(1)}, bf16[576,1152]{1,0:T(8,128)(2,1)S(1)}) custom-call(s32[3]{0:T(128)S(1)} %pad_add_fusion.refs_0_, bf16[2,2,144,1152]{3,2,1,0:T(8,128)(2,1)S(1)} %pad_maximum_fusion.3.refs_5_.refs_1_, ...), custom_call_target="tpu_custom_call" | custom-call | flops 10350000128 | bytes 900000 | tf_op jit(solution)/shard_map/ffn_one/pallas_call | solution.py:44
  277.4 17.0 %ffn_two.4 = (bf16[576,1152]{1,0:T(8,128)(2,1)S(1)}, bf16[576,1152]{1,0:T(8,128)(2,1)}, f32[1,1152]{1,0:T(1,128)S(1)}, f32[768,1152]{1,0:T(8,128)}, f32[768,1152]{1,0:T(8,128)}) custom-call(s32[3]{0:T(128)S(1)} %pad_add_fusion.refs_0_, bf16[2,2,144,1152]{3,2,1,0:T(8,128)(2,1)S(1)} %pad_maximum_fusion.1.refs_6_.refs_1_, ...), custom_call_target="tpu_custom_call" | custom-call | flops 16099999744 | bytes 1400000 | tf_op jit(solution)/shard_map/ffn_two/pallas_call | solution.py:44
  297.5 18.9 %ffn_two.5 = (bf16[576,1152]{1,0:T(8,128)(2,1)S(1)}, bf16[576,1152]{1,0:T(8,128)(2,1)}, f32[1,1152]{1,0:T(1,128)S(1)}, f32[768,1152]{1,0:T(8,128)}, f32[768,1152]{1,0:T(8,128)}) custom-call(s32[3]{0:T(128)S(1)} %pad_add_fusion.refs_0_, ...), custom_call_target="tpu_custom_call", output_to_operand_aliasing={{3}: (17, {}), {4}: (18, {})} | custom-call | flops 16099999744 | bytes 1400000 | tf_op jit(solution)/shard_map/ffn_two/pallas_call | solution.py:44
  320.8 18.8 %ffn_two.6 = (bf16[576,1152]{1,0:T(8,128)(2,1)S(1)}, bf16[576,1152]{1,0:T(8,128)(2,1)}, f32[1,1152]{1,0:T(1,128)S(1)}, f32[768,1152]{1,0:T(8,128)}, f32[768,1152]{1,0:T(8,128)}) custom-call(s32[3]{0:T(128)S(1)} %pad_add_fusion.refs_0_, ...), custom_call_target="tpu_custom_call", output_to_operand_aliasing={{3}: (13, {}), {4}: (14, {})} | custom-call | flops 16099999744 | bytes 1400000 | tf_op jit(solution)/shard_map/ffn_two/pallas_call | solution.py:44
  347.2 18.7 %ffn_two.7 = (bf16[576,1152]{1,0:T(8,128)(2,1)S(1)}, bf16[576,1152]{1,0:T(8,128)(2,1)}, f32[1,1152]{1,0:T(1,128)S(1)}, f32[768,1152]{1,0:T(8,128)}, f32[768,1152]{1,0:T(8,128)}) custom-call(s32[3]{0:T(128)S(1)} %pad_add_fusion.refs_0_, ...), custom_call_target="tpu_custom_call", output_to_operand_aliasing={{3}: (15, {}), {4}: (16, {})} | custom-call | flops 16099999744 | bytes 1400000 | tf_op jit(solution)/shard_map/ffn_two/pallas_call | solution.py:44
  377.3 12.5 %norm_two_back.1 = (bf16[768,1152]{1,0:T(8,128)(2,1)S(1)}, f32[768,1152]{1,0:T(8,128)S(1)}, bf16[768,1152]{1,0:T(8,128)(2,1)S(1)}, bf16[1152,768]{1,0:T(8,128)(2,1)S(1)}, f32[3,1152]{1,0:T(4,128)S(1)}) custom-call(s32[3]{0:T(128)S(1)} %copy-done.46, bf16[2,2,144,1152]{3,2,1,0:T(8,128)(2,1)S(1)} %bitcast.325, bf16[2,2,144,1152]{3,2,1,0:T(8,128)(2,1)S(1)} %bitcast.358, ...), custom_call_target="tpu_custom_call" | custom-call | flops 11500000256 | bytes 1000000 | tf_op jit(solution)/shard_map/norm_two_back/pallas_call | solution.py:44
  403.0 6.5 %collective-permute-done.76 = bf16[144,1152]{1,0:T(8,128)(2,1)S(1)} collective-permute-done((bf16[144,1152]{1,0:T(8,128)(2,1)S(1)}, bf16[144,1152]{1,0:T(8,128)(2,1)S(1)}, u32[]{:S(2)}, u32[]{:S(2)}) %collective-permute-start.76) | collective-permute-done | bytes 331808 | tf_op jit(solution)/shard_map/ppermute | solution.py:442
  420.6 21.8 %attn_bwd.4 = (bf16[576,1152]{1,0:T(8,128)(2,1)S(1)}, bf16[576,1152]{1,0:T(8,128)(2,1)}, f32[1,896]{1,0:T(1,128)S(1)}, f32[768,1152]{1,0:T(8,128)}) custom-call(s32[3]{0:T(128)S(1)} %copy-done.47, bf16[2,2,144,1152]{3,2,1,0:T(8,128)(2,1)} %pad_maximum_fusion.2.refs_1_, bf16[2,2,144,1152]{3,2,1,0:T(8,128)(2,1)} %collective-permute-done.10.refs_2_, ...), custom_call_target="tpu_custom_call" | custom-call | flops 23000000512 | bytes 2000000 | tf_op jit(solution)/shard_map/attn_bwd/pallas_call | solution.py:44
  448.8 21.5 %attn_bwd.5 = (bf16[576,1152]{1,0:T(8,128)(2,1)S(1)}, bf16[576,1152]{1,0:T(8,128)(2,1)}, f32[1,896]{1,0:T(1,128)S(1)}, f32[768,1152]{1,0:T(8,128)}) custom-call(s32[3]{0:T(128)S(1)} %copy-done.47, bf16[2,2,144,1152]{3,2,1,0:T(8,128)(2,1)} %pad_maximum_fusion.2.refs_1_, ...), custom_call_target="tpu_custom_call", output_to_operand_aliasing={{3}: (11, {})} | custom-call | flops 23000000512 | bytes 2000000 | tf_op jit(solution)/shard_map/attn_bwd/pallas_call | solution.py:44
  479.7 23.3 %attn_bwd.6 = (bf16[576,1152]{1,0:T(8,128)(2,1)S(1)}, bf16[576,1152]{1,0:T(8,128)(2,1)}, f32[1,896]{1,0:T(1,128)S(1)}, f32[768,1152]{1,0:T(8,128)}) custom-call(s32[3]{0:T(128)S(1)} %copy-done.47, bf16[2,2,144,1152]{3,2,1,0:T(8,128)(2,1)} %pad_maximum_fusion.refs_1_, ...), custom_call_target="tpu_custom_call", output_to_operand_aliasing={{3}: (14, {})} | custom-call | flops 23000000512 | bytes 2000000 | tf_op jit(solution)/shard_map/attn_bwd/pallas_call | solution.py:44
  507.7 8.7 %collective-permute-done.73 = bf16[144,1152]{1,0:T(8,128)(2,1)S(1)} collective-permute-done((bf16[144,1152]{1,0:T(8,128)(2,1)S(1)}, bf16[144,1152]{1,0:T(8,128)(2,1)S(1)}, u32[]{:S(2)}, u32[]{:S(2)}) %collective-permute-start.73) | collective-permute-done | bytes 331808 | tf_op jit(solution)/shard_map/ppermute | solution.py:442
  520.3 23.6 %attn_bwd.7 = (bf16[576,1152]{1,0:T(8,128)(2,1)S(1)}, bf16[576,1152]{1,0:T(8,128)(2,1)}, f32[1,896]{1,0:T(1,128)S(1)}, f32[768,1152]{1,0:T(8,128)}) custom-call(s32[3]{0:T(128)S(1)} %copy-done.47, bf16[2,2,144,1152]{3,2,1,0:T(8,128)(2,1)} %pad_maximum_fusion.refs_1_, ...), custom_call_target="tpu_custom_call", output_to_operand_aliasing={{3}: (15, {})} | custom-call | flops 23000000512 | bytes 2000000 | tf_op jit(solution)/shard_map/attn_bwd/pallas_call | solution.py:44
  549.7 7.5 %collective-permute-done.50.refs_1_ = bf16[1,144,1152]{2,1,0:T(8,128)(2,1)S(1)} collective-permute-done((bf16[1,144,1152]{2,1,0:T(8,128)(2,1)}, bf16[1,144,1152]{2,1,0:T(8,128)(2,1)S(1)}, u32[]{:S(2)}, u32[]{:S(2)}) %collective-permute-start.50) | collective-permute-done | bytes 331808 | tf_op jit(solution)/shard_map/ppermute | solution.py:446
  566.0 7.8 %norm_back.1 = (bf16[768,1152]{1,0:T(8,128)(2,1)S(1)}, f32[2,1152]{1,0:T(2,128)S(1)}) custom-call(s32[3]{0:T(128)S(1)} %copy-done.48, bf16[1,144,1152]{2,1,0:T(8,128)(2,1)S(1)} %copy-done.34, bf16[2,144,1152]{2,1,0:T(8,128)(2,1)S(1)} %copy-done.31, bf16[2,2,144,1152]{3,2,1,0:T(8,128)(2,1)} %bitcast.78.refs_3_, bf16[768,1152]{1,0:T(8,128)(2,1)S(1)} %pad.17.refs_1_.refs_4_, ...), custom_call_target="tpu_custom_call" | custom-call | flops 9200000000 | bytes 800000 | tf_op jit(solution)/shard_map/norm_back/pallas_call | solution.py:44
  590.1 7.1 %collective-permute-done.66 = bf16[2,144,1152]{2,1,0:T(8,128)(2,1)S(1)} collective-permute-done((bf16[2,144,1152]{2,1,0:T(8,128)(2,1)S(1)}, bf16[2,144,1152]{2,1,0:T(8,128)(2,1)S(1)}, u32[]{:S(2)}, u32[]{:S(2)}) %collective-permute-start.66) | collective-permute-done | bytes 663584 | tf_op jit(solution)/shard_map/ppermute | solution.py:446
  600.7 10.7 %collective-permute-done.67 = bf16[1,144,1152]{2,1,0:T(8,128)(2,1)S(1)} collective-permute-done((bf16[1,144,1152]{2,1,0:T(8,128)(2,1)S(1)}, bf16[1,144,1152]{2,1,0:T(8,128)(2,1)S(1)}, u32[]{:S(2)}, u32[]{:S(2)}) %collective-permute-start.67) | collective-permute-done | bytes 331808 | tf_op jit(solution)/shard_map/ppermute | solution.py:446
  (573 shorter events, 237.9 us)
Async XLA Ops:
  30.6 56.7 %collective-permute-start.29 = (f32[1,2048]{1,0:T(1,128)S(1)}, f32[1,2048]{1,0:T(1,128)S(1)}, u32[]{:S(2)}, u32[]{:S(2)}) collective-permute-start(f32[1,2048]{1,0:T(1,128)S(1)} %bitcast.379), channel_id=1, source_target_pairs={{0,1},{1,2},{2,3},{3,0},{4,5},{5,6},{6,7},{7,4},{8,9},{9,10},{10,1... | collective-permute-start | bytes 24584 | tf_op jit(solution)/shard_map/ppermute | solution.py:442
  30.6 57.7 %collective-permute-start.26 = (f32[1,2048]{1,0:T(1,128)S(1)}, f32[1,2048]{1,0:T(1,128)S(1)}, u32[]{:S(2)}, u32[]{:S(2)}) collective-permute-start(f32[1,2048]{1,0:T(1,128)S(1)} %bitcast.380), channel_id=1, source_target_pairs={{0,2},{1,3},{2,0},{3,1},{4,6},{5,7},{6,4},{7,5},{8,10},{9,11},{10,... | collective-permute-start | bytes 24584 | tf_op jit(solution)/shard_map/ppermute | solution.py:442
  36.3 46.9 %collective-permute-start.6 = (bf16[2,2,144,1152]{3,2,1,0:T(8,128)(2,1)}, bf16[2,2,144,1152]{3,2,1,0:T(8,128)(2,1)}, u32[]{:S(2)}, u32[]{:S(2)}) collective-permute-start(bf16[2,2,144,1152]{3,2,1,0:T(8,128)(2,1)} %pad_maximum_fusion.refs_1_), channel_id=1, source_target_pairs={{0,16},{4,20},{8,24},{12,28},{16,0},{20,4},{24,8},{28,12},{1,17},{... | collective-permute-start | bytes 3981320 | tf_op jit(solution)/shard_map/ppermute | solution.py:446
  83.2 52.7 %collective-permute-start.27 = (bf16[2,2,144,1152]{3,2,1,0:T(8,128)(2,1)}, bf16[2,2,144,1152]{3,2,1,0:T(8,128)(2,1)}, u32[]{:S(2)}, u32[]{:S(2)}) collective-permute-start(bf16[2,2,144,1152]{3,2,1,0:T(8,128)(2,1)} %pad_maximum_fusion.refs_1_), channel_id=1, source_target_pairs={{0,4},{4,0},{8,12},{12,8},{16,20},{20,16},{24,28},{28,24},{1,5},{5... | collective-permute-start | bytes 3981320 | tf_op jit(solution)/shard_map/ppermute | solution.py:446
  87.3 47.5 %collective-permute-start.10 = (bf16[2,2,144,1152]{3,2,1,0:T(8,128)(2,1)}, bf16[2,2,144,1152]{3,2,1,0:T(8,128)(2,1)}, u32[]{:S(2)}, u32[]{:S(2)}) collective-permute-start(bf16[2,2,144,1152]{3,2,1,0:T(8,128)(2,1)} %pad_maximum_fusion.2.refs_1_), channel_id=1, source_target_pairs={{0,8},{4,12},{8,0},{12,4},{16,24},{20,28},{24,16},{28,20},{1,9},{5... | collective-permute-start | bytes 3981320 | tf_op jit(solution)/shard_map/ppermute | solution.py:446
  89.8 43.2 %collective-permute-start.16 = (bf16[2,144,1152]{2,1,0:T(8,128)(2,1)}, bf16[2,144,1152]{2,1,0:T(8,128)(2,1)}, u32[]{:S(2)}, u32[]{:S(2)}) collective-permute-start(bf16[2,144,1152]{2,1,0:T(8,128)(2,1)} %get-tuple-element.254), channel_id=1, source_target_pairs={{0,8},{4,12},{8,0},{12,4},{16,24},{20,28},{24,16},{28,20},{1,9},{5... | collective-permute-start | bytes 1990664 | tf_op jit(solution)/shard_map/ppermute | solution.py:446
  96.0 41.5 %collective-permute-start.28 = (bf16[2,2,144,1152]{3,2,1,0:T(8,128)(2,1)}, bf16[2,2,144,1152]{3,2,1,0:T(8,128)(2,1)}, u32[]{:S(2)}, u32[]{:S(2)}) collective-permute-start(bf16[2,2,144,1152]{3,2,1,0:T(8,128)(2,1)} %collective-permute-done.6.refs_2_), channel_id=1, source_target_pairs={{0,4},{4,0},{8,12},{12,8},{16,20},{20,16},{24,28},{28,24},{1,5},{5... | collective-permute-start | bytes 3981320 | tf_op jit(solution)/shard_map/ppermute | solution.py:446
  119.5 49.9 %collective-permute-start.23 = (bf16[2,2,144,1152]{3,2,1,0:T(8,128)(2,1)}, bf16[2,2,144,1152]{3,2,1,0:T(8,128)(2,1)S(1)}, u32[]{:S(2)}, u32[]{:S(2)}) collective-permute-start(bf16[2,2,144,1152]{3,2,1,0:T(8,128)(2,1)} %pad_maximum_fusion.2.refs_1_), channel_id=1, source_target_pairs={{0,4},{4,0},{8,12},{12,8},{16,20},{20,16},{24,28},{28,24},{1,5},{5... | collective-permute-start | bytes 3981320 | tf_op jit(solution)/shard_map/ppermute | solution.py:446
  166.0 46.5 %collective-permute-start.12 = (bf16[2,2,144,1152]{3,2,1,0:T(8,128)(2,1)S(1)}, bf16[2,2,144,1152]{3,2,1,0:T(8,128)(2,1)}, u32[]{:S(2)}, u32[]{:S(2)}) collective-permute-start(bf16[2,2,144,1152]{3,2,1,0:T(8,128)(2,1)S(1)} %pad_maximum_fusion.1.refs_6_.refs_1_), channel_id=1, source_target_pairs={{0,4},{4,0},{8,12},{12,8},{16,20},{20,16},{24,28},{28,24},{1,5},{5... | collective-permute-start | bytes 3981320 | tf_op jit(solution)/shard_map/ppermute | solution.py:446
  166.0 73.8 %collective-permute-start.33 = (bf16[2,2,144,1152]{3,2,1,0:T(8,128)(2,1)S(1)}, bf16[2,2,144,1152]{3,2,1,0:T(8,128)(2,1)}, u32[]{:S(2)}, u32[]{:S(2)}) collective-permute-start(bf16[2,2,144,1152]{3,2,1,0:T(8,128)(2,1)S(1)} %pad_maximum_fusion.3.refs_5_.refs_1_), channel_id=1, source_target_pairs={{0,4},{4,0},{8,12},{12,8},{16,20},{20,16},{24,28},{28,24},{1,5},{5... | collective-permute-start | bytes 3981320 | tf_op jit(solution)/shard_map/ppermute | solution.py:446
  171.6 41.6 %collective-permute-start.13 = (bf16[2,2,144,1152]{3,2,1,0:T(8,128)(2,1)S(1)}, bf16[2,2,144,1152]{3,2,1,0:T(8,128)(2,1)}, u32[]{:S(2)}, u32[]{:S(2)}) collective-permute-start(bf16[2,2,144,1152]{3,2,1,0:T(8,128)(2,1)S(1)} %collective-permute-done.11.refs_2_), channel_id=1, source_target_pairs={{0,4},{4,0},{8,12},{12,8},{16,20},{20,16},{24,28},{28,24},{1,5},{5... | collective-permute-start | bytes 3981320 | tf_op jit(solution)/shard_map/ppermute | solution.py:446
  209.6 58.4 %collective-permute-start.20 = (bf16[2,2,144,1152]{3,2,1,0:T(8,128)(2,1)S(1)}, bf16[2,2,144,1152]{3,2,1,0:T(8,128)(2,1)}, u32[]{:S(2)}, u32[]{:S(2)}) collective-permute-start(bf16[2,2,144,1152]{3,2,1,0:T(8,128)(2,1)S(1)} %pad_maximum_fusion.4.refs_5_), channel_id=1, source_target_pairs={{0,8},{4,12},{8,0},{12,4},{16,24},{20,28},{24,16},{28,20},{1,9},{5... | collective-permute-start | bytes 3981320 | tf_op jit(solution)/shard_map/ppermute | solution.py:446
  212.6 58.5 %collective-permute-start.39 = (bf16[2,2,144,1152]{3,2,1,0:T(8,128)(2,1)S(1)}, bf16[2,2,144,1152]{3,2,1,0:T(8,128)(2,1)}, u32[]{:S(2)}, u32[]{:S(2)}) collective-permute-start(bf16[2,2,144,1152]{3,2,1,0:T(8,128)(2,1)S(1)} %pad_maximum_fusion.5.refs_5_), channel_id=1, source_target_pairs={{0,16},{4,20},{8,24},{12,28},{16,0},{20,4},{24,8},{28,12},{1,17},{... | collective-permute-start | bytes 3981320 | tf_op jit(solution)/shard_map/ppermute | solution.py:446
  225.1 42.2 %collective-permute-start.31 = (bf16[576,1152]{1,0:T(8,128)(2,1)}, bf16[576,1152]{1,0:T(8,128)(2,1)S(1)}, u32[]{:S(2)}, u32[]{:S(2)}) collective-permute-start(bf16[576,1152]{1,0:T(8,128)(2,1)} %get-tuple-element.135), channel_id=1, source_target_pairs={{0,4},{4,0},{8,12},{12,8},{16,20},{20,16},{24,28},{28,24},{1,5},{5... | collective-permute-start | bytes 3981320 | tf_op jit(solution)/shard_map/ppermute | solution.py:446
  271.1 45.4 %collective-permute-start.40 = (bf16[2,2,144,1152]{3,2,1,0:T(8,128)(2,1)S(1)}, bf16[2,2,144,1152]{3,2,1,0:T(8,128)(2,1)S(1)}, u32[]{:S(2)}, u32[]{:S(2)}) collective-permute-start(bf16[2,2,144,1152]{3,2,1,0:T(8,128)(2,1)S(1)} %pad_maximum_fusion.5.refs_5_), channel_id=1, source_target_pairs={{0,4},{4,0},{8,12},{12,8},{16,20},{20,16},{24,28},{28,24},{1,5},{5... | collective-permute-start | bytes 3981320 | tf_op jit(solution)/shard_map/ppermute | solution.py:446
  271.3 46.9 %collective-permute-start.41 = (bf16[2,2,144,1152]{3,2,1,0:T(8,128)(2,1)}, bf16[2,2,144,1152]{3,2,1,0:T(8,128)(2,1)}, u32[]{:S(2)}, u32[]{:S(2)}) collective-permute-start(bf16[2,2,144,1152]{3,2,1,0:T(8,128)(2,1)} %collective-permute-done.39.refs_6_), channel_id=1, source_target_pairs={{0,4},{4,0},{8,12},{12,8},{16,20},{20,16},{24,28},{28,24},{1,5},{5... | collective-permute-start | bytes 3981320 | tf_op jit(solution)/shard_map/ppermute | solution.py:446
  272.9 66.9 %collective-permute-start.42 = (bf16[4,144,1152]{2,1,0:T(8,128)(2,1)}, bf16[4,144,1152]{2,1,0:T(8,128)(2,1)}, u32[]{:S(2)}, u32[]{:S(2)}) collective-permute-start(bf16[4,144,1152]{2,1,0:T(8,128)(2,1)} %pad_maximum_fusion.6), channel_id=1, source_target_pairs={{0,8},{4,12},{8,0},{12,4},{16,24},{20,28},{24,16},{28,20},{1,9},{5... | collective-permute-start | bytes 3981320 | tf_op jit(solution)/shard_map/ppermute | solution.py:446
  276.4 67.2 %collective-permute-start.43 = (bf16[4,144,1152]{2,1,0:T(8,128)(2,1)}, bf16[4,144,1152]{2,1,0:T(8,128)(2,1)}, u32[]{:S(2)}, u32[]{:S(2)}) collective-permute-start(bf16[4,144,1152]{2,1,0:T(8,128)(2,1)} %pad_maximum_fusion.7), channel_id=1, source_target_pairs={{0,16},{4,20},{8,24},{12,28},{16,0},{20,4},{24,8},{28,12},{1,17},{... | collective-permute-start | bytes 3981320 | tf_op jit(solution)/shard_map/ppermute | solution.py:446
  316.5 53.4 %collective-permute-start.37 = (bf16[576,1152]{1,0:T(8,128)(2,1)}, bf16[576,1152]{1,0:T(8,128)(2,1)S(1)}, u32[]{:S(2)}, u32[]{:S(2)}) collective-permute-start(bf16[576,1152]{1,0:T(8,128)(2,1)} %get-tuple-element.143), channel_id=1, source_target_pairs={{0,4},{4,0},{8,12},{12,8},{16,20},{20,16},{24,28},{28,24},{1,5},{5... | collective-permute-start | bytes 3981320 | tf_op jit(solution)/shard_map/ppermute | solution.py:446
  317.7 55.6 %collective-permute-start.30 = (bf16[576,1152]{1,0:T(8,128)(2,1)}, bf16[576,1152]{1,0:T(8,128)(2,1)S(1)}, u32[]{:S(2)}, u32[]{:S(2)}) collective-permute-start(bf16[576,1152]{1,0:T(8,128)(2,1)} %get-tuple-element.134), channel_id=1, source_target_pairs={{0,4},{4,0},{8,12},{12,8},{16,20},{20,16},{24,28},{28,24},{1,5},{5... | collective-permute-start | bytes 3981320 | tf_op jit(solution)/shard_map/ppermute | solution.py:446
  339.6 53.2 %collective-permute-start.46 = (bf16[576,1152]{1,0:T(8,128)(2,1)}, bf16[576,1152]{1,0:T(8,128)(2,1)}, u32[]{:S(2)}, u32[]{:S(2)}) collective-permute-start(bf16[576,1152]{1,0:T(8,128)(2,1)} %get-tuple-element.163), channel_id=1, source_target_pairs={{0,4},{4,0},{8,12},{12,8},{16,20},{20,16},{24,28},{28,24},{1,5},{5... | collective-permute-start | bytes 3981320 | tf_op jit(solution)/shard_map/ppermute | solution.py:446
  346.2 55.1 %collective-permute-start.45 = (bf16[2,144,1152]{2,1,0:T(8,128)(2,1)}, bf16[2,144,1152]{2,1,0:T(8,128)(2,1)}, u32[]{:S(2)}, u32[]{:S(2)}) collective-permute-start(bf16[2,144,1152]{2,1,0:T(8,128)(2,1)} %pad_maximum_fusion.17), channel_id=1, source_target_pairs={{0,8},{4,12},{8,0},{12,4},{16,24},{20,28},{24,16},{28,20},{1,9},{5... | collective-permute-start | bytes 1990664 | tf_op jit(solution)/shard_map/ppermute | solution.py:446
  367.9 47.3 %collective-permute-start.47 = (bf16[576,1152]{1,0:T(8,128)(2,1)}, bf16[576,1152]{1,0:T(8,128)(2,1)}, u32[]{:S(2)}, u32[]{:S(2)}) collective-permute-start(bf16[576,1152]{1,0:T(8,128)(2,1)} %get-tuple-element.164), channel_id=1, source_target_pairs={{0,4},{4,0},{8,12},{12,8},{16,20},{20,16},{24,28},{28,24},{1,5},{5... | collective-permute-start | bytes 3981320 | tf_op jit(solution)/shard_map/ppermute | solution.py:446
  374.9 67.6 %collective-permute-start.53 = (bf16[4,144,1152]{2,1,0:T(8,128)(2,1)}, bf16[4,144,1152]{2,1,0:T(8,128)(2,1)}, u32[]{:S(2)}, u32[]{:S(2)}) collective-permute-start(bf16[4,144,1152]{2,1,0:T(8,128)(2,1)} %pad_maximum_fusion.8), channel_id=1, source_target_pairs={{0,8},{4,12},{8,0},{12,4},{16,24},{20,28},{24,16},{28,20},{1,9},{5... | collective-permute-start | bytes 3981320 | tf_op jit(solution)/shard_map/ppermute | solution.py:446
  411.7 58.9 %collective-permute-start.77 = (bf16[144,1152]{1,0:T(8,128)(2,1)}, bf16[144,1152]{1,0:T(8,128)(2,1)}, u32[]{:S(2)}, u32[]{:S(2)}) collective-permute-start(bf16[144,1152]{1,0:T(8,128)(2,1)} %fusion.9), channel_id=1, source_target_pairs={{0,3},{1,0},{2,1},{3,2},{4,7},{5,4},{6,5},{7,6},{8,11},{9,8},{10,9... | collective-permute-start | bytes 995336 | tf_op jit(solution)/shard_map/ppermute | solution.py:442
  419.0 56.1 %collective-permute-start.54 = (bf16[4,144,1152]{2,1,0:T(8,128)(2,1)}, bf16[4,144,1152]{2,1,0:T(8,128)(2,1)S(1)}, u32[]{:S(2)}, u32[]{:S(2)}) collective-permute-start(bf16[4,144,1152]{2,1,0:T(8,128)(2,1)} %pad_maximum_fusion.9), channel_id=1, source_target_pairs={{0,16},{4,20},{8,24},{12,28},{16,0},{20,4},{24,8},{28,12},{1,17},{... | collective-permute-start | bytes 3981320 | tf_op jit(solution)/shard_map/ppermute | solution.py:446
  476.5 39.9 %collective-permute-start.57 = (bf16[2,144,1152]{2,1,0:T(8,128)(2,1)S(1)}, bf16[2,144,1152]{2,1,0:T(8,128)(2,1)S(1)}, u32[]{:S(2)}, u32[]{:S(2)}) collective-permute-start(bf16[2,144,1152]{2,1,0:T(8,128)(2,1)S(1)} %pad_maximum_fusion.21), channel_id=1, source_target_pairs={{0,8},{4,12},{8,0},{12,4},{16,24},{20,28},{24,16},{28,20},{1,9},{5... | collective-permute-start | bytes 1990664 | tf_op jit(solution)/shard_map/ppermute | solution.py:446
  478.5 41.8 %collective-permute-start.49 = (bf16[2,144,1152]{2,1,0:T(8,128)(2,1)}, bf16[2,144,1152]{2,1,0:T(8,128)(2,1)S(1)}, u32[]{:S(2)}, u32[]{:S(2)}) collective-permute-start(bf16[2,144,1152]{2,1,0:T(8,128)(2,1)} %pad_maximum_fusion.18), channel_id=1, source_target_pairs={{0,8},{4,12},{8,0},{12,4},{16,24},{20,28},{24,16},{28,20},{1,9},{5... | collective-permute-start | bytes 1990664 | tf_op jit(solution)/shard_map/ppermute | solution.py:446
  503.0 56.6 %collective-permute-start.55 = (bf16[576,1152]{1,0:T(8,128)(2,1)}, bf16[576,1152]{1,0:T(8,128)(2,1)}, u32[]{:S(2)}, u32[]{:S(2)}) collective-permute-start(bf16[576,1152]{1,0:T(8,128)(2,1)} %get-tuple-element.187), channel_id=1, source_target_pairs={{0,4},{4,0},{8,12},{12,8},{16,20},{20,16},{24,28},{28,24},{1,5},{5... | collective-permute-start | bytes 3981320 | tf_op jit(solution)/shard_map/ppermute | solution.py:446
  504.1 40.0 %collective-permute-start.52 = (bf16[2,144,1152]{2,1,0:T(8,128)(2,1)S(1)}, bf16[2,144,1152]{2,1,0:T(8,128)(2,1)S(1)}, u32[]{:S(2)}, u32[]{:S(2)}) collective-permute-start(bf16[2,144,1152]{2,1,0:T(8,128)(2,1)S(1)} %pad_maximum_fusion.19), channel_id=1, source_target_pairs={{0,16},{4,20},{8,24},{12,28},{16,0},{20,4},{24,8},{28,12},{1,17},{... | collective-permute-start | bytes 1990664 | tf_op jit(solution)/shard_map/ppermute | solution.py:446
  518.5 99.5 %collective-permute-start.74 = (bf16[144,1152]{1,0:T(8,128)(2,1)}, bf16[144,1152]{1,0:T(8,128)(2,1)}, u32[]{:S(2)}, u32[]{:S(2)}) collective-permute-start(bf16[144,1152]{1,0:T(8,128)(2,1)} %fusion.14), channel_id=1, source_target_pairs={{0,3},{1,0},{2,1},{3,2},{4,7},{5,4},{6,5},{7,6},{8,11},{9,8},{10,9... | collective-permute-start | bytes 995336 | tf_op jit(solution)/shard_map/ppermute | solution.py:442
  544.0 43.6 %collective-permute-start.63 = (bf16[576,1152]{1,0:T(8,128)(2,1)}, bf16[576,1152]{1,0:T(8,128)(2,1)}, u32[]{:S(2)}, u32[]{:S(2)}) collective-permute-start(bf16[576,1152]{1,0:T(8,128)(2,1)} %get-tuple-element.207), channel_id=1, source_target_pairs={{0,4},{4,0},{8,12},{12,8},{16,20},{20,16},{24,28},{28,24},{1,5},{5... | collective-permute-start | bytes 3981320 | tf_op jit(solution)/shard_map/ppermute | solution.py:446
  (200 other events, 2667.5 us)

commit v2 on v1

v2 whole, which is shorter than its diff:
```python
from functools import partial

import jax
import jax.numpy as jnp
from jax import lax
from jax.experimental import pallas as pl
from jax.experimental.pallas import tpu as pltpu
from jax.sharding import PartitionSpec as P

HD = 72
LANES = 128
EPSILON = 1e-06
SCALE = HD**-0.5
SHARP = SCALE * 1.4426950408889634
GELU_A = 0.7978845608028654
GELU_B = 0.044715
BF = jnp.bfloat16
F32 = jnp.float32
ANY = pl.BlockSpec(memory_space=pl.ANY)
SMEM = pl.BlockSpec(memory_space=pltpu.SMEM)
VMEM = pl.BlockSpec(memory_space=pltpu.VMEM)


def up(value, step):
    return -(-value // step) * step


def nn(left, right):
    return lax.dot_general(left, right, (((1,), (0,)), ((), ())), preferred_element_type=F32)


def nt(left, right):
    return lax.dot_general(left, right, (((1,), (1,)), ((), ())), preferred_element_type=F32)


def whole(shape):
    return pl.BlockSpec(shape, lambda *_: (0,) * len(shape), pipeline_mode=pl.Buffered(1))


def stepped(shape, index=lambda i: i):
    return pl.BlockSpec((1,) + shape, lambda i, *_: (index(i),) + (0,) * len(shape))


def call(
    kernel, name, us, place, weights, after, ins, outs, scratch, late=(), grid=None, specs=None, mib=40,
    prefetch=False,
):
    weights, after, late = list(weights), list(after), list(late)
    lead = 1 + len(weights) + len(after) + len(late)
    scratch = list(scratch)
    if late:
        scratch += [pltpu.VMEM(v.shape, v.dtype) for v in late] + [pltpu.SemaphoreType.DMA((len(late),))]

    def body(*refs):
        if not late:
            return kernel(refs[0], refs[1 : 1 + len(weights)], *refs[lead:])
        n = len(late)
        *rest, sems = refs[lead:]
        inputs = Late(refs[lead - n : lead], rest[-n:], sems)
        return kernel(refs[0], refs[1 : 1 + len(weights)], *rest[:-n], inputs)

    in_specs, out_specs = specs or ([VMEM] * len(ins), [VMEM] * len(outs))
    return pl.pallas_call(
        body,
        grid_spec=pltpu.PrefetchScalarGridSpec(
            num_scalar_prefetch=1 if prefetch else 0,
            grid=grid or (),
            in_specs=([] if prefetch else [SMEM]) + [ANY] * (lead - 1) + list(in_specs),
            out_specs=list(out_specs),
            scratch_shapes=scratch,
        ),
        out_shape=[jax.ShapeDtypeStruct(*out) for out in outs],
        compiler_params=pltpu.CompilerParams(vmem_limit_bytes=mib * 2**20),
        cost_estimate=pl.CostEstimate(
            flops=int(us * 1.15e9), bytes_accessed=int(us * 1e5), transcendentals=0
        ),
        name=name,
    )(place, *weights, *after, *late, *ins)


class Late:
    def __init__(self, sources, buffers, sems):
        self.buffers = buffers
        self.copies = [
            pltpu.make_async_copy(source, buffer, sems.at[i])
            for i, (source, buffer) in enumerate(zip(sources, buffers))
        ]

    def start(self):
        for copy in self.copies:
            copy.start()

    def take(self, i):
        self.copies[i].wait()
        return self.buffers[i]


class Piece:
    def __init__(self, arrays, blocks):
        self.arrays, self.blocks = arrays, blocks

    def fetch(self, refs, place_ref, buffer, sem, columns=None):
        for array, lead, first, rows in self.blocks(place_ref[0], place_ref[1]):
            source = refs[array].at[lead]
            if columns is not None:
                source = source.at[:, :columns]
            pltpu.make_async_copy(source, buffer.at[pl.ds(first, rows), :], sem).start()


def fetch_step(pieces, which, refs, place_ref, buffer, sem):
    begin = 0
    for index, piece in enumerate(pieces):
        mine = refs[begin : begin + len(piece.arrays)]
        begin += len(piece.arrays)

        @pl.when(which == index)
        def _():
            piece.fetch(mine, place_ref, buffer, sem)


def arrays_of(pieces):
    return [array for piece in pieces for array in piece.arrays]


def landed(buffer, sem):
    pltpu.make_async_copy(buffer, buffer, sem).wait()


def turn(cfg, d, value, out_ref, scratch):
    rows, order = cfg["rows"], cfg["order"]
    if order is None:
        out_ref[...] = value.T
        return
    scratch[...] = value.T
    for place, offset in enumerate(order):
        first = pl.multiple_of(jnp.bitwise_xor(d, offset) * rows, 16)
        out_ref[place * rows : (place + 1) * rows, :] = scratch[pl.ds(first, rows), :]


STEP = 32


def over_rows(total, body, carry):
    def step(t, carry):
        return body(pl.ds(pl.multiple_of(t * STEP, STEP), STEP), carry)

    return lax.fori_loop(0, total // STEP, step, carry)


def norm_stats(rows):
    average = jnp.mean(rows, axis=-1, keepdims=True)
    centred = rows - average
    inverse = lax.rsqrt(jnp.mean(centred * centred, axis=-1, keepdims=True) + EPSILON)
    return centred * inverse, inverse


def fold(value):
    return jnp.sum(value.reshape(STEP // 8, 8, value.shape[1]), axis=0)


def total_of(partial_sums):
    return jnp.sum(partial_sums, axis=0, keepdims=True)


def norm_one_kernel(
    cfg, place_ref, _, x_ref, eb_ref, gain_ref, shift_ref, a_ref, at_ref, et_ref, sum_ref, scratch
):
    def rows_of(rows, carry):
        unit, _ = norm_stats(x_ref[rows, :].astype(F32))
        a_ref[rows, :] = (unit * gain_ref[...] + shift_ref[...]).astype(BF)
        return carry + fold(eb_ref[rows, :].astype(F32))

    m, dim = x_ref.shape
    sum_ref[...] = total_of(over_rows(m, rows_of, jnp.zeros((8, dim), F32)))
    turn(cfg, place_ref[0], a_ref[...], at_ref, scratch)
    et_ref[...] = eb_ref[...].T


def norm_one(cfg, place, x, eb, gain, shift):
    m, d = x.shape
    outs = [((m, d), BF), ((d, m), BF), ((d, m), BF), ((1, d), F32)]
    return call(
        partial(norm_one_kernel, cfg), "norm_one", 6, place, [], [], [x, eb, gain, shift], outs,
        [pltpu.VMEM((d, m), BF)],
    )


def norm_two_kernel(cfg, pieces, place_ref, w_refs, b_out, gain, shift, *refs):
    n = len(pieces)
    h_ref, a_ref, at_ref, w, scratch, sems, late = refs
    late.start()
    begin = 0
    for i, piece in enumerate(pieces):
        mine = w_refs[begin : begin + len(piece.arrays)]
        begin += len(piece.arrays)
        piece.fetch(mine, place_ref, w.at[i], sems.at[i], cfg["wide"])
    for i in range(n):
        landed(w.at[i], sems.at[i])
        part = nt(late.take(i)[...], w[i])
        h_ref[...] = part if i == 0 else h_ref[...] + part
    x_ref = late.take(n)

    def rows_of(rows, carry):
        h = x_ref[rows, :].astype(F32) + h_ref[rows, :] + b_out[...]
        h_ref[rows, :] = h
        unit, _ = norm_stats(h)
        a_ref[rows, :] = (unit * gain[...] + shift[...]).astype(BF)
        return carry

    over_rows(x_ref.shape[0], rows_of, 0)
    turn(cfg, place_ref[0], a_ref[...], at_ref, scratch)


def norm_two(cfg, place, after, pieces, x, b_out, gain, shift, o):
    m, d = x.shape
    n = len(pieces)
    outs = [((m, d), F32), ((m, d), BF), ((d, m), BF)]
    return call(
        partial(norm_two_kernel, cfg, pieces), "norm_two", 12, place, arrays_of(pieces), after,
        [b_out, gain, shift], outs,
        [
            pltpu.VMEM((n, d, cfg["wide"]), BF),
            pltpu.VMEM((d, m), BF),
            pltpu.SemaphoreType.DMA((n,)),
        ],
        late=[*o, x],
    )


def mixed_kernel(pieces, place_ref, w_refs, h_ref, g_ref, b_down, out_ref, acc, w, sems):
    step = pl.program_id(0)
    flag = place_ref[2].astype(F32)

    @pl.when(step == 0)
    def _():
        fetch_step(pieces, 0, w_refs, place_ref, w.at[0], sems.at[0])
        acc[...] = h_ref[...] + b_down[...]

    slot = lax.rem(step, 2)
    fetch_step(pieces, step + 1, w_refs, place_ref, w.at[1 - slot], sems.at[1 - slot])
    landed(w.at[slot], sems.at[slot])
    acc[...] += nt(g_ref[0], w[slot])

    @pl.when(step == len(pieces) - 1)
    def _():
        out_ref[...] = (acc[...] * flag).astype(BF)


def mix(place, after, pieces, h, g, b_down):
    m, d = h.shape
    width = g.shape[2]
    return call(
        partial(mixed_kernel, pieces), "mixed", 14, place, arrays_of(pieces), after, [h, g, b_down],
        [((m, d), BF)],
        [pltpu.VMEM((m, d), F32), pltpu.VMEM((2, d, width), BF), pltpu.SemaphoreType.DMA((2,))],
        grid=(len(pieces),),
        specs=([whole((m, d)), stepped((m, width)), whole((1, d))], [whole((m, d))]),
    )[0]


def norm_back_kernel(cfg, pieces, place_ref, w_refs, gain, *refs):
    n = len(pieces)
    out_ref, vec_ref, dn, w, sems, late = refs
    late.start()
    parts, begin = [], 0
    for piece in pieces:
        parts.append(w_refs[begin : begin + len(piece.arrays)])
        begin += len(piece.arrays)
    pieces[0].fetch(parts[0], place_ref, w.at[0], sems.at[0])
    for i in range(n):
        if i + 1 < n:
            pieces[i + 1].fetch(parts[i + 1], place_ref, w.at[(i + 1) % 2], sems.at[(i + 1) % 2])
        landed(w.at[i % 2], sems.at[i % 2])
        part = nt(late.take(i)[...], w[i % 2, :, cfg["base"] :])
        dn[...] = part if i == 0 else dn[...] + part
    x_ref, dh_ref = late.take(n), late.take(n + 1)

    def rows_of(rows, carry):
        unit, inverse = norm_stats(x_ref[rows, :].astype(F32))
        grad = dn[rows, :]
        scaled = grad * gain[...]
        out = dh_ref[rows, :] + inverse * (
            scaled
            - jnp.mean(scaled, axis=-1, keepdims=True)
            - unit * jnp.mean(scaled * unit, axis=-1, keepdims=True)
        )
        out_ref[rows, :] = out.astype(BF)
        return carry[0] + fold(grad * unit), carry[1] + fold(grad)

    m, dim = x_ref.shape
    zero = jnp.zeros((8, dim), F32)
    for i, value in enumerate(over_rows(m, rows_of, (zero, zero))):
        vec_ref[i : i + 1, :] = total_of(value)


def norm_back(cfg, place, after, pieces, x, dh, gain, grads):
    m, d = x.shape
    outs = [((m, d), BF), ((2, d), F32)]
    return call(
        partial(norm_back_kernel, cfg, pieces), "norm_back", 18, place, arrays_of(pieces), after,
        [gain], outs,
        [
            pltpu.VMEM((m, d), F32),
            pltpu.VMEM((2, d, cfg["width"]), BF),
            pltpu.SemaphoreType.DMA((2,)),
        ],
        late=[*grads, x, dh],
    )


def pad_heads(cfg, refs):
    m, seq = cfg["m"], cfg["seq"]
    lane = lax.broadcasted_iota(jnp.int32, (m, LANES - HD), 1)
    row = lax.broadcasted_iota(jnp.int32, (m, LANES - HD), 0)
    one = jnp.where(lane == 0, 1.0, 0.0).astype(BF)
    past = jnp.where((lane == 0) & (row >= seq), -1e30, 0.0).astype(BF)
    for h in range(cfg["heads"]):
        for ref, fill in zip(refs, (one, past, one)):
            ref[h, :, HD:] = fill


def attn_fwd_kernel(cfg, piece, place_ref, w_refs, a_ref, bias_ref, *refs):
    qkv_ref, o_ref, lse_ref, w, q_s, k_s, v_s, vt, ot, sem = refs
    m, heads, base, wide = cfg["m"], cfg["heads"], cfg["base"], cfg["wide"]
    piece.fetch(w_refs, place_ref, w, sem)
    pad_heads(cfg, (q_s, k_s, v_s))
    ot[...] = jnp.zeros_like(ot)
    lse_ref[...] = jnp.zeros_like(lse_ref)
    landed(w, sem)
    qkv_ref[...] = (nn(a_ref[...], w[:, base:]) + bias_ref[...]).astype(BF)
    span = heads * HD
    skip = span - base
    for h in range(heads):
        for n, s in enumerate((q_s, k_s, v_s)):
            at = skip + n * span + h * HD
            s[h, :, :HD] = qkv_ref[:, at : at + HD]
        vt[h] = v_s[h].T
        s = nt(k_s[h], q_s[h])
        highest = jnp.max(s, axis=0, keepdims=True) * SHARP
        p = jnp.exp2(s * SHARP - highest).astype(BF)
        mixed = nn(vt[h], p)
        total = mixed[HD : HD + 1, :]
        ot[h * HD : (h + 1) * HD, :] = mixed[:HD, :] * (1.0 / total)
        lse_ref[h : h + 1, :] = highest + jnp.log2(total)
    o_ref[...] = ot[...].T.astype(BF)


def attn_fwd(cfg, place, after, piece, a, bias):
    m, dim = a.shape
    qw, wide, heads, width = cfg["qw"], cfg["wide"], cfg["heads"], cfg["width"]
    outs = [((m, qw), BF), ((m, wide), BF), ((8, m), F32)]
    scratch = (
        [pltpu.VMEM((dim, width), BF)]
        + [pltpu.VMEM((heads, m, LANES), BF)] * 3
        + [
            pltpu.VMEM((heads, LANES, m), BF),
            pltpu.VMEM((wide, m), F32),
            pltpu.SemaphoreType.DMA,
        ]
    )
    return call(
        partial(attn_fwd_kernel, cfg, piece), "attn_fwd", 8, place, piece.arrays, after, [a, bias],
        outs, scratch, mib=28,
    )


def attn_bwd_kernel(cfg, piece, place_ref, w_refs, *refs):
    dh_ref, qkv_ref, lse_ref, ga_ref, gb_ref, sum_ref, dqkv, *refs = refs
    w, q_s, k_s, v_s, do_s, kt, do_all, dqt, p_s, ds_s, sem, late = refs
    m, heads, base, wide = cfg["m"], cfg["heads"], cfg["base"], cfg["wide"]
    tile = m // 2
    piece.fetch(w_refs, place_ref, w, sem, wide)
    late.start()
    span = heads * HD
    skip = span - base
    pad_heads(cfg, (q_s, k_s))
    dqt[...] = jnp.zeros_like(dqt)
    dqkv[:, :LANES] = jnp.zeros((m, LANES), BF)
    for h in range(heads):
        v_s[h, :, HD:] = jnp.zeros((m, LANES - HD), BF)
        do_s[h, :, HD:] = jnp.zeros((m, LANES - HD), BF)
        for n, s in enumerate((q_s, k_s, v_s)):
            at = skip + n * span + h * HD
            s[h, :, :HD] = qkv_ref[:, at : at + HD]
        kt[h] = k_s[h].T
    landed(w, sem)
    do_all[...] = nn(dh_ref[...], w[...]).astype(BF)
    for h in range(heads):
        do_s[h, :, :HD] = do_all[:, h * HD : (h + 1) * HD]
        for t in range(m // tile):
            cols = slice(t * tile, (t + 1) * tile)
            p = jnp.exp2(nt(k_s[h], q_s[h, cols, :]) * SHARP - lse_ref[h : h + 1, cols])
            dp = nt(v_s[h], do_s[h, cols, :])
            ds = (p * (dp - jnp.sum(dp * p, axis=0, keepdims=True))).astype(BF)
            p_s[h % 2, :, cols] = p.astype(BF)
            ds_s[h % 2, :, cols] = ds
            dqt[h * HD : (h + 1) * HD, cols] = nn(kt[h], ds)[:HD] * SCALE
        dk = (nn(ds_s[h % 2], q_s[h]) * SCALE).astype(BF)
        dv = nn(p_s[h % 2], do_s[h]).astype(BF)
        at = skip + span + h * HD
        dqkv[:, at : at + HD] = dk[:, :HD]
        at = skip + 2 * span + h * HD
        dqkv[:, at : at + HD] = dv[:, :HD]
    dqkv[:, skip : skip + span] = dqt[...].T.astype(BF)[:, :span]
    grads = dqkv[...]
    sum_ref[...] = jnp.sum(grads.astype(F32), axis=0, keepdims=True)
    at_ref, dht_ref, o_ref = (late.take(i) for i in range(3))
    half = at_ref.shape[0] // 2
    for n, g_ref in ((1, gb_ref), (0, ga_ref)):
        rows = slice(n * half, (n + 1) * half)
        left = nn(dht_ref[rows, :], o_ref[...])
        right = nn(at_ref[rows, :], grads)
        g_ref[0, :, :base] = left[:, :base].astype(BF)
        g_ref[0, :, base:wide] = (left[:, base:] + right[:, : wide - base]).astype(BF)
        g_ref[0, :, wide:] = right[:, wide - base :].astype(BF)


def attn_bwd(cfg, place, after, piece, at, dh, dht, qkv, o, lse):
    dim, m = at.shape
    qw, wide, heads, width = cfg["qw"], cfg["wide"], cfg["heads"], cfg["width"]
    outs = [((1, dim // 2, width), BF)] * 2 + [((1, qw), F32), ((m, qw), BF)]
    scratch = (
        [pltpu.VMEM((dim, wide), BF)]
        + [pltpu.VMEM((heads, m, LANES), BF)] * 4
        + [
            pltpu.VMEM((heads, LANES, m), BF),
            pltpu.VMEM((m, wide), BF),
            pltpu.VMEM((wide, m), F32),
            pltpu.VMEM((2, m, m), BF),
            pltpu.VMEM((2, m, m), BF),
            pltpu.SemaphoreType.DMA,
        ]
    )
    return call(
        partial(attn_bwd_kernel, cfg, piece), "attn_bwd", 17, place, piece.arrays, after,
        [dh, qkv, lse], outs, scratch, late=[at, dht, o], mib=36,
    )


def ffn_one_kernel(cfg, pieces, place_ref, w_refs, a_ref, bias_ref, *refs):
    g_ref, gp_ref, grad_ref, w, sems, late = refs
    step = pl.program_id(0)

    @pl.when(step == 0)
    def _():
        late.start()
        fetch_step(pieces, 0, w_refs, place_ref, w.at[0], sems.at[0])

    slot = lax.rem(step, 2)
    fetch_step(pieces, step + 1, w_refs, place_ref, w.at[1 - slot], sems.at[1 - slot])
    landed(w.at[slot], sems.at[slot])
    width = g_ref.shape[2]
    for n in range(0, width, 256):
        cols = slice(n, min(n + 256, width))
        pre = nn(a_ref[...], w[slot, :, cols]) + bias_ref[0, :, cols]
        square = pre * pre
        bent = jnp.tanh(pre * (GELU_A + GELU_A * GELU_B * square))
        half = 0.5 + 0.5 * bent
        g_ref[0, :, cols] = (pre * half).astype(BF)
        slope = half + 0.5 * pre * (1.0 - bent * bent) * (GELU_A + 3 * GELU_A * GELU_B * square)
        gp_ref[0, :, cols] = slope.astype(BF)

    @pl.when(step == 0)
    def _():
        late.take(0)

    et_ref = late.buffers[0]
    count, _, rows, _ = grad_ref.shape
    for part in range(2):
        half = et_ref.shape[0] // 2
        value = nn(et_ref[part * half : (part + 1) * half, :], g_ref[0]).astype(BF)
        for i in range(count // 2):
            grad_ref[part * count // 2 + i, 0] = value[i * rows : (i + 1) * rows]


def ffn_one(cfg, place, after, pieces, a, bias, et):
    dim, m = et.shape
    n, width = len(pieces), bias.shape[2]
    rows = cfg["rows"] if cfg["rows"] % 16 == 0 else dim // 2
    outs = [((n, m, width), BF)] * 2 + [((dim // rows, n, rows, width), BF)]
    return call(
        partial(ffn_one_kernel, cfg, pieces), "ffn_one", 30, place, arrays_of(pieces), after,
        [a, bias], outs,
        [pltpu.VMEM((2, dim, width), BF), pltpu.SemaphoreType.DMA((2,))],
        late=[et], grid=(n,),
        specs=(
            [whole((m, dim)), stepped((1, width))],
            [stepped((m, width))] * 2
            + [
                pl.BlockSpec(
                    (dim // rows, 1, rows, width),
                    lambda i, place_ref: (0, lax.rem(place_ref[1] - i + n, n), 0, 0),
                )
            ],
        ),
        mib=56, prefetch=True,
    )


def ffn_two_kernel(cfg, ups, downs, first, last, place_ref, w_refs, eb_ref, gp_ref, *refs):
    *refs, late = refs
    if last:
        gain, *refs = refs
    near_ref, far_ref, sum_ref, *refs = refs
    if last:
        dh_ref, dhb_ref, dht_ref, vec_ref, *refs = refs
        wu, wd, dz, dn_ref, scratch, sems = refs
    else:
        dn_ref, wu, wd, dz, sems = refs
    step = pl.program_id(0)
    count = len(arrays_of(ups))
    n = len(ups)

    at_ref = late.buffers[0]

    def get(which, slot):
        fetch_step(downs, which, w_refs[count:], place_ref, wd.at[slot], sems.at[1, slot])
        fetch_step(ups, which, w_refs[:count], place_ref, wu.at[slot], sems.at[0, slot])

    @pl.when(step == 0)
    def _():
        get(0, 0)
        late.start()
        if first:
            dn_ref[...] = jnp.zeros_like(dn_ref)

    slot = lax.rem(step, 2)
    get(step + 1, 1 - slot)
    landed(wd.at[slot], sems.at[1, slot])
    width = dz.shape[1]
    for c in range(0, width, 256):
        cols = slice(c, min(c + 256, width))
        grad = (nn(eb_ref[...], wd[slot, :, cols]) * gp_ref[0, :, cols].astype(F32)).astype(BF)
        dz[:, cols] = grad
        sum_ref[0, :, cols] = jnp.sum(grad.astype(F32), axis=0, keepdims=True)
    landed(wu.at[slot], sems.at[0, slot])
    part = nt(dz[...], wu[slot])

    @pl.when(step == 0)
    def _():
        late.take(0)
        if not first:
            dn_ref[...] = late.take(1)[...]

    dn_ref[...] += part
    middle = at_ref.shape[0] // 2
    far_ref[0] = nn(at_ref[middle:, :], dz[...]).astype(BF)
    near_ref[0] = nn(at_ref[:middle, :], dz[...]).astype(BF)
    if not last:
        return

    @pl.when(step == n - 1)
    def _():
        h_ref = late.take(2)

        def rows_of(rows, carry):
            unit, inverse = norm_stats(h_ref[rows, :])
            grad = dn_ref[rows, :]
            scaled = grad * gain[...]
            dh = eb_ref[rows, :].astype(F32) + inverse * (
                scaled
                - jnp.mean(scaled, axis=-1, keepdims=True)
                - unit * jnp.mean(scaled * unit, axis=-1, keepdims=True)
            )
            dh_ref[rows, :] = dh
            dhb_ref[rows, :] = dh.astype(BF)
            return carry[0] + fold(grad * unit), carry[1] + fold(grad), carry[2] + fold(dh)

        m, dim = h_ref.shape
        zero = jnp.zeros((8, dim), F32)
        sums = over_rows(m, rows_of, (zero, zero, zero))
        for i, value in enumerate(sums):
            vec_ref[i : i + 1, :] = total_of(value)
        turn(cfg, place_ref[0], dhb_ref[...], dht_ref, scratch)


def ffn_two(cfg, place, after, ups, downs, ks, eb, at, gp, dn, closing=None):
    dim, m = at.shape
    n, width = len(ups), gp.shape[2]
    block = (dim // 2, width)
    at_k = lambda i: ks[0] + i if ks[0] < ks[-1] else ks[0] - i
    ins, in_specs, late = [eb, gp], [whole((m, dim)), stepped((m, width), at_k)], [at]
    if closing:
        ins.append(closing[1])
        in_specs.append(whole((1, dim)))
        late += [dn, closing[0]]
    outs = [((n,) + block, BF)] * 2 + [((n, 1, width), F32)]
    out_specs = [stepped(block)] * 2 + [stepped((1, width))]
    scratch = [
        pltpu.VMEM((2, dim, width), BF), pltpu.VMEM((2, dim, width), BF), pltpu.VMEM((m, width), BF)
    ]
    if closing:
        shapes = [((m, dim), F32), ((m, dim), BF), ((dim, m), BF), ((3, dim), F32)]
        scratch += [pltpu.VMEM((m, dim), F32), pltpu.VMEM((dim, m), BF)]
    else:
        shapes = [((m, dim), F32)]
    outs += shapes
    out_specs += [whole(shape) for shape, _ in shapes]
    return call(
        partial(ffn_two_kernel, cfg, ups, downs, dn is None, bool(closing)), "ffn_two",
        30 if closing else 24, place, arrays_of(ups) + arrays_of(downs), after, ins, outs,
        scratch + [pltpu.SemaphoreType.DMA((2, 2))], late=late, grid=(n,),
        specs=(in_specs, out_specs), mib=58,
    )


CORE, ACROSS, ALONG = 1, 2, 4
CUBE = 8
ORDER = (0, ACROSS, ALONG, ACROSS + ALONG, CORE, CORE + ACROSS, CORE + ALONG, CORE + ACROSS + ALONG)


def ring(value, by, size):
    return lax.ppermute(value, "tensor", [(i, (i + by) % size) for i in range(size)])


def swap(value, offset):
    return lax.ppermute(value, "dp", [(i, i ^ offset) for i in range(lax.axis_size("dp"))])


def tie(value, *others):
    return lax.optimization_barrier((value, *others))[0]


def ties(values, mark):
    return list(lax.optimization_barrier((*values, mark))[:-1])


def gather_all(own, split):
    dp, size = lax.axis_size("dp"), lax.axis_size("tensor")
    rows = own.shape[0]
    full = lax.all_gather(own, ("dp", "tensor"), axis=0, tiled=False)
    if split:

        def blocks(k, d, z):
            t = lax.rem(z - k + size, size)
            return [(0, i * size + t, i * rows, rows) for i in range(dp)]
    else:
        full = full.reshape(dp, size, rows, -1).transpose(1, 0, 2, 3)
        full = full.reshape(size, dp * rows, -1)

        def blocks(k, d, z):
            return [(0, lax.rem(z - k + size, size), 0, dp * rows)]

    return [Piece([full], partial(blocks, k)) for k in range(size)]


def gather_ring(own):
    size = lax.axis_size("tensor")
    held = [own]
    for _ in range(size - 1):
        held.append(ring(held[-1], 1, size))
    return held


def gather_near(held, group):
    mine = jnp.stack(held[2 * group : 2 * group + 2])
    return jnp.stack([mine, swap(mine, (ACROSS, ALONG)[group])])


def gather_far(both, group):
    return swap(both, (ALONG, ACROSS)[group])


def gather_pieces(nears, fars, firsts, rows):
    own = jnp.stack([jnp.stack(pair) for pair in zip(nears, fars)])
    arrays = [own, swap(own, CORE)]

    def blocks(n, d, z):
        first = firsts[n]
        second = ACROSS + ALONG - first
        return [
            (
                core,
                (n, i, j),
                pl.multiple_of(jnp.bitwise_xor(d, core * CORE + i * second + j * first) * rows, 16),
                rows,
            )
            for core in range(2)
            for i in range(2)
            for j in range(2)
        ]

    return [Piece(arrays, partial(blocks, n)) for n in range(len(nears))]


def gather_groups(both, both_core, far, far_core, rows):
    firsts = (ACROSS, ACROSS, ALONG, ALONG)

    def blocks(k, d, z):
        group, n = k // 2, k % 2
        first = firsts[k]
        second = ACROSS + ALONG - first
        out = []
        for other in range(2):
            for index, lead, offset in (
                (group, (other, n), 0),
                (2, (group, other, n), CORE),
                (3 + group, (other, n), second),
                (5, (group, other, n), CORE + second),
            ):
                at = pl.multiple_of(jnp.bitwise_xor(d, offset + other * first) * rows, 16)
                out.append((index, lead, at, rows))
        return out

    return [Piece([*both, both_core, *far, far_core], partial(blocks, k)) for k in range(4)]


def scatter_all(near, far):
    size, dp = lax.axis_size("tensor"), lax.axis_size("dp")
    z = lax.axis_index("tensor")
    pieces = jnp.stack([jnp.concatenate(halves) for halves in zip(near, far)])
    dim, width = pieces.shape[1:]
    order = jnp.stack([lax.rem(z - t + size, size) for t in range(size)])
    return scatter_placed(jnp.take(pieces, order, axis=0)[None])


def scatter_placed(value):
    size, dp = lax.axis_size("tensor"), lax.axis_size("dp")
    blocks, _, rows, width = value.shape
    if blocks != dp:
        value = value.transpose(1, 0, 2, 3).reshape(size, dp, -1, width).transpose(1, 0, 2, 3)
    value = value.reshape(dp * size, -1, width)
    return lax.psum_scatter(value, ("dp", "tensor"), scatter_dimension=0, tiled=True)[0]


def add(*terms):
    total = terms[0].astype(F32)
    for term in terms[1:]:
        total = total + term.astype(F32)
    return total


class Scatter:
    def __init__(self, halves, links):
        self.links = links
        self.near = [piece for near, _ in halves for piece in self.split(near)]
        self.far = [far for _, far in halves]

    def split(self, value):
        count, half, width = value.shape
        value = value.reshape(count, 2, 2, half // 4, width)
        return [value[i] for i in range(count)]

    def pick(self, value, link, i, j):
        return value[j, i] if link == ACROSS else value[i, j]

    def send(self, step, outs):
        got, sent = [None] * len(outs), []
        for link in (ACROSS, ALONG):
            mine = [i for i, first in enumerate(self.links) if (first == link) == (step == 1)]
            if not mine:
                continue
            value = swap(jnp.stack([v for i in mine for v in outs[i]]), link)
            sent.append(value)
            for n, i in enumerate(mine):
                count = len(outs[i])
                got[i] = [value[n * count + c] for c in range(count)]
        return got, sent

    def step_core(self):
        sent = [swap(far, CORE) for far in self.far]
        self.core = [piece for value in sent for piece in self.split(value)]
        return sent

    def step_first(self, mark=None):
        if mark is not None:
            self.core = ties(self.core, mark)
        outs = [
            [add(self.pick(a, link, 1, j), self.pick(b, link, 1, j)).astype(BF) for j in range(2)]
            for a, b, link in zip(self.near, self.core, self.links)
        ]
        self.one, sent = self.send(1, outs)
        return sent

    def step_second(self, mark=None):
        if mark is not None:
            flat = ties([v for one in self.one for v in one], mark)
            self.one = [flat[2 * i : 2 * i + 2] for i in range(len(self.one))]
        outs = [
            [add(self.pick(a, link, 0, 1), self.pick(b, link, 0, 1), one[1]).astype(BF)]
            for a, b, one, link in zip(self.near, self.core, self.one, self.links)
        ]
        self.two, sent = self.send(2, outs)
        return sent

    def terms(self, i):
        link = self.links[i]
        return [
            self.pick(self.near[i], link, 0, 0),
            self.pick(self.core[i], link, 0, 0),
            self.one[i][0],
            self.two[i][0],
        ]


class Around:
    def __init__(self, terms, size):
        self.terms, self.size, self.k, self.total = terms, size, size - 1, None

    def step(self, mark=None):
        terms = self.terms(self.k) + ([] if self.total is None else [self.total])
        if mark is not None:
            terms = terms[:-1] + [tie(terms[-1], mark)]
        total = add(*terms)
        self.k -= 1
        if self.k < 0:
            return total
        self.total = ring(total.astype(BF), -1, self.size)
        return [self.total]


def sum_all(vector, cube):
    if not cube:
        return lax.psum(vector, ("dp", "tensor"))
    size = lax.axis_size("tensor")
    for offset in (CORE, ACROSS, ALONG):
        vector = vector + swap(vector, offset)
    offset = 1
    while offset < size:
        vector = vector + lax.ppermute(vector, "tensor", [(i, i ^ offset) for i in range(size)])
        offset *= 2
    return vector


def on_device(
    tokens, image_flags, cotangent, gain_one, shift_one, w_query, b_query, w_key, w_value, b_value,
    w_out, b_out, gain_two, shift_two, w_up, b_up, w_down, b_down,
):
    dp, size = lax.axis_size("dp"), lax.axis_size("tensor")
    d, z = lax.axis_index("dp"), lax.axis_index("tensor")
    images = image_flags.shape[0]
    all_rows, dim = tokens.shape
    seq = all_rows // images
    assert images == size
    m = up(seq, 256)
    rows = dim // dp
    split = rows % 16 == 0
    span = w_query.shape[1]
    units = w_up.shape[1]
    hidden = up(units, LANES)
    width = 4 * span
    base, wide = span // LANES * LANES, up(span, LANES)
    qw = width - base
    cube = dp == CUBE and split and size == 4
    cfg = dict(m=m, seq=seq, heads=span // HD, base=base, wide=wide, width=width, qw=qw)
    cfg.update(rows=rows, order=ORDER if cube else None)

    own_attn = jnp.concatenate([w_out.T, w_query, w_key, w_value], axis=1).astype(BF)
    own_up = jnp.pad(w_up.astype(BF), ((0, 0), (0, hidden - units)))
    own_down = jnp.pad(w_down.T.astype(BF), ((0, 0), (0, hidden - units)))
    skip = jnp.zeros((span - base,), F32)
    own_bias = jnp.concatenate(
        [skip, b_query, jnp.zeros((span,), F32), b_value, b_up, jnp.zeros((hidden - units,), F32)]
    )[None]
    flag = lax.dynamic_index_in_dim(image_flags, z, 0, keepdims=False)
    place = jnp.stack([d, z, flag]).astype(jnp.int32)

    pad_rows = ((0, m - seq), (0, 0))
    x = jnp.pad(lax.dynamic_slice_in_dim(tokens, z * seq, seq, 0), pad_rows)
    eb = jnp.pad(lax.dynamic_slice_in_dim(cotangent, z * seq, seq, 0) * flag.astype(BF), pad_rows)
    a1, a1t, et, sum_e = norm_one(cfg, place, x, eb, gain_one[None], shift_one[None])

    every = list(range(size))
    pin = {}
    if cube:
        held = gather_ring(own_attn)
        firsts = [ACROSS if k % 2 == 0 else ALONG for k in every]
        nears, fars = [], []
        for k in every:
            nears.append(jnp.stack([held[k], swap(held[k], firsts[k])]))
            fars.append(swap(nears[k], ACROSS + ALONG - firsts[k]))
        attn_w = gather_pieces(nears[:2], fars[:2], firsts[:2], rows)
        attn_w += gather_pieces(nears[2:], fars[2:], firsts[2:], rows)
        bits = []
        for _ in range(3):
            top = lax.reduce_precision(own_bias[0], 8, 7)
            bits.append(top.astype(BF))
            own_bias = own_bias - top[None]
        bits = jnp.concatenate(bits)
        count = bits.shape[0]
        extra = up(-(-count // hidden), 16)
        bits = jnp.pad(bits, (0, extra * hidden - count)).reshape(extra, hidden)
        ffn_held = gather_ring(tie(jnp.concatenate([own_up, bits]), held[-1]))
        bias = []
        for v in ffn_held:
            v = v[rows:].reshape(-1)[:count].reshape(3, -1).astype(F32)
            bias.append((v[0] + v[1] + v[2])[None])
        ffn_held = ties(ffn_held, fars[3])
        up_held = [v[:rows] for v in ffn_held]
        both_up = [gather_near(up_held, i) for i in range(2)]
    else:
        bias = gather_ring(own_bias)
        attn_w, up_w = (gather_all(w, split) for w in (own_attn, own_up))
    kept = [
        attn_fwd(cfg, place, pin.get(f"attn{k}", []), attn_w[k], a1, bias[k][:, :qw]) for k in every
    ]
    if cube:
        far_up = [gather_far(both_up[i], i) for i in range(2)]
        core_up = swap(jnp.stack(both_up), CORE)
    h, a2, a2t = norm_two(
        cfg, place, pin.get("norm_two", []), attn_w, x, b_out[None], gain_two[None], shift_two[None],
        [o for _, o, _ in kept],
    )
    down_w = gather_all(own_down, split)
    if cube:
        far_up = ties(far_up, kept[3][2])
        up_w = gather_groups(both_up, core_up, far_up, swap(jnp.stack(far_up), CORE), rows)
    g, gp, g_down = ffn_one(
        cfg, place, pin.get("ffn_one", []), up_w, a2, jnp.stack(bias)[:, :, qw:], et
    )

    sum_down = scatter_placed(g_down)

    low, high = [1, 0], [3, 2]
    near3, far3, sum_high, dn2 = ffn_two(
        cfg, place, pin.get("two0", []), [up_w[k] for k in high], [down_w[k] for k in high], high, eb,
        a2t, gp, None,
    )
    mixed_links = [ACROSS, ALONG]
    if cube:
        up_high = Scatter([(near3, far3)], mixed_links)
        up_high_core = up_high.step_core()
    near1, far1, sum_low, dh, dhb, dht, vec_two = ffn_two(
        cfg, place, pin.get("two1", []), [up_w[k] for k in low], [down_w[k] for k in low], low, eb,
        a2t, gp, dn2, [h, gain_two[None]],
    )
    sum_dz = [sum_low[1], sum_low[0], sum_high[1], sum_high[0]]
    grads = [None] * size

    def backward(k, after):
        near, far, sums, dqkv = attn_bwd(cfg, place, after, attn_w[k], a1t, dhb, dht, *kept[k])
        grads[k] = (near, far, sums, dqkv)
        return Scatter([(near, far)], [ACROSS if k % 2 else ALONG])

    def finish(after):
        return mix(place, after, down_w, h, g, b_down[None])

    def finish_norm(after):
        return norm_back(
            cfg, place, after, attn_w, x, dh, gain_one[None], [grads[k][3] for k in every]
        )

    if cube:
        up_low = Scatter([(near1, far1)], mixed_links)
        up_z = Around(lambda k: (up_high if k > 1 else up_low).terms(1 - k % 2), size)
        attn_z = Around(lambda k: out[k].terms(0), size)
        out = {}
        pins = {k: [] for k in ("a3", "a2", "a1", "a0", "nb", "mix")}
        pins["a3"] += up_high_core
        pins["a2"] += up_low.step_core() + up_high.step_first(vec_two)
        out[3] = backward(3, pins["a3"])
        mark = grads[3][2]
        pins["a1"] += up_high.step_second(mark) + up_low.step_first(mark) + out[3].step_core()
        out[2] = backward(2, pins["a2"])
        mark = grads[2][2]
        pins["a0"] += up_low.step_second(mark) + out[3].step_first(mark) + out[2].step_core()
        out[1] = backward(1, pins["a1"])
        mark = grads[1][2]
        pins["nb"] += out[3].step_second(mark) + out[2].step_first(mark) + out[1].step_core()
        pins["nb"] += up_z.step(mark)
        out[0] = backward(0, pins["a0"])
        mark = grads[0][2]
        pins["nb"] += out[0].step_core()
        pins["mix"] += out[1].step_first(mark) + out[2].step_second(mark) + attn_z.step(mark)
        pins["mix"] += out[0].step_first() + up_z.step(mark)
        tokens_grad, vec_one = finish_norm(pins["nb"])
        out[1].step_second(vec_one)
        out[0].step_second(vec_one)
        attn_z.step(vec_one)
        up_z.step(vec_one)
        mixed = finish(pins["mix"])
        attn_z.step(mixed)
        grad_up, grad_attn = up_z.step(), attn_z.step()
    else:
        for k in high + low:
            backward(k, [])
        mixed = finish([])
        tokens_grad, vec_one = finish_norm([])
        rejoin = lambda a, b: [a[1], a[0], b[1], b[0]]
        grad_up = scatter_all(rejoin(near1, near3), rejoin(far1, far3))
        grad_attn = scatter_all([g[0][0] for g in grads], [g[1][0] for g in grads])
    sum_qkv = [g[2] for g in grads]
    grad_down = tie(sum_down, vec_one).astype(F32)[:, :units].T
    grad_up, grad_attn = grad_up.astype(F32), grad_attn.astype(F32)
    grad_up = grad_up[:, :units]
    pieces = jnp.concatenate([jnp.concatenate(sum_qkv), jnp.concatenate(sum_dz)], axis=1)
    order = jnp.stack([lax.rem(z - t + size, size) for t in range(size)])
    pieces = jnp.take(pieces, order, axis=0)
    sums = sum_all(
        jnp.concatenate([pieces.reshape(-1), vec_one.reshape(-1), vec_two.reshape(-1), sum_e[0]]),
        cube,
    )
    per = qw + hidden
    mine = lax.dynamic_index_in_dim(sums[: size * per].reshape(size, per), z, 0, keepdims=False)
    rest = sums[size * per :].reshape(6, dim)
    at = span - base
    return (
        mixed[:seq],
        tokens_grad[:seq],
        rest[0],
        rest[1],
        grad_attn[:, span : 2 * span],
        mine[at : at + span],
        grad_attn[:, 2 * span : 3 * span],
        grad_attn[:, 3 * span :],
        mine[at + 2 * span : at + 3 * span],
        grad_attn[:, :span].T,
        rest[4],
        rest[2],
        rest[3],
        grad_up,
        mine[qw : qw + units],
        grad_down,
        rest[5],
    )


SPECS_IN = (
    P("dp", None), P("dp"), P("dp", None), P(), P(), P("dp", "tensor"), P("tensor"),
    P("dp", "tensor"), P("dp", "tensor"), P("tensor"), P("tensor", "dp"), P(), P(), P(),
    P("dp", "tensor"), P("tensor"), P("tensor", "dp"), P(),
)
SPECS_OUT = (
    P(("dp", "tensor"), None), P(("dp", "tensor"), None), P(), P(), P("dp", "tensor"), P("tensor"),
    P("dp", "tensor"), P("dp", "tensor"), P("tensor"), P("tensor", "dp"), P(), P(), P(),
    P("dp", "tensor"), P("tensor"), P("tensor", "dp"), P(),
)


def solution(mesh):
    return jax.shard_map(
        on_device, mesh=mesh, in_specs=SPECS_IN, out_specs=SPECS_OUT, check_vma=False
    )
```

time: 635 us -> 553 us (0.87)
  Pallas kernels: 274 us -> 244 us
  other arithmetic: 82.4 us -> 59.6 us
  local copies, waits for them, and re-layouts: 75.6 us -> 58 us
  starting transfers between devices: 65 us -> 49.8 us
  between operations: 3.31 us -> 16.7 us
  waiting for transfers between devices: 127 us -> 117 us
    unnamed x313 -> x205, local copies, waits for them, and re-layouts: 62.6 us -> 25.3 us
    pallas_call x20 -> x15, Pallas kernels: 274 us -> 244 us  [call(): pl.pallas_call(body, grid_spec=pltpu.PrefetchScalarGridSpec(num_scalar_pr...]
    ppermute x21 -> x12, waiting for transfers between devices: 59.9 us -> 32.4 us  [ring(): lax.ppermute(value, 'tensor', [(i, (i + by) % size) for i in range(size)])]
    convert_element_type x27 -> x18, other arithmetic: 37.1 us -> 14.6 us  [the longest x6 12 us: step(): self.total = ring(total.astype(BF), -1, self.size)]
    another operation x15 -> x34, other arithmetic: 12 us -> 31.8 us  [the longest x10 13.9 us: gather_pieces(): own = jnp.stack([jnp.stack(pair) for pair in zip(nears, fars)])]
    another operation x12 -> x2, other arithmetic: 17.3 us -> 0.2 us  [gather_near(): return jnp.stack([mine, swap(mine, (ACROSS, ALONG)[group])])]
    ppermute x55 -> x41, waiting for transfers between devices: 66.9 us -> 81.4 us  [swap(): lax.ppermute(value, 'dp', [(i, i ^ offset) for i in range(lax.axis_size('...]
    slice x4 -> x12, local copies, waits for them, and re-layouts: 0.01 us -> 9.75 us  [the longest x4 7.93 us: split(): return [value[i] for i in range(count)]]
  transfers between devices with their start and end apart: 78 -> 57, of which waited for: 17 -> 19; matrix products, arithmetic and copies ran while one was open for 15% -> 16% of each run, Pallas kernels for 44% -> 45%
where the time goes in v2:
time: 553 us; the launch traced here: 544 us
  Pallas kernels  244 us (44%)
  waiting for transfers between devices  117 us (21%)
  other arithmetic  59.6 us (11%)
  local copies, waits for them, and re-layouts  58 us (10%)
  starting transfers between devices  49.8 us (9%)
  between operations  16.7 us (3%)
    pallas_call x15, Pallas kernels, call(): pl.pallas_call(body, grid_spec=pltpu.PrefetchScalarGridSpec(num_scalar_pr...  244 us
    ppermute x41, waiting for transfers between devices, swap(): lax.ppermute(value, 'dp', [(i, i ^ offset) for i in range(lax.axis_size('...  81.4 us
    ppermute x12, waiting for transfers between devices, ring(): lax.ppermute(value, 'tensor', [(i, (i + by) % size) for i in range(size)])  32.4 us
    ppermute x41, starting transfers between devices, swap(): lax.ppermute(value, 'dp', [(i, i ^ offset) for i in range(lax.axis_size('...  30.3 us
    unnamed x205, local copies, waits for them, and re-layouts  25.3 us
    ppermute x12, starting transfers between devices, ring(): lax.ppermute(value, 'tensor', [(i, (i + by) % size) for i in range(size)])  19.1 us
    another operation x10, other arithmetic, gather_pieces(): own = jnp.stack([jnp.stack(pair) for pair in zip(nears, fars)])  13.9 us
    another operation x16, other arithmetic, send(): value = swap(jnp.stack([v for i in mine for v in outs[i]]), link)  13.4 us
  transfers between devices with their start and end apart: 57, of which 19 were waited for; matrix products, arithmetic and copies ran while one was open for 16% of the time, Pallas kernels for 45%

profile of v2, /device:TPU:0, one launch (start us, length us, event | category | flops | bytes accessed | tf_op | source)
XLA Modules:
  0.0 544.4 jit_solution(4749687059944466693)
XLA Ops:
  12.1 3.1 collective-permute-start.2
  26.1 6.7 %norm_one.1 = (bf16[768,1152]{1,0:T(8,128)(2,1)S(1)}, bf16[1152,768]{1,0:T(8,128)(2,1)S(1)}, bf16[1152,768]{1,0:T(8,128)(2,1)S(1)}, f32[1,1152]{1,0:T(1,128)S(1)}) custom-call(s32[3]{0:T(128)S(1)} %pad_add_fusion.refs_0_, bf16[768,1152]{1,0:T(8,128)(2,1)S(1)} %pad.21.refs_1_.refs_13_.refs_18_, bf16[768,1152]{1,0:T(8,128)(2,1)S(1)} %pad.22.refs_2_.refs_16_.refs_18_, ...), custom_call_target="tpu_custom_call" | custom-call | flops 6899999744 | bytes 600000 | tf_op jit(solution)/shard_map/norm_one/pallas_call | solution.py:63
  43.1 8.9 %collective-permute-done.6 = bf16[144,1152]{1,0:T(8,128)(2,1)} collective-permute-done((bf16[144,1152]{1,0:T(8,128)(2,1)}, bf16[144,1152]{1,0:T(8,128)(2,1)}, u32[]{:S(2)}, u32[]{:S(2)}) %collective-permute-start.6) | collective-permute-done | bytes 331808 | tf_op jit(solution)/shard_map/ppermute | solution.py:613
  52.0 4.3 collective-permute-start.7
  62.2 8.0 %collective-permute-done.7 = bf16[144,1152]{1,0:T(8,128)(2,1)} collective-permute-done((bf16[144,1152]{1,0:T(8,128)(2,1)}, bf16[144,1152]{1,0:T(8,128)(2,1)}, u32[]{:S(2)}, u32[]{:S(2)}) %collective-permute-start.7) | collective-permute-done | bytes 331808 | tf_op jit(solution)/shard_map/ppermute | solution.py:613
  73.3 6.2 %collective-permute-done.18 = bf16[144,1152]{1,0:T(8,128)(2,1)} collective-permute-done((bf16[144,1152]{1,0:T(8,128)(2,1)}, bf16[144,1152]{1,0:T(8,128)(2,1)}, u32[]{:S(2)}, u32[]{:S(2)}) %collective-permute-start.18) | collective-permute-done | bytes 331808 | tf_op jit(solution)/shard_map/ppermute | solution.py:617
  84.4 4.2 collective-permute-done.11
  94.0 18.3 %collective-permute-done.19 = bf16[2,144,1152]{2,1,0:T(8,128)(2,1)} collective-permute-done((bf16[2,144,1152]{2,1,0:T(8,128)(2,1)}, bf16[2,144,1152]{2,1,0:T(8,128)(2,1)}, u32[]{:S(2)}, u32[]{:S(2)}) %collective-permute-start.19) | collective-permute-done | bytes 663584 | tf_op jit(solution)/shard_map/ppermute | solution.py:617
  112.4 2.7 maximum_bitcast_fusion.2
  120.5 13.1 %collective-permute-done.10 = bf16[160,1152]{1,0:T(8,128)(2,1)S(1)} collective-permute-done((bf16[160,1152]{1,0:T(8,128)(2,1)}, bf16[160,1152]{1,0:T(8,128)(2,1)S(1)}, u32[]{:S(2)}, u32[]{:S(2)}) %collective-permute-start.10) | collective-permute-done | bytes 368672 | tf_op jit(solution)/shard_map/ppermute | solution.py:613
  138.7 10.4 %collective-permute-done.14 = bf16[2,144,1152]{2,1,0:T(8,128)(2,1)S(1)} collective-permute-done((bf16[2,144,1152]{2,1,0:T(8,128)(2,1)S(1)}, bf16[2,144,1152]{2,1,0:T(8,128)(2,1)S(1)}, u32[]{:S(2)}, u32[]{:S(2)}) %collective-permute-start.14) | collective-permute-done | bytes 663584 | tf_op jit(solution)/shard_map/ppermute | solution.py:617
  149.3 6.5 %collective-permute-done.13 = bf16[2,144,1152]{2,1,0:T(8,128)(2,1)S(1)} collective-permute-done((bf16[2,144,1152]{2,1,0:T(8,128)(2,1)S(1)}, bf16[2,144,1152]{2,1,0:T(8,128)(2,1)S(1)}, u32[]{:S(2)}, u32[]{:S(2)}) %collective-permute-start.13) | collective-permute-done | bytes 663584 | tf_op jit(solution)/shard_map/ppermute | solution.py:617
  158.0 8.1 %attn_fwd.6 = (bf16[768,896]{1,0:T(8,128)(2,1)S(1)}, bf16[768,384]{1,0:T(8,128)(2,1)S(1)}, f32[8,768]{1,0:T(8,128)S(1)}) custom-call(s32[3]{0:T(128)S(1)} %pad_add_fusion.refs_0_, bf16[2,2,2,144,1152]{4,3,2,1,0:T(8,128)(2,1)S(1)} %pad_maximum_fusion.refs_1_.refs_3_, bf16[2,2,2,144,1152]{4,3,2,1,0:T(8,128)(2,1)} %collective-permute-done.5.refs_2_.refs_4_, ...), custom_call_target="tpu_custom_call" | custom-call | flops 9200000000 | bytes 800000 | tf_op jit(solution)/shard_map/attn_fwd/pallas_call | solution.py:63
  167.2 7.9 %attn_fwd.4 = (bf16[768,896]{1,0:T(8,128)(2,1)S(1)}, bf16[768,384]{1,0:T(8,128)(2,1)S(1)}, f32[8,768]{1,0:T(8,128)S(1)}) custom-call(s32[3]{0:T(128)S(1)} %pad_add_fusion.refs_0_, bf16[2,2,2,144,1152]{4,3,2,1,0:T(8,128)(2,1)} %pad_maximum_fusion.2.refs_1_.refs_5_.refs_7_, bf16[2,2,2,144,1152]{4,3,2,1,0:T(8,128)(2,1)} %collective-permute-done.20.refs_2_.refs_6_.refs_8_, ...), custom_call_target="tpu_custom_call" | custom-call | flops 9200000000 | bytes 800000 | tf_op jit(solution)/shard_map/attn_fwd/pallas_call | solution.py:63
  175.2 5.1 collective-permute-done.17.refs_5_.refs_11_.refs_17_.refs_23_
  181.8 8.2 %attn_fwd.5 = (bf16[768,896]{1,0:T(8,128)(2,1)S(1)}, bf16[768,384]{1,0:T(8,128)(2,1)S(1)}, f32[8,768]{1,0:T(8,128)S(1)}) custom-call(s32[3]{0:T(128)S(1)} %pad_add_fusion.refs_0_, bf16[2,2,2,144,1152]{4,3,2,1,0:T(8,128)(2,1)S(1)} %pad_maximum_fusion.refs_1_.refs_3_, bf16[2,2,2,144,1152]{4,3,2,1,0:T(8,128)(2,1)} %collective-permute-done.5.refs_2_.refs_4_, ...), custom_call_target="tpu_custom_call" | custom-call | flops 9200000000 | bytes 800000 | tf_op jit(solution)/shard_map/attn_fwd/pallas_call | solution.py:63
  191.1 8.1 %attn_fwd.7 = (bf16[768,896]{1,0:T(8,128)(2,1)S(1)}, bf16[768,384]{1,0:T(8,128)(2,1)S(1)}, f32[8,768]{1,0:T(8,128)S(1)}) custom-call(s32[3]{0:T(128)S(1)} %pad_add_fusion.refs_0_, bf16[2,2,2,144,1152]{4,3,2,1,0:T(8,128)(2,1)} %pad_maximum_fusion.2.refs_1_.refs_5_.refs_7_, bf16[2,2,2,144,1152]{4,3,2,1,0:T(8,128)(2,1)} %collective-permute-done.20.refs_2_.refs_6_.refs_8_, ...), custom_call_target="tpu_custom_call" | custom-call | flops 9200000000 | bytes 800000 | tf_op jit(solution)/shard_map/attn_fwd/pallas_call | solution.py:63
  200.4 15.0 %norm_two.1 = (f32[768,1152]{1,0:T(8,128)}, bf16[768,1152]{1,0:T(8,128)(2,1)S(1)}, bf16[1152,768]{1,0:T(8,128)(2,1)S(1)}) custom-call(s32[3]{0:T(128)S(1)} %pad_add_fusion.refs_0_, bf16[2,2,2,144,1152]{4,3,2,1,0:T(8,128)(2,1)S(1)} %pad_maximum_fusion.refs_1_.refs_3_, bf16[2,2,2,144,1152]{4,3,2,1,0:T(8,128)(2,1)} %collective-permute-done.5.refs_2_.refs_4_, ...), custom_call_target="tpu_custom_call" | custom-call | flops 13799999488 | bytes 1200000 | tf_op jit(solution)/shard_map/norm_two/pallas_call | solution.py:63
  217.9 34.4 %ffn_one.1 = (bf16[4,768,1152]{2,1,0:T(8,128)(2,1)}, bf16[4,768,1152]{2,1,0:T(8,128)(2,1)}, bf16[8,4,144,1152]{3,2,1,0:T(8,128)(2,1)}) custom-call(s32[3]{0:T(128)} %copy-done.22, bf16[2,2,144,1152]{3,2,1,0:T(8,128)(2,1)} %copy-done.75, bf16[2,2,144,1152]{3,2,1,0:T(8,128)(2,1)} %copy-done.73, ...), custom_call_target="tpu_custom_call" | custom-call | flops 34500001792 | bytes 3000000 | tf_op jit(solution)/shard_map/ffn_one/pallas_call | solution.py:63
  252.4 23.9 %ffn_two.2 = (bf16[2,576,1152]{2,1,0:T(8,128)(2,1)}, bf16[2,576,1152]{2,1,0:T(8,128)(2,1)}, f32[2,1,1152]{2,1,0:T(1,128)}, f32[768,1152]{1,0:T(8,128)}) custom-call(s32[3]{0:T(128)} %copy-done.22, bf16[2,2,144,1152]{3,2,1,0:T(8,128)(2,1)} %copy-done.75, bf16[2,2,144,1152]{3,2,1,0:T(8,128)(2,1)} %copy-done.73, ...), custom_call_target="tpu_custom_call" | custom-call | flops 27599998976 | bytes 2400000 | tf_op jit(solution)/shard_map/ffn_two/pallas_call | solution.py:63
  276.8 34.2 %ffn_two.3 = (bf16[2,576,1152]{2,1,0:T(8,128)(2,1)}, bf16[2,576,1152]{2,1,0:T(8,128)(2,1)}, f32[2,1,1152]{2,1,0:T(1,128)}, f32[768,1152]{1,0:T(8,128)}, bf16[768...) custom-call(s32[3]{0:T(128)} %copy-done.22, bf16[2,2,144,1152]{3,2,1,0:T(8,128)(2,1)} %copy-done.75, ...), custom_call_target="tpu_custom_call" | custom-call | flops 34500001792 | bytes 3000000 | tf_op jit(solution)/shard_map/ffn_two/pallas_call | solution.py:63
  322.8 15.8 %attn_bwd.4 = (bf16[1,576,1152]{2,1,0:T(8,128)(2,1)S(1)}, bf16[1,576,1152]{2,1,0:T(8,128)(2,1)S(1)}, f32[1,896]{1,0:T(1,128)S(1)}, bf16[768,896]{1,0:T(8,128)(2,1)S(1)}) custom-call(s32[3]{0:T(128)S(1)} %copy-done.23, bf16[2,2,2,144,1152]{4,3,2,1,0:T(8,128)(2,1)} %pad_maximum_fusion.2.refs_1_.refs_5_.refs_7_, ...), custom_call_target="tpu_custom_call" | custom-call | flops 19549999104 | bytes 1700000 | tf_op jit(solution)/shard_map/attn_bwd/pallas_call | solution.py:63
  352.6 15.4 %attn_bwd.6 = (bf16[1,576,1152]{2,1,0:T(8,128)(2,1)S(1)}, bf16[1,576,1152]{2,1,0:T(8,128)(2,1)}, f32[1,896]{1,0:T(1,128)S(1)}, bf16[768,896]{1,0:T(8,128)(2,1)S(1)}) custom-call(s32[3]{0:T(128)S(1)} %copy-done.23, bf16[2,2,2,144,1152]{4,3,2,1,0:T(8,128)(2,1)} %pad_maximum_fusion.2.refs_1_.refs_5_.refs_7_, ...), custom_call_target="tpu_custom_call" | custom-call | flops 19549999104 | bytes 1700000 | tf_op jit(solution)/shard_map/attn_bwd/pallas_call | solution.py:63
  376.1 6.0 %collective-permute-done.26.refs_4_ = bf16[1,144,1152]{2,1,0:T(8,128)(2,1)S(1)} collective-permute-done((bf16[1,144,1152]{2,1,0:T(8,128)(2,1)S(1)}, bf16[1,144,1152]{2,1,0:T(8,128)(2,1)S(1)}, u32[]{:S(2)}, u32[]{:S(2)}) %collective-permute-start.26) | collective-permute-done | bytes 331808 | tf_op jit(solution)/shard_map/ppermute | solution.py:617
  382.8 15.5 %attn_bwd.5 = (bf16[1,576,1152]{2,1,0:T(8,128)(2,1)S(1)}, bf16[1,576,1152]{2,1,0:T(8,128)(2,1)}, f32[1,896]{1,0:T(1,128)S(1)}, bf16[768,896]{1,0:T(8,128)(2,1)S(1)}) custom-call(s32[3]{0:T(128)S(1)} %copy-done.23, bf16[2,2,2,144,1152]{4,3,2,1,0:T(8,128)(2,1)S(1)} %pad_maximum_fusion.refs_1_.refs_3_, ...), custom_call_target="tpu_custom_call" | custom-call | flops 19549999104 | bytes 1700000 | tf_op jit(solution)/shard_map/attn_bwd/pallas_call | solution.py:63
  400.3 3.4 collective-permute-start.43
  405.8 15.5 %attn_bwd.7 = (bf16[1,576,1152]{2,1,0:T(8,128)(2,1)S(1)}, bf16[1,576,1152]{2,1,0:T(8,128)(2,1)S(1)}, f32[1,896]{1,0:T(1,128)S(1)}, bf16[768,896]{1,0:T(8,128)(2,1)S(1)}) custom-call(s32[3]{0:T(128)S(1)} %copy-done.23, bf16[2,2,2,144,1152]{4,3,2,1,0:T(8,128)(2,1)S(1)} %pad_maximum_fusion.refs_1_.refs_3_, ...), custom_call_target="tpu_custom_call" | custom-call | flops 19549999104 | bytes 1700000 | tf_op jit(solution)/shard_map/attn_bwd/pallas_call | solution.py:63
  430.5 10.1 %collective-permute-done.37.refs_10_ = bf16[2,144,1152]{2,1,0:T(8,128)(2,1)S(1)} collective-permute-done((bf16[2,144,1152]{2,1,0:T(8,128)(2,1)S(1)}, bf16[2,144,1152]{2,1,0:T(8,128)(2,1)S(1)}, u32[]{:S(2)}, u32[]{:S(2)}) %collective-permute-start.37) | collective-permute-done | bytes 663584 | tf_op jit(solution)/shard_map/ppermute | solution.py:617
  450.5 20.3 %norm_back.1 = (bf16[768,1152]{1,0:T(8,128)(2,1)S(1)}, f32[2,1152]{1,0:T(2,128)S(1)}) custom-call(s32[3]{0:T(128)S(1)} %copy-done.23, bf16[2,2,2,144,1152]{4,3,2,1,0:T(8,128)(2,1)} %copy-done, bf16[2,2,2,144,1152]{4,3,2,1,0:T(8,128)(2,1)} %collective-permute-done.5.refs_2_.refs_4_, bf16[2,2,2,144,1152]{4,3,2,1,0:T(8,128)(2,1)} %copy-done, ...), custom_call_target="tpu_custom_call" | custom-call | flops 20700000256 | bytes 1800000 | tf_op jit(solution)/shard_map/norm_back/pallas_call | solution.py:63
  483.7 5.1 collective-permute-done.47
  501.0 5.7 %collective-permute-done.42.refs_8_ = bf16[2,144,1152]{2,1,0:T(8,128)(2,1)} collective-permute-done((bf16[2,144,1152]{2,1,0:T(8,128)(2,1)}, bf16[2,144,1152]{2,1,0:T(8,128)(2,1)}, u32[]{:S(2)}, u32[]{:S(2)}) %collective-permute-start.42) | collective-permute-done | bytes 663584 | tf_op jit(solution)/shard_map/ppermute | solution.py:617
  508.7 14.7 %mixed.1 = bf16[768,1152]{1,0:T(8,128)(2,1)S(1)} custom-call(s32[3]{0:T(128)S(1)} %copy-done.23, bf16[32,144,1152]{2,1,0:T(8,128)(2,1)} %bitcast.356, bf16[32,144,1152]{2,1,0:T(8,128)(2,1)} %bitcast.357, bf16[32,144,1152]{2,1,0:T(8,128)(2,1)} %bitcast.358, bf16[32,144,1152]{2,1,0:T(8,128)(2,1)} %bitcast.359, ...), custom_call_target="tpu_custom_call" | custom-call | flops 16099999744 | bytes 1400000 | tf_op jit(solution)/shard_map/mixed/pallas_call | solution.py:63
  (449 shorter events, 162.9 us)
Async XLA Ops:
  7.2 245.2 %all-gather.3.cloned.1.call-start = ((), (), s32[]{:S(2)}) async-start(), calls=%async_computation.2 | async-start | bytes 10948608 | tf_op jit(solution)/shard_map/all_gather | solution.py:631
  12.1 26.5 %collective-permute-start.2 = (bf16[144,1152]{1,0:T(8,128)(2,1)}, bf16[144,1152]{1,0:T(8,128)(2,1)}, u32[]{:S(2)}, u32[]{:S(2)}) collective-permute-start(bf16[144,1152]{1,0:T(8,128)(2,1)} %concatenate.75), channel_id=1, source_target_pairs={{0,1},{1,2},{2,3},{3,0},{4,5},{5,6},{6,7},{7,4},{8,9},{9,10},{10,1... | collective-permute-start | bytes 995336 | tf_op jit(solution)/shard_map/ppermute | solution.py:613
  15.2 41.1 %collective-permute-start = (bf16[144,1152]{1,0:T(8,128)(2,1)}, bf16[144,1152]{1,0:T(8,128)(2,1)}, u32[]{:S(2)}, u32[]{:S(2)}) collective-permute-start(bf16[144,1152]{1,0:T(8,128)(2,1)} %concatenate.75), channel_id=1, source_target_pairs={{0,8},{4,12},{8,0},{12,4},{16,24},{20,28},{24,16},{28,20},{1,9},{5... | collective-permute-start | bytes 995336 | tf_op jit(solution)/shard_map/ppermute | solution.py:617
  17.6 453.3 %reduce-scatter.2.cloned.1.call-start = ((), (), s32[]{:S(2)}) async-start(), calls=%async_computation.1 | async-start | bytes 10948608 | tf_op jit(solution)/shard_map/reduce_scatter | solution.py:723
  57.4 25.8 %collective-permute-start.1 = (bf16[2,144,1152]{2,1,0:T(8,128)(2,1)S(1)}, bf16[2,144,1152]{2,1,0:T(8,128)(2,1)}, u32[]{:S(2)}, u32[]{:S(2)}) collective-permute-start(bf16[2,144,1152]{2,1,0:T(8,128)(2,1)S(1)} %get-tuple-element.253), channel_id=1, source_target_pairs={{0,16},{4,20},{8,24},{12,28},{16,0},{20,4},{24,8},{28,12},{1,17},{... | collective-permute-start | bytes 1990664 | tf_op jit(solution)/shard_map/ppermute | solution.py:617
  60.1 30.6 %collective-permute-start.4 = (bf16[2,144,1152]{2,1,0:T(8,128)(2,1)S(1)}, bf16[2,144,1152]{2,1,0:T(8,128)(2,1)S(1)}, u32[]{:S(2)}, u32[]{:S(2)}) collective-permute-start(bf16[2,144,1152]{2,1,0:T(8,128)(2,1)S(1)} %get-tuple-element.255), channel_id=1, source_target_pairs={{0,8},{4,12},{8,0},{12,4},{16,24},{20,28},{24,16},{28,20},{1,9},{5... | collective-permute-start | bytes 1990664 | tf_op jit(solution)/shard_map/ppermute | solution.py:617
  81.7 30.7 %collective-permute-start.19 = (bf16[2,144,1152]{2,1,0:T(8,128)(2,1)}, bf16[2,144,1152]{2,1,0:T(8,128)(2,1)}, u32[]{:S(2)}, u32[]{:S(2)}) collective-permute-start(bf16[2,144,1152]{2,1,0:T(8,128)(2,1)} %get-tuple-element.245), channel_id=1, source_target_pairs={{0,16},{4,20},{8,24},{12,28},{16,0},{20,4},{24,8},{28,12},{1,17},{... | collective-permute-start | bytes 1990664 | tf_op jit(solution)/shard_map/ppermute | solution.py:617
  90.7 26.5 %collective-permute-start.12 = (bf16[2,144,1152]{2,1,0:T(8,128)(2,1)}, bf16[2,144,1152]{2,1,0:T(8,128)(2,1)}, u32[]{:S(2)}, u32[]{:S(2)}) collective-permute-start(bf16[2,144,1152]{2,1,0:T(8,128)(2,1)} %get-tuple-element.247), channel_id=1, source_target_pairs={{0,8},{4,12},{8,0},{12,4},{16,24},{20,28},{24,16},{28,20},{1,9},{5... | collective-permute-start | bytes 1990664 | tf_op jit(solution)/shard_map/ppermute | solution.py:617
  91.1 66.0 %collective-permute-start.5 = (bf16[2,2,2,144,1152]{4,3,2,1,0:T(8,128)(2,1)S(1)}, bf16[2,2,2,144,1152]{4,3,2,1,0:T(8,128)(2,1)}, u32[]{:S(2)}, u32[]{:S(2)}) collective-permute-start(bf16[2,2,2,144,1152]{4,3,2,1,0:T(8,128)(2,1)S(1)} %pad_maximum_fusion.refs_1_.refs_3_), channel_id=1, source_target_pairs={{0,4},{4,0},{8,12},{12,8},{16,20},{20,16},{24,28},{28,24},{1,5},{5... | collective-permute-start | bytes 7962632 | tf_op jit(solution)/shard_map/ppermute | solution.py:617
  120.5 46.8 %collective-permute-start.20 = (bf16[2,2,2,144,1152]{4,3,2,1,0:T(8,128)(2,1)}, bf16[2,2,2,144,1152]{4,3,2,1,0:T(8,128)(2,1)}, u32[]{:S(2)}, u32[]{:S(2)}) collective-permute-start(bf16[2,2,2,144,1152]{4,3,2,1,0:T(8,128)(2,1)} %pad_maximum_fusion.2.refs_1_.refs_5_.refs_7_), channel_id=1, source_target_pairs={{0,4},{4,0},{8,12},{12,8},{16,20},{20,16},{24,28},{28,24},{1,5},{5... | collective-permute-start | bytes 7962632 | tf_op jit(solution)/shard_map/ppermute | solution.py:617
  149.2 31.0 %collective-permute-start.17 = (bf16[2,2,144,1152]{3,2,1,0:T(8,128)(2,1)S(1)}, bf16[2,2,144,1152]{3,2,1,0:T(8,128)(2,1)S(1)}, u32[]{:S(2)}, u32[]{:S(2)}) collective-permute-start(bf16[2,2,144,1152]{3,2,1,0:T(8,128)(2,1)S(1)} %get-tuple-element.223.refs_2_.refs_8_.refs_14_.refs_20_), channel_id=1, source_target_pairs={{0,8},{4,12},{8,0},{12,4},{16,24},{20,28},{24,16},{28,20},{1,9},{5... | collective-permute-start | bytes 3981320 | tf_op jit(solution)/shard_map/ppermute | solution.py:617
  156.1 24.2 %collective-permute-start.16 = (bf16[2,2,144,1152]{3,2,1,0:T(8,128)(2,1)S(1)}, bf16[2,2,144,1152]{3,2,1,0:T(8,128)(2,1)S(1)}, u32[]{:S(2)}, u32[]{:S(2)}) collective-permute-start(bf16[2,2,144,1152]{3,2,1,0:T(8,128)(2,1)S(1)} %get-tuple-element.221.refs_1_.refs_7_.refs_13_.refs_19_), channel_id=1, source_target_pairs={{0,16},{4,20},{8,24},{12,28},{16,0},{20,4},{24,8},{28,12},{1,17},{... | collective-permute-start | bytes 3981320 | tf_op jit(solution)/shard_map/ppermute | solution.py:617
  157.2 60.7 %collective-permute-start.15 = (bf16[2,2,2,144,1152]{4,3,2,1,0:T(8,128)(2,1)S(1)}, bf16[2,2,2,144,1152]{4,3,2,1,0:T(8,128)(2,1)}, u32[]{:S(2)}, u32[]{:S(2)}) collective-permute-start(bf16[2,2,2,144,1152]{4,3,2,1,0:T(8,128)(2,1)S(1)} %pad_maximum_fusion.1), channel_id=1, source_target_pairs={{0,4},{4,0},{8,12},{12,8},{16,20},{20,16},{24,28},{28,24},{1,5},{5... | collective-permute-start | bytes 7962632 | tf_op jit(solution)/shard_map/ppermute | solution.py:617
  181.8 36.1 %collective-permute-start.21 = (bf16[2,2,2,144,1152]{4,3,2,1,0:T(8,128)(2,1)S(1)}, bf16[2,2,2,144,1152]{4,3,2,1,0:T(8,128)(2,1)}, u32[]{:S(2)}, u32[]{:S(2)}) collective-permute-start(bf16[2,2,2,144,1152]{4,3,2,1,0:T(8,128)(2,1)S(1)} %pad_maximum_fusion.3), channel_id=1, source_target_pairs={{0,4},{4,0},{8,12},{12,8},{16,20},{20,16},{24,28},{28,24},{1,5},{5... | collective-permute-start | bytes 7962632 | tf_op jit(solution)/shard_map/ppermute | solution.py:617
  276.2 40.4 %collective-permute-start.22 = (bf16[2,576,1152]{2,1,0:T(8,128)(2,1)}, bf16[2,576,1152]{2,1,0:T(8,128)(2,1)}, u32[]{:S(2)}, u32[]{:S(2)}) collective-permute-start(bf16[2,576,1152]{2,1,0:T(8,128)(2,1)} %get-tuple-element.123), channel_id=1, source_target_pairs={{0,4},{4,0},{8,12},{12,8},{16,20},{20,16},{24,28},{28,24},{1,5},{5... | collective-permute-start | bytes 7962632 | tf_op jit(solution)/shard_map/ppermute | solution.py:617
  311.8 28.5 %collective-permute-start.27 = (bf16[2,576,1152]{2,1,0:T(8,128)(2,1)}, bf16[2,576,1152]{2,1,0:T(8,128)(2,1)}, u32[]{:S(2)}, u32[]{:S(2)}) collective-permute-start(bf16[2,576,1152]{2,1,0:T(8,128)(2,1)} %get-tuple-element.137), channel_id=1, source_target_pairs={{0,4},{4,0},{8,12},{12,8},{16,20},{20,16},{24,28},{28,24},{1,5},{5... | collective-permute-start | bytes 7962632 | tf_op jit(solution)/shard_map/ppermute | solution.py:617
  320.2 28.0 %collective-permute-start.23 = (bf16[2,144,1152]{2,1,0:T(8,128)(2,1)S(1)}, bf16[2,144,1152]{2,1,0:T(8,128)(2,1)S(1)}, u32[]{:S(2)}, u32[]{:S(2)}) collective-permute-start(bf16[2,144,1152]{2,1,0:T(8,128)(2,1)S(1)} %pad_maximum_fusion.12), channel_id=1, source_target_pairs={{0,8},{4,12},{8,0},{12,4},{16,24},{20,28},{24,16},{28,20},{1,9},{5... | collective-permute-start | bytes 1990664 | tf_op jit(solution)/shard_map/ppermute | solution.py:617
  321.0 27.2 %collective-permute-start.24 = (bf16[2,144,1152]{2,1,0:T(8,128)(2,1)S(1)}, bf16[2,144,1152]{2,1,0:T(8,128)(2,1)S(1)}, u32[]{:S(2)}, u32[]{:S(2)}) collective-permute-start(bf16[2,144,1152]{2,1,0:T(8,128)(2,1)S(1)} %pad_maximum_fusion.13), channel_id=1, source_target_pairs={{0,16},{4,20},{8,24},{12,28},{16,0},{20,4},{24,8},{28,12},{1,17},{... | collective-permute-start | bytes 1990664 | tf_op jit(solution)/shard_map/ppermute | solution.py:617
  339.7 36.1 %collective-permute-start.30 = (bf16[1,576,1152]{2,1,0:T(8,128)(2,1)S(1)}, bf16[1,576,1152]{2,1,0:T(8,128)(2,1)S(1)}, u32[]{:S(2)}, u32[]{:S(2)}) collective-permute-start(bf16[1,576,1152]{2,1,0:T(8,128)(2,1)S(1)} %get-tuple-element.140), channel_id=1, source_target_pairs={{0,4},{4,0},{8,12},{12,8},{16,20},{20,16},{24,28},{28,24},{1,5},{5... | collective-permute-start | bytes 3981320 | tf_op jit(solution)/shard_map/ppermute | solution.py:617
  344.2 24.9 %collective-permute-start.28 = (bf16[2,144,1152]{2,1,0:T(8,128)(2,1)}, bf16[2,144,1152]{2,1,0:T(8,128)(2,1)S(1)}, u32[]{:S(2)}, u32[]{:S(2)}) collective-permute-start(bf16[2,144,1152]{2,1,0:T(8,128)(2,1)} %pad_maximum_fusion.14), channel_id=1, source_target_pairs={{0,8},{4,12},{8,0},{12,4},{16,24},{20,28},{24,16},{28,20},{1,9},{5... | collective-permute-start | bytes 1990664 | tf_op jit(solution)/shard_map/ppermute | solution.py:617
  350.4 31.7 %collective-permute-start.26 = (bf16[1,144,1152]{2,1,0:T(8,128)(2,1)S(1)}, bf16[1,144,1152]{2,1,0:T(8,128)(2,1)S(1)}, u32[]{:S(2)}, u32[]{:S(2)}) collective-permute-start(bf16[1,144,1152]{2,1,0:T(8,128)(2,1)S(1)} %fusion.42), channel_id=1, source_target_pairs={{0,16},{4,20},{8,24},{12,28},{16,0},{20,4},{24,8},{28,12},{1,17},{... | collective-permute-start | bytes 995336 | tf_op jit(solution)/shard_map/ppermute | solution.py:617
  351.9 30.9 %collective-permute-start.25 = (bf16[1,144,1152]{2,1,0:T(8,128)(2,1)}, bf16[1,144,1152]{2,1,0:T(8,128)(2,1)S(1)}, u32[]{:S(2)}, u32[]{:S(2)}) collective-permute-start(bf16[1,144,1152]{2,1,0:T(8,128)(2,1)} %fusion.41), channel_id=1, source_target_pairs={{0,8},{4,12},{8,0},{12,4},{16,24},{20,28},{24,16},{28,20},{1,9},{5... | collective-permute-start | bytes 995336 | tf_op jit(solution)/shard_map/ppermute | solution.py:617
  372.5 32.8 %collective-permute-start.33 = (bf16[1,144,1152]{2,1,0:T(8,128)(2,1)S(1)}, bf16[1,144,1152]{2,1,0:T(8,128)(2,1)S(1)}, u32[]{:S(2)}, u32[]{:S(2)}) collective-permute-start(bf16[1,144,1152]{2,1,0:T(8,128)(2,1)S(1)} %fusion.44), channel_id=1, source_target_pairs={{0,16},{4,20},{8,24},{12,28},{16,0},{20,4},{24,8},{28,12},{1,17},{... | collective-permute-start | bytes 995336 | tf_op jit(solution)/shard_map/ppermute | solution.py:617
  374.4 31.4 %collective-permute-start.32 = (bf16[1,144,1152]{2,1,0:T(8,128)(2,1)S(1)}, bf16[1,144,1152]{2,1,0:T(8,128)(2,1)S(1)}, u32[]{:S(2)}, u32[]{:S(2)}) collective-permute-start(bf16[1,144,1152]{2,1,0:T(8,128)(2,1)S(1)} %fusion.43), channel_id=1, source_target_pairs={{0,8},{4,12},{8,0},{12,4},{16,24},{20,28},{24,16},{28,20},{1,9},{5... | collective-permute-start | bytes 995336 | tf_op jit(solution)/shard_map/ppermute | solution.py:617
  375.8 30.0 %collective-permute-start.35 = (bf16[1,576,1152]{2,1,0:T(8,128)(2,1)}, bf16[1,576,1152]{2,1,0:T(8,128)(2,1)S(1)}, u32[]{:S(2)}, u32[]{:S(2)}) collective-permute-start(bf16[1,576,1152]{2,1,0:T(8,128)(2,1)} %get-tuple-element.152), channel_id=1, source_target_pairs={{0,4},{4,0},{8,12},{12,8},{16,20},{20,16},{24,28},{28,24},{1,5},{5... | collective-permute-start | bytes 3981320 | tf_op jit(solution)/shard_map/ppermute | solution.py:617
  403.7 37.8 %collective-permute-start.31 = (bf16[1,576,1152]{2,1,0:T(8,128)(2,1)}, bf16[1,576,1152]{2,1,0:T(8,128)(2,1)}, u32[]{:S(2)}, u32[]{:S(2)}) collective-permute-start(bf16[1,576,1152]{2,1,0:T(8,128)(2,1)} %get-tuple-element.144), channel_id=1, source_target_pairs={{0,4},{4,0},{8,12},{12,8},{16,20},{20,16},{24,28},{28,24},{1,5},{5... | collective-permute-start | bytes 3981320 | tf_op jit(solution)/shard_map/ppermute | solution.py:617
  428.0 49.0 %collective-permute-start.44 = (bf16[144,1152]{1,0:T(8,128)(2,1)}, bf16[144,1152]{1,0:T(8,128)(2,1)}, u32[]{:S(2)}, u32[]{:S(2)}) collective-permute-start(bf16[144,1152]{1,0:T(8,128)(2,1)} %fusion.11), channel_id=1, source_target_pairs={{0,3},{1,0},{2,1},{3,2},{4,7},{5,4},{6,5},{7,6},{8,11},{9,8},{10,9... | collective-permute-start | bytes 995336 | tf_op jit(solution)/shard_map/ppermute | solution.py:613
  430.4 46.6 %collective-permute-start.40 = (bf16[144,1152]{1,0:T(8,128)(2,1)}, bf16[144,1152]{1,0:T(8,128)(2,1)}, u32[]{:S(2)}, u32[]{:S(2)}) collective-permute-start(bf16[144,1152]{1,0:T(8,128)(2,1)} %fusion.18), channel_id=1, source_target_pairs={{0,3},{1,0},{2,1},{3,2},{4,7},{5,4},{6,5},{7,6},{8,11},{9,8},{10,9... | collective-permute-start | bytes 995336 | tf_op jit(solution)/shard_map/ppermute | solution.py:613
  443.4 36.5 %collective-permute-start.38 = (bf16[1,144,1152]{2,1,0:T(8,128)(2,1)}, bf16[1,144,1152]{2,1,0:T(8,128)(2,1)}, u32[]{:S(2)}, u32[]{:S(2)}) collective-permute-start(bf16[1,144,1152]{2,1,0:T(8,128)(2,1)} %fusion.45), channel_id=1, source_target_pairs={{0,8},{4,12},{8,0},{12,4},{16,24},{20,28},{24,16},{28,20},{1,9},{5... | collective-permute-start | bytes 995336 | tf_op jit(solution)/shard_map/ppermute | solution.py:617
  477.0 49.1 %collective-permute-start.51 = (bf16[1,144,1152]{2,1,0:T(8,128)(2,1)}, bf16[1,144,1152]{2,1,0:T(8,128)(2,1)}, u32[]{:S(2)}, u32[]{:S(2)}) collective-permute-start(bf16[1,144,1152]{2,1,0:T(8,128)(2,1)} %fusion.48), channel_id=1, source_target_pairs={{0,16},{4,20},{8,24},{12,28},{16,0},{20,4},{24,8},{28,12},{1,17},{... | collective-permute-start | bytes 995336 | tf_op jit(solution)/shard_map/ppermute | solution.py:617
  482.1 42.6 %collective-permute-start.52 = (bf16[144,1152]{1,0:T(8,128)(2,1)}, bf16[144,1152]{1,0:T(8,128)(2,1)}, u32[]{:S(2)}, u32[]{:S(2)}) collective-permute-start(bf16[144,1152]{1,0:T(8,128)(2,1)} %fusion.6), channel_id=1, source_target_pairs={{0,3},{1,0},{2,1},{3,2},{4,7},{5,4},{6,5},{7,6},{8,11},{9,8},{10,9... | collective-permute-start | bytes 995336 | tf_op jit(solution)/shard_map/ppermute | solution.py:613
  495.6 32.1 %collective-permute-start.54 = (bf16[144,1152]{1,0:T(8,128)(2,1)}, bf16[144,1152]{1,0:T(8,128)(2,1)}, u32[]{:S(2)}, u32[]{:S(2)}) collective-permute-start(bf16[144,1152]{1,0:T(8,128)(2,1)} %fusion.4), channel_id=1, source_target_pairs={{0,3},{1,0},{2,1},{3,2},{4,7},{5,4},{6,5},{7,6},{8,11},{9,8},{10,9... | collective-permute-start | bytes 995336 | tf_op jit(solution)/shard_map/ppermute | solution.py:613
  (127 other events, 1829.5 us)
Sparse Core Ops, SparseCore 0:
  17.7 115.3 all-gather.2
  252.5 160.1 reduce-scatter.1

commit v3 on v2

--- a/solution.py
+++ b/solution.py
@@ -144,7 +144,7 @@
     def step(t, carry):
         return body(pl.ds(pl.multiple_of(t * STEP, STEP), STEP), carry)
 
-    return lax.fori_loop(0, total // STEP, step, carry)
+    return lax.fori_loop(0, total // STEP, step, carry, unroll=4)
 
 
 def norm_stats(rows):
@@ -454,10 +454,9 @@
         cols = slice(n, min(n + 256, width))
         pre = nn(a_ref[...], w[slot, :, cols]) + bias_ref[0, :, cols]
         square = pre * pre
-        bent = jnp.tanh(pre * (GELU_A + GELU_A * GELU_B * square))
-        half = 0.5 + 0.5 * bent
+        half = 0.5 + 0.5 * jnp.tanh(pre * (GELU_A + GELU_A * GELU_B * square))
         g_ref[0, :, cols] = (pre * half).astype(BF)
-        slope = half + 0.5 * pre * (1.0 - bent * bent) * (GELU_A + 3 * GELU_A * GELU_B * square)
+        slope = half + (half - half * half) * (pre * (2 * GELU_A + 6 * GELU_A * GELU_B * square))
         gp_ref[0, :, cols] = slope.astype(BF)
 
     @pl.when(step == 0)
@@ -661,28 +660,6 @@
     return swap(both, (ALONG, ACROSS)[group])
 
 
-def gather_pieces(nears, fars, firsts, rows):
-    own = jnp.stack([jnp.stack(pair) for pair in zip(nears, fars)])
-    arrays = [own, swap(own, CORE)]
-
-    def blocks(n, d, z):
-        first = firsts[n]
-        second = ACROSS + ALONG - first
-        return [
-            (
-                core,
-                (n, i, j),
-                pl.multiple_of(jnp.bitwise_xor(d, core * CORE + i * second + j * first) * rows, 16),
-                rows,
-            )
-            for core in range(2)
-            for i in range(2)
-            for j in range(2)
-        ]
-
-    return [Piece(arrays, partial(blocks, n)) for n in range(len(nears))]
-
-
 def gather_groups(both, both_core, far, far_core, rows):
     firsts = (ACROSS, ACROSS, ALONG, ALONG)
 
@@ -862,15 +839,8 @@
 
     every = list(range(size))
     pin = {}
+    attn_w = gather_all(own_attn, split)
     if cube:
-        held = gather_ring(own_attn)
-        firsts = [ACROSS if k % 2 == 0 else ALONG for k in every]
-        nears, fars = [], []
-        for k in every:
-            nears.append(jnp.stack([held[k], swap(held[k], firsts[k])]))
-            fars.append(swap(nears[k], ACROSS + ALONG - firsts[k]))
-        attn_w = gather_pieces(nears[:2], fars[:2], firsts[:2], rows)
-        attn_w += gather_pieces(nears[2:], fars[2:], firsts[2:], rows)
         bits = []
         for _ in range(3):
             top = lax.reduce_precision(own_bias[0], 8, 7)
@@ -880,30 +850,29 @@
         count = bits.shape[0]
         extra = up(-(-count // hidden), 16)
         bits = jnp.pad(bits, (0, extra * hidden - count)).reshape(extra, hidden)
-        ffn_held = gather_ring(tie(jnp.concatenate([own_up, bits]), held[-1]))
+        ffn_held = gather_ring(jnp.concatenate([own_up, bits]))
         bias = []
         for v in ffn_held:
             v = v[rows:].reshape(-1)[:count].reshape(3, -1).astype(F32)
             bias.append((v[0] + v[1] + v[2])[None])
-        ffn_held = ties(ffn_held, fars[3])
         up_held = [v[:rows] for v in ffn_held]
-        both_up = [gather_near(up_held, i) for i in range(2)]
+        both_up = [gather_near(up_held, 0), gather_near(ties(up_held, sum_e), 1)]
+        far_up = [gather_far(both_up[i], i) for i in range(2)]
+        core_up = swap(jnp.stack(both_up), CORE)
+        pin["attn0"] = [*far_up]
+        own_down = tie(own_down, *far_up)
     else:
         bias = gather_ring(own_bias)
-        attn_w, up_w = (gather_all(w, split) for w in (own_attn, own_up))
+        up_w = gather_all(own_up, split)
     kept = [
         attn_fwd(cfg, place, pin.get(f"attn{k}", []), attn_w[k], a1, bias[k][:, :qw]) for k in every
     ]
-    if cube:
-        far_up = [gather_far(both_up[i], i) for i in range(2)]
-        core_up = swap(jnp.stack(both_up), CORE)
     h, a2, a2t = norm_two(
         cfg, place, pin.get("norm_two", []), attn_w, x, b_out[None], gain_two[None], shift_two[None],
         [o for _, o, _ in kept],
     )
-    down_w = gather_all(own_down, split)
+    down_w = gather_all(tie(own_down, attn_w[0].arrays[0]), split)
     if cube:
-        far_up = ties(far_up, kept[3][2])
         up_w = gather_groups(both_up, core_up, far_up, swap(jnp.stack(far_up), CORE), rows)
     g, gp, g_down = ffn_one(
         cfg, place, pin.get("ffn_one", []), up_w, a2, jnp.stack(bias)[:, :, qw:], et

time: 553 us -> 505 us (0.913)
  Pallas kernels: 244 us -> 225 us
  starting transfers between devices: 49.8 us -> 38.7 us
  other arithmetic: 59.6 us -> 52.5 us
  local copies, waits for them, and re-layouts: 58 us -> 51.8 us
    pallas_call x15, Pallas kernels: 244 us -> 225 us  [call(): pl.pallas_call(body, grid_spec=pltpu.PrefetchScalarGridSpec(num_scalar_pr...]
    another operation x13 -> x0, other arithmetic: 16.8 us -> none  [the longest x10 13.9 us: gather_pieces(): own = jnp.stack([jnp.stack(pair) for pair in zip(nears, fars)])]
    ppermute x41 -> x31, starting transfers between devices: 30.3 us -> 21.1 us  [swap(): lax.ppermute(value, 'dp', [(i, i ^ offset) for i in range(lax.axis_size('...]
    all_gather x1 -> x2, waiting for transfers between devices: 0.02 us -> 8.51 us  [gather_all(): full = lax.all_gather(own, ('dp', 'tensor'), axis=0, tiled=False)]
    ppermute x41 -> x31, waiting for transfers between devices: 81.4 us -> 74.5 us  [swap(): lax.ppermute(value, 'dp', [(i, i ^ offset) for i in range(lax.axis_size('...]
    ppermute x12 -> x9, waiting for transfers between devices: 32.4 us -> 28.4 us  [ring(): lax.ppermute(value, 'tensor', [(i, (i + by) % size) for i in range(size)])]
    ppermute x12 -> x9, starting transfers between devices: 19.1 us -> 15.2 us  [ring(): lax.ppermute(value, 'tensor', [(i, (i + by) % size) for i in range(size)])]
    unnamed x205 -> x183, local copies, waits for them, and re-layouts: 25.3 us -> 22.4 us
  transfers between devices with their start and end apart: 57 -> 45, of which waited for: 19 -> 16; matrix products, arithmetic and copies ran while one was open for 16% -> 15% of each run, Pallas kernels for 45% -> 45%
where the time goes in v3:
time: 505 us; the launch traced here: 498 us
  Pallas kernels  225 us (45%)
  waiting for transfers between devices  114 us (23%)
  other arithmetic  52.5 us (10%)
  local copies, waits for them, and re-layouts  51.8 us (10%)
  starting transfers between devices  38.7 us (8%)
  between operations  16 us (3%)
    pallas_call x15, Pallas kernels, call(): pl.pallas_call(body, grid_spec=pltpu.PrefetchScalarGridSpec(num_scalar_pr...  225 us
    ppermute x31, waiting for transfers between devices, swap(): lax.ppermute(value, 'dp', [(i, i ^ offset) for i in range(lax.axis_size('...  74.5 us
    ppermute x9, waiting for transfers between devices, ring(): lax.ppermute(value, 'tensor', [(i, (i + by) % size) for i in range(size)])  28.4 us
    unnamed x183, local copies, waits for them, and re-layouts  22.4 us
    ppermute x31, starting transfers between devices, swap(): lax.ppermute(value, 'dp', [(i, i ^ offset) for i in range(lax.axis_size('...  21.1 us
    ppermute x9, starting transfers between devices, ring(): lax.ppermute(value, 'tensor', [(i, (i + by) % size) for i in range(size)])  15.2 us
    another operation x16, other arithmetic, send(): value = swap(jnp.stack([v for i in mine for v in outs[i]]), link)  14.1 us
    convert_element_type x6, other arithmetic, step(): self.total = ring(total.astype(BF), -1, self.size)  11.1 us
  transfers between devices with their start and end apart: 45, of which 16 were waited for; matrix products, arithmetic and copies ran while one was open for 15% of the time, Pallas kernels for 45%

profile of v3, /device:TPU:0, one launch (start us, length us, event | category | flops | bytes accessed | tf_op | source)
XLA Modules:
  0.0 498.4 jit_solution(13762593114627599518)
XLA Ops:
  13.8 3.0 collective-permute-start
  20.3 2.5 constant_dynamic-slice_fusion
  23.8 4.3 collective-permute-done
  32.5 11.2 %collective-permute-done.3 = bf16[160,1152]{1,0:T(8,128)(2,1)S(1)} collective-permute-done((bf16[160,1152]{1,0:T(8,128)(2,1)}, bf16[160,1152]{1,0:T(8,128)(2,1)S(1)}, u32[]{:S(2)}, u32[]{:S(2)}) %collective-permute-start.3) | collective-permute-done | bytes 368672 | tf_op jit(solution)/shard_map/ppermute | solution.py:612
  43.7 3.3 norm_one.1
  49.5 10.9 %collective-permute-done.4 = bf16[160,1152]{1,0:T(8,128)(2,1)S(1)} collective-permute-done((bf16[160,1152]{1,0:T(8,128)(2,1)S(1)}, bf16[160,1152]{1,0:T(8,128)(2,1)S(1)}, u32[]{:S(2)}, u32[]{:S(2)}) %collective-permute-start.4) | collective-permute-done | bytes 368672 | tf_op jit(solution)/shard_map/ppermute | solution.py:612
  64.9 18.6 %collective-permute-done.5 = bf16[2,144,1152]{2,1,0:T(8,128)(2,1)S(1)} collective-permute-done((bf16[2,144,1152]{2,1,0:T(8,128)(2,1)S(1)}, bf16[2,144,1152]{2,1,0:T(8,128)(2,1)S(1)}, u32[]{:S(2)}, u32[]{:S(2)}) %collective-permute-start.5) | collective-permute-done | bytes 663584 | tf_op jit(solution)/shard_map/ppermute | solution.py:616
  86.3 32.5 %collective-permute-done.2.refs_2_.refs_4_.refs_10_.refs_16_.refs_22_ = bf16[2,2,144,1152]{3,2,1,0:T(8,128)(2,1)S(1)} collective-permute-done((bf16[2,2,144,1152]{3,2,1,0:T(8,128)(2,1)}, bf16[2,2,144,1152]{3,2,1,0:T(8,128)(2,1)S(1)}, u32[]{:S(2)}, u32[]{:S(2)}) %collective-permute-start.2) | collective-permute-done | bytes 1327136 | tf_op jit(solution)/shard_map/ppermute | solution.py:616
  118.7 8.5 %all-gather.4.cloned.1.call-done.refs_1_.refs_2_.refs_3_.refs_4_ = bf16[32,144,1152]{2,1,0:T(8,128)(2,1)} async-done(((bf16[1,144,1152]{2,1,0:T(8,128)(2,1)}), bf16[32,144,1152]{2,1,0:T(8,128)(2,1)}) %all-gather.4.cloned.1.call-update) | async-done | bytes 10616848 | tf_op jit(solution)/shard_map/all_gather | solution.py:630
  135.1 4.1 pad_maximum_fusion.1
  140.9 8.0 %attn_fwd.4 = (bf16[768,896]{1,0:T(8,128)(2,1)S(1)}, bf16[768,384]{1,0:T(8,128)(2,1)S(1)}, f32[8,768]{1,0:T(8,128)S(1)}) custom-call(s32[3]{0:T(128)S(1)} %copy-done.21, bf16[32,144,1152]{2,1,0:T(8,128)(2,1)S(1)} %copy-done.23, bf16[2,2,144,1152]{3,2,1,0:T(8,128)(2,1)S(1)} %collective-permute-done.2.refs_2_.refs_4_.refs_10_.refs_16_.refs_22_, ...), custom_call_target="tpu_custom_call" | custom-call | flops 9200000000 | bytes 800000 | tf_op jit(solution)/shard_map/attn_fwd/pallas_call | solution.py:63
  150.0 7.5 %attn_fwd.7 = (bf16[768,896]{1,0:T(8,128)(2,1)S(1)}, bf16[768,384]{1,0:T(8,128)(2,1)S(1)}, f32[8,768]{1,0:T(8,128)S(1)}) custom-call(s32[3]{0:T(128)S(1)} %copy-done.21, bf16[32,144,1152]{2,1,0:T(8,128)(2,1)S(1)} %copy-done.23, bf16[768,1152]{1,0:T(8,128)(2,1)S(1)} %copy-done.36, f32[1,896]{1,0:T(1,128)S(1)} %slice.620.refs_3_), custom_call_target="tpu_custom_call" | custom-call | flops 9200000000 | bytes 800000 | tf_op jit(solution)/shard_map/attn_fwd/pallas_call | solution.py:63
  157.5 7.6 %attn_fwd.6 = (bf16[768,896]{1,0:T(8,128)(2,1)S(1)}, bf16[768,384]{1,0:T(8,128)(2,1)S(1)}, f32[8,768]{1,0:T(8,128)S(1)}) custom-call(s32[3]{0:T(128)S(1)} %copy-done.21, bf16[32,144,1152]{2,1,0:T(8,128)(2,1)S(1)} %copy-done.23, bf16[768,1152]{1,0:T(8,128)(2,1)S(1)} %copy-done.36, f32[1,896]{1,0:T(1,128)S(1)} %slice.614.refs_3_), custom_call_target="tpu_custom_call" | custom-call | flops 9200000000 | bytes 800000 | tf_op jit(solution)/shard_map/attn_fwd/pallas_call | solution.py:63
  166.2 7.4 %attn_fwd.5 = (bf16[768,896]{1,0:T(8,128)(2,1)S(1)}, bf16[768,384]{1,0:T(8,128)(2,1)S(1)}, f32[8,768]{1,0:T(8,128)S(1)}) custom-call(s32[3]{0:T(128)S(1)} %copy-done.21, bf16[32,144,1152]{2,1,0:T(8,128)(2,1)S(1)} %copy-done.23, bf16[768,1152]{1,0:T(8,128)(2,1)S(1)} %copy-done.36, f32[1,896]{1,0:T(1,128)S(1)} %slice.608.refs_3_), custom_call_target="tpu_custom_call" | custom-call | flops 9200000000 | bytes 800000 | tf_op jit(solution)/shard_map/attn_fwd/pallas_call | solution.py:63
  174.7 10.3 %norm_two.1 = (f32[768,1152]{1,0:T(8,128)S(1)}, bf16[768,1152]{1,0:T(8,128)(2,1)S(1)}, bf16[1152,768]{1,0:T(8,128)(2,1)S(1)}) custom-call(s32[3]{0:T(128)S(1)} %copy-done.21, bf16[32,144,1152]{2,1,0:T(8,128)(2,1)} %all-gather.4.cloned.1.call-done.refs_1_.refs_2_.refs_3_.refs_4_, ...), custom_call_target="tpu_custom_call" | custom-call | flops 13799999488 | bytes 1200000 | tf_op jit(solution)/shard_map/norm_two/pallas_call | solution.py:63
  189.2 33.9 %ffn_one.1 = (bf16[4,768,1152]{2,1,0:T(8,128)(2,1)}, bf16[4,768,1152]{2,1,0:T(8,128)(2,1)}, bf16[8,4,144,1152]{3,2,1,0:T(8,128)(2,1)}) custom-call(s32[3]{0:T(128)} %copy-done.20, bf16[2,2,144,1152]{3,2,1,0:T(8,128)(2,1)} %get-tuple-element.215.refs_1_.refs_7_.refs_13_.refs_19_, ...), custom_call_target="tpu_custom_call" | custom-call | flops 34500001792 | bytes 3000000 | tf_op jit(solution)/shard_map/ffn_one/pallas_call | solution.py:63
  223.2 24.1 %ffn_two.2 = (bf16[2,576,1152]{2,1,0:T(8,128)(2,1)}, bf16[2,576,1152]{2,1,0:T(8,128)(2,1)}, f32[2,1,1152]{2,1,0:T(1,128)}, f32[768,1152]{1,0:T(8,128)}) custom-call(s32[3]{0:T(128)} %copy-done.20, bf16[2,2,144,1152]{3,2,1,0:T(8,128)(2,1)} %get-tuple-element.215.refs_1_.refs_7_.refs_13_.refs_19_, ...), custom_call_target="tpu_custom_call" | custom-call | flops 27599998976 | bytes 2400000 | tf_op jit(solution)/shard_map/ffn_two/pallas_call | solution.py:63
  247.7 30.4 %ffn_two.3 = (bf16[2,576,1152]{2,1,0:T(8,128)(2,1)}, bf16[2,576,1152]{2,1,0:T(8,128)(2,1)}, f32[2,1,1152]{2,1,0:T(1,128)}, f32[768,1152]{1,0:T(8,128)}, bf16[768...) custom-call(s32[3]{0:T(128)} %copy-done.20, ...), custom_call_target="tpu_custom_call" | custom-call | flops 34500001792 | bytes 3000000 | tf_op jit(solution)/shard_map/ffn_two/pallas_call | solution.py:63
  289.2 15.6 %attn_bwd.4 = (bf16[1,576,1152]{2,1,0:T(8,128)(2,1)S(1)}, bf16[1,576,1152]{2,1,0:T(8,128)(2,1)S(1)}, f32[1,896]{1,0:T(1,128)S(1)}, bf16[768,896]{1,0:T(8,128)(2,1)S(1)}) custom-call(s32[3]{0:T(128)S(1)} %copy-done.22, bf16[32,144,1152]{2,1,0:T(8,128)(2,1)} %all-gather.4.cloned.1.call-done.refs_1_.refs_2_.refs_3_.refs_4_, ...), custom_call_target="tpu_custom_call" | custom-call | flops 19549999104 | bytes 1700000 | tf_op jit(solution)/shard_map/attn_bwd/pallas_call | solution.py:63
  316.6 15.4 %attn_bwd.6 = (bf16[1,576,1152]{2,1,0:T(8,128)(2,1)S(1)}, bf16[1,576,1152]{2,1,0:T(8,128)(2,1)S(1)}, f32[1,896]{1,0:T(1,128)S(1)}, bf16[768,896]{1,0:T(8,128)(2,1)S(1)}) custom-call(s32[3]{0:T(128)S(1)} %copy-done.22, bf16[32,144,1152]{2,1,0:T(8,128)(2,1)} %all-gather.4.cloned.1.call-done.refs_1_.refs_2_.refs_3_.refs_4_, ...), custom_call_target="tpu_custom_call" | custom-call | flops 19549999104 | bytes 1700000 | tf_op jit(solution)/shard_map/attn_bwd/pallas_call | solution.py:63
  339.6 15.4 %attn_bwd.5 = (bf16[1,576,1152]{2,1,0:T(8,128)(2,1)S(1)}, bf16[1,576,1152]{2,1,0:T(8,128)(2,1)}, f32[1,896]{1,0:T(1,128)S(1)}, bf16[768,896]{1,0:T(8,128)(2,1)S(1)}) custom-call(s32[3]{0:T(128)S(1)} %copy-done.22, bf16[32,144,1152]{2,1,0:T(8,128)(2,1)} %all-gather.4.cloned.1.call-done.refs_1_.refs_2_.refs_3_.refs_4_, ...), custom_call_target="tpu_custom_call" | custom-call | flops 19549999104 | bytes 1700000 | tf_op jit(solution)/shard_map/attn_bwd/pallas_call | solution.py:63
  355.1 2.2 fusion.14
  358.3 2.4 collective-permute-done.21.refs_4_
  363.8 15.4 %attn_bwd.7 = (bf16[1,576,1152]{2,1,0:T(8,128)(2,1)S(1)}, bf16[1,576,1152]{2,1,0:T(8,128)(2,1)S(1)}, f32[1,896]{1,0:T(1,128)S(1)}, bf16[768,896]{1,0:T(8,128)(2,1)S(1)}) custom-call(s32[3]{0:T(128)S(1)} %copy-done.22, bf16[32,144,1152]{2,1,0:T(8,128)(2,1)} %all-gather.4.cloned.1.call-done.refs_1_.refs_2_.refs_3_.refs_4_, ...), custom_call_target="tpu_custom_call" | custom-call | flops 19549999104 | bytes 1700000 | tf_op jit(solution)/shard_map/attn_bwd/pallas_call | solution.py:63
  388.5 9.7 %collective-permute-done.24.refs_6_ = bf16[2,144,1152]{2,1,0:T(8,128)(2,1)} collective-permute-done((bf16[2,144,1152]{2,1,0:T(8,128)(2,1)}, bf16[2,144,1152]{2,1,0:T(8,128)(2,1)}, u32[]{:S(2)}, u32[]{:S(2)}) %collective-permute-start.24) | collective-permute-done | bytes 663584 | tf_op jit(solution)/shard_map/ppermute | solution.py:616
  409.7 15.9 %norm_back.1 = (bf16[768,1152]{1,0:T(8,128)(2,1)S(1)}, f32[2,1152]{1,0:T(2,128)S(1)}) custom-call(s32[3]{0:T(128)S(1)} %copy-done.22, bf16[32,144,1152]{2,1,0:T(8,128)(2,1)} %all-gather.4.cloned.1.call-done.refs_1_.refs_2_.refs_3_.refs_4_, bf16[32,144,1152]{2,1,0:T(8,128)(2,1)} %all-gather.4.cloned.1.call-done.refs_1_.refs_2_.refs_3_.refs_4_, ...), custom_call_target="tpu_custom_call" | custom-call | flops 20700000256 | bytes 1800000 | tf_op jit(solution)/shard_map/norm_back/pallas_call | solution.py:63
  433.2 2.2 fusion.5
  439.1 4.6 collective-permute-done.34
  445.7 2.3 collective-permute-done.35
  455.9 5.9 %collective-permute-done.29.refs_8_ = bf16[2,144,1152]{2,1,0:T(8,128)(2,1)} collective-permute-done((bf16[2,144,1152]{2,1,0:T(8,128)(2,1)}, bf16[2,144,1152]{2,1,0:T(8,128)(2,1)}, u32[]{:S(2)}, u32[]{:S(2)}) %collective-permute-start.29) | collective-permute-done | bytes 663584 | tf_op jit(solution)/shard_map/ppermute | solution.py:616
  463.8 14.7 %mixed.1 = bf16[768,1152]{1,0:T(8,128)(2,1)S(1)} custom-call(s32[3]{0:T(128)S(1)} %copy-done.22, bf16[32,144,1152]{2,1,0:T(8,128)(2,1)} %bitcast.327, bf16[32,144,1152]{2,1,0:T(8,128)(2,1)} %bitcast.328, bf16[32,144,1152]{2,1,0:T(8,128)(2,1)} %bitcast.329, bf16[32,144,1152]{2,1,0:T(8,128)(2,1)} %bitcast.330, ...), custom_call_target="tpu_custom_call" | custom-call | flops 16099999744 | bytes 1400000 | tf_op jit(solution)/shard_map/mixed/pallas_call | solution.py:63
  482.0 2.7 collective-permute-start.40
  (389 shorter events, 129.9 us)
Async XLA Ops:
  7.2 120.0 %all-gather.4.cloned.1.call-start = ((), (), s32[]{:S(2)}) async-start(), calls=%async_computation.1 | async-start | bytes 10948608 | tf_op jit(solution)/shard_map/all_gather | solution.py:630
  11.3 211.8 %all-gather.6.cloned.1.call-start = ((), (), s32[]{:S(2)}) async-start(), calls=%async_computation.3 | async-start | bytes 10948608 | tf_op jit(solution)/shard_map/all_gather | solution.py:630
  31.0 31.4 %collective-permute-start.1 = (bf16[2,144,1152]{2,1,0:T(8,128)(2,1)S(1)}, bf16[2,144,1152]{2,1,0:T(8,128)(2,1)S(1)}, u32[]{:S(2)}, u32[]{:S(2)}) collective-permute-start(bf16[2,144,1152]{2,1,0:T(8,128)(2,1)S(1)} %get-tuple-element.241), channel_id=1, source_target_pairs={{0,8},{4,12},{8,0},{12,4},{16,24},{20,28},{24,16},{28,20},{1,9},{5... | collective-permute-start | bytes 1990664 | tf_op jit(solution)/shard_map/ppermute | solution.py:616
  61.2 22.3 %collective-permute-start.5 = (bf16[2,144,1152]{2,1,0:T(8,128)(2,1)S(1)}, bf16[2,144,1152]{2,1,0:T(8,128)(2,1)S(1)}, u32[]{:S(2)}, u32[]{:S(2)}) collective-permute-start(bf16[2,144,1152]{2,1,0:T(8,128)(2,1)S(1)} %get-tuple-element.239), channel_id=1, source_target_pairs={{0,16},{4,20},{8,24},{12,28},{16,0},{20,4},{24,8},{28,12},{1,17},{... | collective-permute-start | bytes 1990664 | tf_op jit(solution)/shard_map/ppermute | solution.py:616
  64.1 54.6 %collective-permute-start.2 = (bf16[2,2,144,1152]{3,2,1,0:T(8,128)(2,1)}, bf16[2,2,144,1152]{3,2,1,0:T(8,128)(2,1)S(1)}, u32[]{:S(2)}, u32[]{:S(2)}) collective-permute-start(bf16[2,2,144,1152]{3,2,1,0:T(8,128)(2,1)} %get-tuple-element.215.refs_1_.refs_7_.refs_13_.refs_19_), channel_id=1, source_target_pairs={{0,16},{4,20},{8,24},{12,28},{16,0},{20,4},{24,8},{28,12},{1,17},{... | collective-permute-start | bytes 3981320 | tf_op jit(solution)/shard_map/ppermute | solution.py:616
  85.2 33.5 %collective-permute-start.6 = (bf16[2,2,144,1152]{3,2,1,0:T(8,128)(2,1)}, bf16[2,2,144,1152]{3,2,1,0:T(8,128)(2,1)}, u32[]{:S(2)}, u32[]{:S(2)}) collective-permute-start(bf16[2,2,144,1152]{3,2,1,0:T(8,128)(2,1)} %get-tuple-element.217.refs_2_.refs_8_.refs_14_.refs_20_), channel_id=1, source_target_pairs={{0,8},{4,12},{8,0},{12,4},{16,24},{20,28},{24,16},{28,20},{1,9},{5... | collective-permute-start | bytes 3981320 | tf_op jit(solution)/shard_map/ppermute | solution.py:616
  127.2 298.4 %reduce-scatter.2.cloned.1.call-start = ((), (), s32[]{:S(2)}) async-start(), calls=%async_computation.2 | async-start | bytes 10948608 | tf_op jit(solution)/shard_map/reduce_scatter | solution.py:700
  134.8 54.4 %collective-permute-start.7 = (bf16[2,2,2,144,1152]{4,3,2,1,0:T(8,128)(2,1)S(1)}, bf16[2,2,2,144,1152]{4,3,2,1,0:T(8,128)(2,1)}, u32[]{:S(2)}, u32[]{:S(2)}) collective-permute-start(bf16[2,2,2,144,1152]{4,3,2,1,0:T(8,128)(2,1)S(1)} %pad_maximum_fusion), channel_id=1, source_target_pairs={{0,4},{4,0},{8,12},{12,8},{16,20},{20,16},{24,28},{28,24},{1,5},{5... | collective-permute-start | bytes 7962632 | tf_op jit(solution)/shard_map/ppermute | solution.py:616
  139.2 50.0 %collective-permute-start.8 = (bf16[2,2,2,144,1152]{4,3,2,1,0:T(8,128)(2,1)}, bf16[2,2,2,144,1152]{4,3,2,1,0:T(8,128)(2,1)}, u32[]{:S(2)}, u32[]{:S(2)}) collective-permute-start(bf16[2,2,2,144,1152]{4,3,2,1,0:T(8,128)(2,1)} %pad_maximum_fusion.1), channel_id=1, source_target_pairs={{0,4},{4,0},{8,12},{12,8},{16,20},{20,16},{24,28},{28,24},{1,5},{5... | collective-permute-start | bytes 7962632 | tf_op jit(solution)/shard_map/ppermute | solution.py:616
  247.3 36.9 %collective-permute-start.9 = (bf16[2,576,1152]{2,1,0:T(8,128)(2,1)}, bf16[2,576,1152]{2,1,0:T(8,128)(2,1)S(1)}, u32[]{:S(2)}, u32[]{:S(2)}) collective-permute-start(bf16[2,576,1152]{2,1,0:T(8,128)(2,1)} %get-tuple-element.117), channel_id=1, source_target_pairs={{0,4},{4,0},{8,12},{12,8},{16,20},{20,16},{24,28},{28,24},{1,5},{5... | collective-permute-start | bytes 7962632 | tf_op jit(solution)/shard_map/ppermute | solution.py:616
  279.4 25.8 %collective-permute-start.14 = (bf16[2,576,1152]{2,1,0:T(8,128)(2,1)}, bf16[2,576,1152]{2,1,0:T(8,128)(2,1)S(1)}, u32[]{:S(2)}, u32[]{:S(2)}) collective-permute-start(bf16[2,576,1152]{2,1,0:T(8,128)(2,1)} %get-tuple-element.132), channel_id=1, source_target_pairs={{0,4},{4,0},{8,12},{12,8},{16,20},{20,16},{24,28},{28,24},{1,5},{5... | collective-permute-start | bytes 7962632 | tf_op jit(solution)/shard_map/ppermute | solution.py:616
  285.5 25.1 %collective-permute-start.10 = (bf16[2,144,1152]{2,1,0:T(8,128)(2,1)S(1)}, bf16[2,144,1152]{2,1,0:T(8,128)(2,1)S(1)}, u32[]{:S(2)}, u32[]{:S(2)}) collective-permute-start(bf16[2,144,1152]{2,1,0:T(8,128)(2,1)S(1)} %pad_maximum_fusion.6), channel_id=1, source_target_pairs={{0,8},{4,12},{8,0},{12,4},{16,24},{20,28},{24,16},{28,20},{1,9},{5... | collective-permute-start | bytes 1990664 | tf_op jit(solution)/shard_map/ppermute | solution.py:616
  287.5 23.1 %collective-permute-start.11 = (bf16[2,144,1152]{2,1,0:T(8,128)(2,1)S(1)}, bf16[2,144,1152]{2,1,0:T(8,128)(2,1)S(1)}, u32[]{:S(2)}, u32[]{:S(2)}) collective-permute-start(bf16[2,144,1152]{2,1,0:T(8,128)(2,1)S(1)} %pad_maximum_fusion.7), channel_id=1, source_target_pairs={{0,16},{4,20},{8,24},{12,28},{16,0},{20,4},{24,8},{28,12},{1,17},{... | collective-permute-start | bytes 1990664 | tf_op jit(solution)/shard_map/ppermute | solution.py:616
  304.8 33.3 %collective-permute-start.17 = (bf16[1,576,1152]{2,1,0:T(8,128)(2,1)S(1)}, bf16[1,576,1152]{2,1,0:T(8,128)(2,1)S(1)}, u32[]{:S(2)}, u32[]{:S(2)}) collective-permute-start(bf16[1,576,1152]{2,1,0:T(8,128)(2,1)S(1)} %get-tuple-element.135), channel_id=1, source_target_pairs={{0,4},{4,0},{8,12},{12,8},{16,20},{20,16},{24,28},{28,24},{1,5},{5... | collective-permute-start | bytes 3981320 | tf_op jit(solution)/shard_map/ppermute | solution.py:616
  307.0 26.2 %collective-permute-start.15 = (bf16[2,144,1152]{2,1,0:T(8,128)(2,1)}, bf16[2,144,1152]{2,1,0:T(8,128)(2,1)S(1)}, u32[]{:S(2)}, u32[]{:S(2)}) collective-permute-start(bf16[2,144,1152]{2,1,0:T(8,128)(2,1)} %pad_maximum_fusion.8), channel_id=1, source_target_pairs={{0,8},{4,12},{8,0},{12,4},{16,24},{20,28},{24,16},{28,20},{1,9},{5... | collective-permute-start | bytes 1990664 | tf_op jit(solution)/shard_map/ppermute | solution.py:616
  310.2 23.8 %collective-permute-start.16 = (bf16[2,144,1152]{2,1,0:T(8,128)(2,1)}, bf16[2,144,1152]{2,1,0:T(8,128)(2,1)S(1)}, u32[]{:S(2)}, u32[]{:S(2)}) collective-permute-start(bf16[2,144,1152]{2,1,0:T(8,128)(2,1)} %pad_maximum_fusion.9), channel_id=1, source_target_pairs={{0,16},{4,20},{8,24},{12,28},{16,0},{20,4},{24,8},{28,12},{1,17},{... | collective-permute-start | bytes 1990664 | tf_op jit(solution)/shard_map/ppermute | solution.py:616
  314.2 24.2 %collective-permute-start.13 = (bf16[1,144,1152]{2,1,0:T(8,128)(2,1)}, bf16[1,144,1152]{2,1,0:T(8,128)(2,1)S(1)}, u32[]{:S(2)}, u32[]{:S(2)}) collective-permute-start(bf16[1,144,1152]{2,1,0:T(8,128)(2,1)} %fusion.40), channel_id=1, source_target_pairs={{0,16},{4,20},{8,24},{12,28},{16,0},{20,4},{24,8},{28,12},{1,17},{... | collective-permute-start | bytes 995336 | tf_op jit(solution)/shard_map/ppermute | solution.py:616
  315.8 23.5 %collective-permute-start.12 = (bf16[1,144,1152]{2,1,0:T(8,128)(2,1)}, bf16[1,144,1152]{2,1,0:T(8,128)(2,1)S(1)}, u32[]{:S(2)}, u32[]{:S(2)}) collective-permute-start(bf16[1,144,1152]{2,1,0:T(8,128)(2,1)} %fusion.39), channel_id=1, source_target_pairs={{0,8},{4,12},{8,0},{12,4},{16,24},{20,28},{24,16},{28,20},{1,9},{5... | collective-permute-start | bytes 995336 | tf_op jit(solution)/shard_map/ppermute | solution.py:616
  335.1 27.2 %collective-permute-start.20 = (bf16[1,144,1152]{2,1,0:T(8,128)(2,1)S(1)}, bf16[1,144,1152]{2,1,0:T(8,128)(2,1)S(1)}, u32[]{:S(2)}, u32[]{:S(2)}) collective-permute-start(bf16[1,144,1152]{2,1,0:T(8,128)(2,1)S(1)} %fusion.42), channel_id=1, source_target_pairs={{0,16},{4,20},{8,24},{12,28},{16,0},{20,4},{24,8},{28,12},{1,17},{... | collective-permute-start | bytes 995336 | tf_op jit(solution)/shard_map/ppermute | solution.py:616
  336.8 27.0 %collective-permute-start.19 = (bf16[1,144,1152]{2,1,0:T(8,128)(2,1)S(1)}, bf16[1,144,1152]{2,1,0:T(8,128)(2,1)S(1)}, u32[]{:S(2)}, u32[]{:S(2)}) collective-permute-start(bf16[1,144,1152]{2,1,0:T(8,128)(2,1)S(1)} %fusion.41), channel_id=1, source_target_pairs={{0,8},{4,12},{8,0},{12,4},{16,24},{20,28},{24,16},{28,20},{1,9},{5... | collective-permute-start | bytes 995336 | tf_op jit(solution)/shard_map/ppermute | solution.py:616
  338.1 25.7 %collective-permute-start.22 = (bf16[1,576,1152]{2,1,0:T(8,128)(2,1)S(1)}, bf16[1,576,1152]{2,1,0:T(8,128)(2,1)S(1)}, u32[]{:S(2)}, u32[]{:S(2)}) collective-permute-start(bf16[1,576,1152]{2,1,0:T(8,128)(2,1)S(1)} %get-tuple-element.147), channel_id=1, source_target_pairs={{0,4},{4,0},{8,12},{12,8},{16,20},{20,16},{24,28},{28,24},{1,5},{5... | collective-permute-start | bytes 3981320 | tf_op jit(solution)/shard_map/ppermute | solution.py:616
  338.4 22.3 %collective-permute-start.21 = (bf16[2,144,1152]{2,1,0:T(8,128)(2,1)S(1)}, bf16[2,144,1152]{2,1,0:T(8,128)(2,1)S(1)}, u32[]{:S(2)}, u32[]{:S(2)}) collective-permute-start(bf16[2,144,1152]{2,1,0:T(8,128)(2,1)S(1)} %pad_maximum_fusion.10), channel_id=1, source_target_pairs={{0,8},{4,12},{8,0},{12,4},{16,24},{20,28},{24,16},{28,20},{1,9},{5... | collective-permute-start | bytes 1990664 | tf_op jit(solution)/shard_map/ppermute | solution.py:616
  357.3 22.0 %collective-permute-start.30 = (bf16[144,1152]{1,0:T(8,128)(2,1)S(1)}, bf16[144,1152]{1,0:T(8,128)(2,1)S(1)}, u32[]{:S(2)}, u32[]{:S(2)}) collective-permute-start(bf16[144,1152]{1,0:T(8,128)(2,1)S(1)} %fusion.14), channel_id=1, source_target_pairs={{0,3},{1,0},{2,1},{3,2},{4,7},{5,4},{6,5},{7,6},{8,11},{9,8},{10,9... | collective-permute-start | bytes 995336 | tf_op jit(solution)/shard_map/ppermute | solution.py:612
  360.6 39.4 %collective-permute-start.18 = (bf16[1,576,1152]{2,1,0:T(8,128)(2,1)}, bf16[1,576,1152]{2,1,0:T(8,128)(2,1)}, u32[]{:S(2)}, u32[]{:S(2)}) collective-permute-start(bf16[1,576,1152]{2,1,0:T(8,128)(2,1)} %get-tuple-element.139), channel_id=1, source_target_pairs={{0,4},{4,0},{8,12},{12,8},{16,20},{20,16},{24,28},{28,24},{1,5},{5... | collective-permute-start | bytes 3981320 | tf_op jit(solution)/shard_map/ppermute | solution.py:616
  362.3 23.0 %collective-permute-start.26 = (bf16[1,144,1152]{2,1,0:T(8,128)(2,1)}, bf16[1,144,1152]{2,1,0:T(8,128)(2,1)S(1)}, u32[]{:S(2)}, u32[]{:S(2)}) collective-permute-start(bf16[1,144,1152]{2,1,0:T(8,128)(2,1)} %fusion.44), channel_id=1, source_target_pairs={{0,16},{4,20},{8,24},{12,28},{16,0},{20,4},{24,8},{28,12},{1,17},{... | collective-permute-start | bytes 995336 | tf_op jit(solution)/shard_map/ppermute | solution.py:616
  383.2 48.7 %collective-permute-start.31 = (bf16[144,1152]{1,0:T(8,128)(2,1)}, bf16[144,1152]{1,0:T(8,128)(2,1)}, u32[]{:S(2)}, u32[]{:S(2)}) collective-permute-start(bf16[144,1152]{1,0:T(8,128)(2,1)} %fusion.10), channel_id=1, source_target_pairs={{0,3},{1,0},{2,1},{3,2},{4,7},{5,4},{6,5},{7,6},{8,11},{9,8},{10,9... | collective-permute-start | bytes 995336 | tf_op jit(solution)/shard_map/ppermute | solution.py:612
  385.3 21.2 %collective-permute-start.28 = (bf16[1,576,1152]{2,1,0:T(8,128)(2,1)}, bf16[1,576,1152]{2,1,0:T(8,128)(2,1)S(1)}, u32[]{:S(2)}, u32[]{:S(2)}) collective-permute-start(bf16[1,576,1152]{2,1,0:T(8,128)(2,1)} %copy-done.24), channel_id=1, source_target_pairs={{0,4},{4,0},{8,12},{12,8},{16,20},{20,16},{24,28},{28,24},{1,5},{5... | collective-permute-start | bytes 3981320 | tf_op jit(solution)/shard_map/ppermute | solution.py:616
  387.4 44.5 %collective-permute-start.27 = (bf16[144,1152]{1,0:T(8,128)(2,1)}, bf16[144,1152]{1,0:T(8,128)(2,1)}, u32[]{:S(2)}, u32[]{:S(2)}) collective-permute-start(bf16[144,1152]{1,0:T(8,128)(2,1)} %fusion.17), channel_id=1, source_target_pairs={{0,3},{1,0},{2,1},{3,2},{4,7},{5,4},{6,5},{7,6},{8,11},{9,8},{10,9... | collective-permute-start | bytes 995336 | tf_op jit(solution)/shard_map/ppermute | solution.py:612
  402.1 31.0 %collective-permute-start.25 = (bf16[1,144,1152]{2,1,0:T(8,128)(2,1)}, bf16[1,144,1152]{2,1,0:T(8,128)(2,1)}, u32[]{:S(2)}, u32[]{:S(2)}) collective-permute-start(bf16[1,144,1152]{2,1,0:T(8,128)(2,1)} %fusion.43), channel_id=1, source_target_pairs={{0,8},{4,12},{8,0},{12,4},{16,24},{20,28},{24,16},{28,20},{1,9},{5... | collective-permute-start | bytes 995336 | tf_op jit(solution)/shard_map/ppermute | solution.py:616
  431.9 48.6 %collective-permute-start.38 = (bf16[1,144,1152]{2,1,0:T(8,128)(2,1)}, bf16[1,144,1152]{2,1,0:T(8,128)(2,1)}, u32[]{:S(2)}, u32[]{:S(2)}) collective-permute-start(bf16[1,144,1152]{2,1,0:T(8,128)(2,1)} %fusion.46), channel_id=1, source_target_pairs={{0,16},{4,20},{8,24},{12,28},{16,0},{20,4},{24,8},{28,12},{1,17},{... | collective-permute-start | bytes 995336 | tf_op jit(solution)/shard_map/ppermute | solution.py:616
  435.4 44.3 %collective-permute-start.39 = (bf16[144,1152]{1,0:T(8,128)(2,1)}, bf16[144,1152]{1,0:T(8,128)(2,1)}, u32[]{:S(2)}, u32[]{:S(2)}) collective-permute-start(bf16[144,1152]{1,0:T(8,128)(2,1)} %fusion.5), channel_id=1, source_target_pairs={{0,3},{1,0},{2,1},{3,2},{4,7},{5,4},{6,5},{7,6},{8,11},{9,8},{10,9... | collective-permute-start | bytes 995336 | tf_op jit(solution)/shard_map/ppermute | solution.py:612
  451.8 32.9 %collective-permute-start.41 = (bf16[144,1152]{1,0:T(8,128)(2,1)}, bf16[144,1152]{1,0:T(8,128)(2,1)}, u32[]{:S(2)}, u32[]{:S(2)}) collective-permute-start(bf16[144,1152]{1,0:T(8,128)(2,1)} %fusion.3), channel_id=1, source_target_pairs={{0,3},{1,0},{2,1},{3,2},{4,7},{5,4},{6,5},{7,6},{8,11},{9,8},{10,9... | collective-permute-start | bytes 995336 | tf_op jit(solution)/shard_map/ppermute | solution.py:612
  (105 other events, 1295.2 us)
Sparse Core Ops, SparseCore 0:
  11.4 115.7 all-gather.3
  130.0 85.7 all-gather.5
  223.2 159.3 reduce-scatter.1

commit v4 on v3

--- a/solution.py
+++ b/solution.py
@@ -450,26 +450,33 @@
     fetch_step(pieces, step + 1, w_refs, place_ref, w.at[1 - slot], sems.at[1 - slot])
     landed(w.at[slot], sems.at[slot])
     width = g_ref.shape[2]
-    for n in range(0, width, 256):
-        cols = slice(n, min(n + 256, width))
-        pre = nn(a_ref[...], w[slot, :, cols]) + bias_ref[0, :, cols]
+
+    @pl.when(step == 0)
+    def _():
+        late.take(0)
+
+    et_ref = late.buffers[0]
+    count, _, rows, _ = grad_ref.shape
+    half_rows = et_ref.shape[0] // 2
+    blocks = [slice(n, min(n + 256, width)) for n in range(0, width, 256)]
+
+    def before(cols):
+        return nn(a_ref[...], w[slot, :, cols]) + bias_ref[0, :, cols]
+
+    pre = before(blocks[0])
+    for n, cols in enumerate(blocks):
+        following = before(blocks[n + 1]) if n + 1 < len(blocks) else None
         square = pre * pre
         half = 0.5 + 0.5 * jnp.tanh(pre * (GELU_A + GELU_A * GELU_B * square))
         g_ref[0, :, cols] = (pre * half).astype(BF)
         slope = half + (half - half * half) * (pre * (2 * GELU_A + 6 * GELU_A * GELU_B * square))
         gp_ref[0, :, cols] = slope.astype(BF)
-
-    @pl.when(step == 0)
-    def _():
-        late.take(0)
-
-    et_ref = late.buffers[0]
-    count, _, rows, _ = grad_ref.shape
-    for part in range(2):
-        half = et_ref.shape[0] // 2
-        value = nn(et_ref[part * half : (part + 1) * half, :], g_ref[0]).astype(BF)
-        for i in range(count // 2):
-            grad_ref[part * count // 2 + i, 0] = value[i * rows : (i + 1) * rows]
+        for part in range(2):
+            left = et_ref[part * half_rows : (part + 1) * half_rows, :]
+            value = nn(left, g_ref[0, :, cols]).astype(BF)
+            for i in range(count // 2):
+                grad_ref[part * count // 2 + i, 0, :, cols] = value[i * rows : (i + 1) * rows]
+        pre = following
 
 
 def ffn_one(cfg, place, after, pieces, a, bias, et):
@@ -786,14 +793,18 @@
         return [self.total]
 
 
-def sum_all(vector, cube):
-    if not cube:
+def sum_all(vector, marks):
+    if marks is None:
         return lax.psum(vector, ("dp", "tensor"))
     size = lax.axis_size("tensor")
     for offset in (CORE, ACROSS, ALONG):
+        if offset == ALONG:
+            vector = tie(vector, *marks[0])
         vector = vector + swap(vector, offset)
     offset = 1
     while offset < size:
+        if 2 * offset == size:
+            vector = tie(vector, *marks[1])
         vector = vector + lax.ppermute(vector, "tensor", [(i, i ^ offset) for i in range(size)])
         offset *= 2
     return vector
@@ -931,14 +942,15 @@
         mark = grads[0][2]
         pins["nb"] += out[0].step_core()
         pins["mix"] += out[1].step_first(mark) + out[2].step_second(mark) + attn_z.step(mark)
-        pins["mix"] += out[0].step_first() + up_z.step(mark)
+        zero_first = out[0].step_first()
+        pins["mix"] += up_z.step(mark)
         tokens_grad, vec_one = finish_norm(pins["nb"])
-        out[1].step_second(vec_one)
-        out[0].step_second(vec_one)
+        vec_one = tie(vec_one, *zero_first)
+        seconds = out[1].step_second(vec_one) + out[0].step_second(vec_one)
         attn_z.step(vec_one)
         up_z.step(vec_one)
         mixed = finish(pins["mix"])
-        attn_z.step(mixed)
+        marks = (seconds + [mixed], attn_z.step())
         grad_up, grad_attn = up_z.step(), attn_z.step()
     else:
         for k in high + low:
@@ -957,7 +969,7 @@
     pieces = jnp.take(pieces, order, axis=0)
     sums = sum_all(
         jnp.concatenate([pieces.reshape(-1), vec_one.reshape(-1), vec_two.reshape(-1), sum_e[0]]),
-        cube,
+        marks if cube else None,
     )
     per = qw + hidden
     mine = lax.dynamic_index_in_dim(sums[: size * per].reshape(size, per), z, 0, keepdims=False)

time: 505 us -> 494 us (0.978)
  waiting for transfers between devices: 114 us -> 124 us
  local copies, waits for them, and re-layouts: 51.8 us -> 42.7 us
  other arithmetic: 52.5 us -> 45.2 us
    ppermute x2, waiting for transfers between devices: 2.92 us -> 9.73 us  [sum_all(): lax.ppermute(vector, 'tensor', [(i, i ^ offset) for i in range(size)])]
    unnamed x183 -> x201, local copies, waits for them, and re-layouts: 22.4 us -> 16.9 us
  transfers between devices with their start and end apart: 45 -> 45, of which waited for: 16 -> 17; matrix products, arithmetic and copies ran while one was open for 15% -> 13% of each run, Pallas kernels for 45% -> 45%
where the time goes in v4:
time: 494 us; the launch traced here: 488 us
  Pallas kernels  221 us (45%)
  waiting for transfers between devices  124 us (25%)
  other arithmetic  45.2 us (9%)
  local copies, waits for them, and re-layouts  42.7 us (9%)
  starting transfers between devices  39.1 us (8%)
  between operations  16.2 us (3%)
    pallas_call x15, Pallas kernels, call(): pl.pallas_call(body, grid_spec=pltpu.PrefetchScalarGridSpec(num_scalar_pr...  221 us
    ppermute x31, waiting for transfers between devices, swap(): lax.ppermute(value, 'dp', [(i, i ^ offset) for i in range(lax.axis_size('...  79.3 us
    ppermute x9, waiting for transfers between devices, ring(): lax.ppermute(value, 'tensor', [(i, (i + by) % size) for i in range(size)])  26.4 us
    ppermute x31, starting transfers between devices, swap(): lax.ppermute(value, 'dp', [(i, i ^ offset) for i in range(lax.axis_size('...  22.6 us
    unnamed x201, local copies, waits for them, and re-layouts  16.9 us
    ppermute x9, starting transfers between devices, ring(): lax.ppermute(value, 'tensor', [(i, (i + by) % size) for i in range(size)])  14.7 us
    another operation x16, other arithmetic, send(): value = swap(jnp.stack([v for i in mine for v in outs[i]]), link)  10.8 us
  transfers between devices with their start and end apart: 45, of which 17 were waited for; matrix products, arithmetic and copies ran while one was open for 13% of the time, Pallas kernels for 45%

profile of v4, /device:TPU:0, one launch (start us, length us, event | category | flops | bytes accessed | tf_op | source)
XLA Modules:
  0.0 488.4 jit_solution(1069914888913637097)
XLA Ops:
  13.8 3.0 collective-permute-start
  20.3 2.5 constant_dynamic-slice_fusion
  23.8 4.3 collective-permute-done
  32.5 11.2 %collective-permute-done.3 = bf16[160,1152]{1,0:T(8,128)(2,1)S(1)} collective-permute-done((bf16[160,1152]{1,0:T(8,128)(2,1)}, bf16[160,1152]{1,0:T(8,128)(2,1)S(1)}, u32[]{:S(2)}, u32[]{:S(2)}) %collective-permute-start.3) | collective-permute-done | bytes 368672 | tf_op jit(solution)/shard_map/ppermute | solution.py:619
  43.7 3.3 norm_one.1
  49.5 10.9 %collective-permute-done.4 = bf16[160,1152]{1,0:T(8,128)(2,1)S(1)} collective-permute-done((bf16[160,1152]{1,0:T(8,128)(2,1)S(1)}, bf16[160,1152]{1,0:T(8,128)(2,1)S(1)}, u32[]{:S(2)}, u32[]{:S(2)}) %collective-permute-start.4) | collective-permute-done | bytes 368672 | tf_op jit(solution)/shard_map/ppermute | solution.py:619
  64.9 18.6 %collective-permute-done.5 = bf16[2,144,1152]{2,1,0:T(8,128)(2,1)S(1)} collective-permute-done((bf16[2,144,1152]{2,1,0:T(8,128)(2,1)S(1)}, bf16[2,144,1152]{2,1,0:T(8,128)(2,1)S(1)}, u32[]{:S(2)}, u32[]{:S(2)}) %collective-permute-start.5) | collective-permute-done | bytes 663584 | tf_op jit(solution)/shard_map/ppermute | solution.py:623
  86.3 32.4 %collective-permute-done.2.refs_2_.refs_4_.refs_10_.refs_16_.refs_22_ = bf16[2,2,144,1152]{3,2,1,0:T(8,128)(2,1)S(1)} collective-permute-done((bf16[2,2,144,1152]{3,2,1,0:T(8,128)(2,1)}, bf16[2,2,144,1152]{3,2,1,0:T(8,128)(2,1)S(1)}, u32[]{:S(2)}, u32[]{:S(2)}) %collective-permute-start.2) | collective-permute-done | bytes 1327136 | tf_op jit(solution)/shard_map/ppermute | solution.py:623
  118.7 8.5 %all-gather.4.cloned.1.call-done.refs_1_.refs_2_.refs_3_.refs_4_ = bf16[32,144,1152]{2,1,0:T(8,128)(2,1)} async-done(((bf16[1,144,1152]{2,1,0:T(8,128)(2,1)}), bf16[32,144,1152]{2,1,0:T(8,128)(2,1)}) %all-gather.4.cloned.1.call-update) | async-done | bytes 10616848 | tf_op jit(solution)/shard_map/all_gather | solution.py:637
  134.4 4.0 pad_maximum_fusion.1
  140.1 7.6 %attn_fwd.4 = (bf16[768,896]{1,0:T(8,128)(2,1)S(1)}, bf16[768,384]{1,0:T(8,128)(2,1)S(1)}, f32[8,768]{1,0:T(8,128)S(1)}) custom-call(s32[3]{0:T(128)S(1)} %copy-done.27, bf16[32,144,1152]{2,1,0:T(8,128)(2,1)S(1)} %copy-done.29, bf16[2,2,144,1152]{3,2,1,0:T(8,128)(2,1)S(1)} %collective-permute-done.2.refs_2_.refs_4_.refs_10_.refs_16_.refs_22_, ...), custom_call_target="tpu_custom_call" | custom-call | flops 9200000000 | bytes 800000 | tf_op jit(solution)/shard_map/attn_fwd/pallas_call | solution.py:63
  147.8 7.5 %attn_fwd.7 = (bf16[768,896]{1,0:T(8,128)(2,1)S(1)}, bf16[768,384]{1,0:T(8,128)(2,1)S(1)}, f32[8,768]{1,0:T(8,128)S(1)}) custom-call(s32[3]{0:T(128)S(1)} %copy-done.27, bf16[32,144,1152]{2,1,0:T(8,128)(2,1)S(1)} %copy-done.29, bf16[768,1152]{1,0:T(8,128)(2,1)S(1)} %copy-done.43, f32[1,896]{1,0:T(1,128)S(1)} %slice.620.refs_3_), custom_call_target="tpu_custom_call" | custom-call | flops 9200000000 | bytes 800000 | tf_op jit(solution)/shard_map/attn_fwd/pallas_call | solution.py:63
  155.3 7.6 %attn_fwd.6 = (bf16[768,896]{1,0:T(8,128)(2,1)S(1)}, bf16[768,384]{1,0:T(8,128)(2,1)S(1)}, f32[8,768]{1,0:T(8,128)S(1)}) custom-call(s32[3]{0:T(128)S(1)} %copy-done.27, bf16[32,144,1152]{2,1,0:T(8,128)(2,1)S(1)} %copy-done.29, bf16[768,1152]{1,0:T(8,128)(2,1)S(1)} %copy-done.43, f32[1,896]{1,0:T(1,128)S(1)} %slice.614.refs_3_), custom_call_target="tpu_custom_call" | custom-call | flops 9200000000 | bytes 800000 | tf_op jit(solution)/shard_map/attn_fwd/pallas_call | solution.py:63
  163.0 7.4 %attn_fwd.5 = (bf16[768,896]{1,0:T(8,128)(2,1)S(1)}, bf16[768,384]{1,0:T(8,128)(2,1)S(1)}, f32[8,768]{1,0:T(8,128)S(1)}) custom-call(s32[3]{0:T(128)S(1)} %copy-done.27, bf16[32,144,1152]{2,1,0:T(8,128)(2,1)S(1)} %copy-done.29, bf16[768,1152]{1,0:T(8,128)(2,1)S(1)} %copy-done.43, f32[1,896]{1,0:T(1,128)S(1)} %slice.608.refs_3_), custom_call_target="tpu_custom_call" | custom-call | flops 9200000000 | bytes 800000 | tf_op jit(solution)/shard_map/attn_fwd/pallas_call | solution.py:63
  170.5 10.5 %norm_two.1 = (f32[768,1152]{1,0:T(8,128)S(1)}, bf16[768,1152]{1,0:T(8,128)(2,1)S(1)}, bf16[1152,768]{1,0:T(8,128)(2,1)S(1)}) custom-call(s32[3]{0:T(128)S(1)} %copy-done.27, bf16[32,144,1152]{2,1,0:T(8,128)(2,1)} %all-gather.4.cloned.1.call-done.refs_1_.refs_2_.refs_3_.refs_4_, ...), custom_call_target="tpu_custom_call" | custom-call | flops 13799999488 | bytes 1200000 | tf_op jit(solution)/shard_map/norm_two/pallas_call | solution.py:63
  185.1 31.8 %ffn_one.1 = (bf16[4,768,1152]{2,1,0:T(8,128)(2,1)}, bf16[4,768,1152]{2,1,0:T(8,128)(2,1)}, bf16[8,4,144,1152]{3,2,1,0:T(8,128)(2,1)}) custom-call(s32[3]{0:T(128)} %copy-done.26, bf16[2,2,144,1152]{3,2,1,0:T(8,128)(2,1)} %get-tuple-element.219.refs_1_.refs_7_.refs_13_.refs_19_, ...), custom_call_target="tpu_custom_call" | custom-call | flops 34500001792 | bytes 3000000 | tf_op jit(solution)/shard_map/ffn_one/pallas_call | solution.py:63
  217.0 23.9 %ffn_two.2 = (bf16[2,576,1152]{2,1,0:T(8,128)(2,1)}, bf16[2,576,1152]{2,1,0:T(8,128)(2,1)}, f32[2,1,1152]{2,1,0:T(1,128)}, f32[768,1152]{1,0:T(8,128)}) custom-call(s32[3]{0:T(128)} %copy-done.26, bf16[2,2,144,1152]{3,2,1,0:T(8,128)(2,1)} %get-tuple-element.219.refs_1_.refs_7_.refs_13_.refs_19_, ...), custom_call_target="tpu_custom_call" | custom-call | flops 27599998976 | bytes 2400000 | tf_op jit(solution)/shard_map/ffn_two/pallas_call | solution.py:63
  241.1 30.0 %ffn_two.3 = (bf16[2,576,1152]{2,1,0:T(8,128)(2,1)}, bf16[2,576,1152]{2,1,0:T(8,128)(2,1)}, f32[2,1,1152]{2,1,0:T(1,128)}, f32[768,1152]{1,0:T(8,128)}, bf16[768...) custom-call(s32[3]{0:T(128)} %copy-done.26, ...), custom_call_target="tpu_custom_call" | custom-call | flops 34500001792 | bytes 3000000 | tf_op jit(solution)/shard_map/ffn_two/pallas_call | solution.py:63
  281.9 15.8 %attn_bwd.4 = (bf16[1,576,1152]{2,1,0:T(8,128)(2,1)S(1)}, bf16[1,576,1152]{2,1,0:T(8,128)(2,1)S(1)}, f32[1,896]{1,0:T(1,128)S(1)}, bf16[768,896]{1,0:T(8,128)(2,1)S(1)}) custom-call(s32[3]{0:T(128)S(1)} %copy-done.28, bf16[32,144,1152]{2,1,0:T(8,128)(2,1)} %all-gather.4.cloned.1.call-done.refs_1_.refs_2_.refs_3_.refs_4_, ...), custom_call_target="tpu_custom_call" | custom-call | flops 19549999104 | bytes 1700000 | tf_op jit(solution)/shard_map/attn_bwd/pallas_call | solution.py:63
  307.7 15.4 %attn_bwd.6 = (bf16[1,576,1152]{2,1,0:T(8,128)(2,1)S(1)}, bf16[1,576,1152]{2,1,0:T(8,128)(2,1)S(1)}, f32[1,896]{1,0:T(1,128)S(1)}, bf16[768,896]{1,0:T(8,128)(2,1)S(1)}) custom-call(s32[3]{0:T(128)S(1)} %copy-done.28, bf16[32,144,1152]{2,1,0:T(8,128)(2,1)} %all-gather.4.cloned.1.call-done.refs_1_.refs_2_.refs_3_.refs_4_, ...), custom_call_target="tpu_custom_call" | custom-call | flops 19549999104 | bytes 1700000 | tf_op jit(solution)/shard_map/attn_bwd/pallas_call | solution.py:63
  332.9 2.9 collective-permute-done.13.refs_3_
  336.2 15.4 %attn_bwd.5 = (bf16[1,576,1152]{2,1,0:T(8,128)(2,1)S(1)}, bf16[1,576,1152]{2,1,0:T(8,128)(2,1)}, f32[1,896]{1,0:T(1,128)S(1)}, bf16[768,896]{1,0:T(8,128)(2,1)S(1)}) custom-call(s32[3]{0:T(128)S(1)} %copy-done.28, bf16[32,144,1152]{2,1,0:T(8,128)(2,1)} %all-gather.4.cloned.1.call-done.refs_1_.refs_2_.refs_3_.refs_4_, ...), custom_call_target="tpu_custom_call" | custom-call | flops 19549999104 | bytes 1700000 | tf_op jit(solution)/shard_map/attn_bwd/pallas_call | solution.py:63
  353.2 2.4 collective-permute-start.28
  355.6 3.5 collective-permute-done.21.refs_4_
  362.2 15.4 %attn_bwd.7 = (bf16[1,576,1152]{2,1,0:T(8,128)(2,1)S(1)}, bf16[1,576,1152]{2,1,0:T(8,128)(2,1)S(1)}, f32[1,896]{1,0:T(1,128)S(1)}, bf16[768,896]{1,0:T(8,128)(2,1)S(1)}) custom-call(s32[3]{0:T(128)S(1)} %copy-done.28, bf16[32,144,1152]{2,1,0:T(8,128)(2,1)} %all-gather.4.cloned.1.call-done.refs_1_.refs_2_.refs_3_.refs_4_, ...), custom_call_target="tpu_custom_call" | custom-call | flops 19549999104 | bytes 1700000 | tf_op jit(solution)/shard_map/attn_bwd/pallas_call | solution.py:63
  387.5 9.2 %collective-permute-done.24.refs_6_ = bf16[2,144,1152]{2,1,0:T(8,128)(2,1)S(1)} collective-permute-done((bf16[2,144,1152]{2,1,0:T(8,128)(2,1)}, bf16[2,144,1152]{2,1,0:T(8,128)(2,1)S(1)}, u32[]{:S(2)}, u32[]{:S(2)}) %collective-permute-start.24) | collective-permute-done | bytes 663584 | tf_op jit(solution)/shard_map/ppermute | solution.py:623
  404.4 15.9 %norm_back.1 = (bf16[768,1152]{1,0:T(8,128)(2,1)S(1)}, f32[2,1152]{1,0:T(2,128)S(1)}) custom-call(s32[3]{0:T(128)S(1)} %copy-done.28, bf16[32,144,1152]{2,1,0:T(8,128)(2,1)} %all-gather.4.cloned.1.call-done.refs_1_.refs_2_.refs_3_.refs_4_, bf16[32,144,1152]{2,1,0:T(8,128)(2,1)} %all-gather.4.cloned.1.call-done.refs_1_.refs_2_.refs_3_.refs_4_, ...), custom_call_target="tpu_custom_call" | custom-call | flops 20700000256 | bytes 1800000 | tf_op jit(solution)/shard_map/norm_back/pallas_call | solution.py:63
  422.2 3.0 copy-done.31
  425.2 13.6 %mixed.1 = bf16[768,1152]{1,0:T(8,128)(2,1)S(1)} custom-call(s32[3]{0:T(128)S(1)} %copy-done.28, bf16[32,144,1152]{2,1,0:T(8,128)(2,1)} %bitcast.326, bf16[32,144,1152]{2,1,0:T(8,128)(2,1)} %bitcast.327, bf16[32,144,1152]{2,1,0:T(8,128)(2,1)} %bitcast.328, bf16[32,144,1152]{2,1,0:T(8,128)(2,1)} %bitcast.329, ...), custom_call_target="tpu_custom_call" | custom-call | flops 16099999744 | bytes 1400000 | tf_op jit(solution)/shard_map/mixed/pallas_call | solution.py:63
  454.8 6.8 %collective-permute-done.33 = f32[15104]{0:T(1024)S(1)} collective-permute-done((f32[15104]{0:T(1024)S(1)}, f32[15104]{0:T(1024)S(1)}, u32[]{:S(2)}, u32[]{:S(2)}) %collective-permute-start.33) | collective-permute-done | bytes 60448 | tf_op jit(solution)/shard_map/ppermute | solution.py:623
  467.7 6.6 %collective-permute-done.37 = f32[15104]{0:T(1024)S(1)} collective-permute-done((f32[15104]{0:T(1024)S(1)}, f32[15104]{0:T(1024)S(1)}, u32[]{:S(2)}, u32[]{:S(2)}) %collective-permute-start.37) | collective-permute-done | bytes 60448 | tf_op jit(solution)/shard_map/ppermute | solution.py:808
  476.5 3.1 collective-permute-done.40
  (407 shorter events, 118.0 us)
Async XLA Ops:
  7.2 120.0 %all-gather.4.cloned.1.call-start = ((), (), s32[]{:S(2)}) async-start(), calls=%async_computation.1 | async-start | bytes 10948608 | tf_op jit(solution)/shard_map/all_gather | solution.py:637
  11.3 205.7 %all-gather.6.cloned.1.call-start = ((), (), s32[]{:S(2)}) async-start(), calls=%async_computation.3 | async-start | bytes 10948608 | tf_op jit(solution)/shard_map/all_gather | solution.py:637
  31.0 31.4 %collective-permute-start.1 = (bf16[2,144,1152]{2,1,0:T(8,128)(2,1)S(1)}, bf16[2,144,1152]{2,1,0:T(8,128)(2,1)S(1)}, u32[]{:S(2)}, u32[]{:S(2)}) collective-permute-start(bf16[2,144,1152]{2,1,0:T(8,128)(2,1)S(1)} %get-tuple-element.245), channel_id=1, source_target_pairs={{0,8},{4,12},{8,0},{12,4},{16,24},{20,28},{24,16},{28,20},{1,9},{5... | collective-permute-start | bytes 1990664 | tf_op jit(solution)/shard_map/ppermute | solution.py:623
  61.2 22.3 %collective-permute-start.5 = (bf16[2,144,1152]{2,1,0:T(8,128)(2,1)S(1)}, bf16[2,144,1152]{2,1,0:T(8,128)(2,1)S(1)}, u32[]{:S(2)}, u32[]{:S(2)}) collective-permute-start(bf16[2,144,1152]{2,1,0:T(8,128)(2,1)S(1)} %get-tuple-element.243), channel_id=1, source_target_pairs={{0,16},{4,20},{8,24},{12,28},{16,0},{20,4},{24,8},{28,12},{1,17},{... | collective-permute-start | bytes 1990664 | tf_op jit(solution)/shard_map/ppermute | solution.py:623
  64.1 54.6 %collective-permute-start.2 = (bf16[2,2,144,1152]{3,2,1,0:T(8,128)(2,1)}, bf16[2,2,144,1152]{3,2,1,0:T(8,128)(2,1)S(1)}, u32[]{:S(2)}, u32[]{:S(2)}) collective-permute-start(bf16[2,2,144,1152]{3,2,1,0:T(8,128)(2,1)} %get-tuple-element.219.refs_1_.refs_7_.refs_13_.refs_19_), channel_id=1, source_target_pairs={{0,16},{4,20},{8,24},{12,28},{16,0},{20,4},{24,8},{28,12},{1,17},{... | collective-permute-start | bytes 3981320 | tf_op jit(solution)/shard_map/ppermute | solution.py:623
  85.2 33.5 %collective-permute-start.6 = (bf16[2,2,144,1152]{3,2,1,0:T(8,128)(2,1)}, bf16[2,2,144,1152]{3,2,1,0:T(8,128)(2,1)}, u32[]{:S(2)}, u32[]{:S(2)}) collective-permute-start(bf16[2,2,144,1152]{3,2,1,0:T(8,128)(2,1)} %get-tuple-element.221.refs_2_.refs_8_.refs_14_.refs_20_), channel_id=1, source_target_pairs={{0,8},{4,12},{8,0},{12,4},{16,24},{20,28},{24,16},{28,20},{1,9},{5... | collective-permute-start | bytes 3981320 | tf_op jit(solution)/shard_map/ppermute | solution.py:623
  127.2 315.1 %reduce-scatter.2.cloned.1.call-start = ((), (), s32[]{:S(2)}) async-start(), calls=%async_computation.2 | async-start | bytes 10948608 | tf_op jit(solution)/shard_map/reduce_scatter | solution.py:707
  134.1 51.1 %collective-permute-start.7 = (bf16[2,2,2,144,1152]{4,3,2,1,0:T(8,128)(2,1)S(1)}, bf16[2,2,2,144,1152]{4,3,2,1,0:T(8,128)(2,1)}, u32[]{:S(2)}, u32[]{:S(2)}) collective-permute-start(bf16[2,2,2,144,1152]{4,3,2,1,0:T(8,128)(2,1)S(1)} %pad_maximum_fusion), channel_id=1, source_target_pairs={{0,4},{4,0},{8,12},{12,8},{16,20},{20,16},{24,28},{28,24},{1,5},{5... | collective-permute-start | bytes 7962632 | tf_op jit(solution)/shard_map/ppermute | solution.py:623
  138.4 46.7 %collective-permute-start.8 = (bf16[2,2,2,144,1152]{4,3,2,1,0:T(8,128)(2,1)}, bf16[2,2,2,144,1152]{4,3,2,1,0:T(8,128)(2,1)}, u32[]{:S(2)}, u32[]{:S(2)}) collective-permute-start(bf16[2,2,2,144,1152]{4,3,2,1,0:T(8,128)(2,1)} %pad_maximum_fusion.1), channel_id=1, source_target_pairs={{0,4},{4,0},{8,12},{12,8},{16,20},{20,16},{24,28},{28,24},{1,5},{5... | collective-permute-start | bytes 7962632 | tf_op jit(solution)/shard_map/ppermute | solution.py:623
  240.9 35.2 %collective-permute-start.9 = (bf16[2,576,1152]{2,1,0:T(8,128)(2,1)}, bf16[2,576,1152]{2,1,0:T(8,128)(2,1)S(1)}, u32[]{:S(2)}, u32[]{:S(2)}) collective-permute-start(bf16[2,576,1152]{2,1,0:T(8,128)(2,1)} %get-tuple-element.119), channel_id=1, source_target_pairs={{0,4},{4,0},{8,12},{12,8},{16,20},{20,16},{24,28},{28,24},{1,5},{5... | collective-permute-start | bytes 7962632 | tf_op jit(solution)/shard_map/ppermute | solution.py:623
  271.9 26.2 %collective-permute-start.14 = (bf16[2,576,1152]{2,1,0:T(8,128)(2,1)}, bf16[2,576,1152]{2,1,0:T(8,128)(2,1)S(1)}, u32[]{:S(2)}, u32[]{:S(2)}) collective-permute-start(bf16[2,576,1152]{2,1,0:T(8,128)(2,1)} %get-tuple-element.134), channel_id=1, source_target_pairs={{0,4},{4,0},{8,12},{12,8},{16,20},{20,16},{24,28},{28,24},{1,5},{5... | collective-permute-start | bytes 7962632 | tf_op jit(solution)/shard_map/ppermute | solution.py:623
  277.5 25.7 %collective-permute-start.10 = (bf16[2,144,1152]{2,1,0:T(8,128)(2,1)}, bf16[2,144,1152]{2,1,0:T(8,128)(2,1)S(1)}, u32[]{:S(2)}, u32[]{:S(2)}) collective-permute-start(bf16[2,144,1152]{2,1,0:T(8,128)(2,1)} %pad_maximum_fusion.6), channel_id=1, source_target_pairs={{0,8},{4,12},{8,0},{12,4},{16,24},{20,28},{24,16},{28,20},{1,9},{5... | collective-permute-start | bytes 1990664 | tf_op jit(solution)/shard_map/ppermute | solution.py:623
  280.6 22.8 %collective-permute-start.11 = (bf16[2,144,1152]{2,1,0:T(8,128)(2,1)}, bf16[2,144,1152]{2,1,0:T(8,128)(2,1)S(1)}, u32[]{:S(2)}, u32[]{:S(2)}) collective-permute-start(bf16[2,144,1152]{2,1,0:T(8,128)(2,1)} %pad_maximum_fusion.7), channel_id=1, source_target_pairs={{0,16},{4,20},{8,24},{12,28},{16,0},{20,4},{24,8},{28,12},{1,17},{... | collective-permute-start | bytes 1990664 | tf_op jit(solution)/shard_map/ppermute | solution.py:623
  297.7 34.9 %collective-permute-start.17 = (bf16[1,576,1152]{2,1,0:T(8,128)(2,1)S(1)}, bf16[1,576,1152]{2,1,0:T(8,128)(2,1)S(1)}, u32[]{:S(2)}, u32[]{:S(2)}) collective-permute-start(bf16[1,576,1152]{2,1,0:T(8,128)(2,1)S(1)} %get-tuple-element.137), channel_id=1, source_target_pairs={{0,4},{4,0},{8,12},{12,8},{16,20},{20,16},{24,28},{28,24},{1,5},{5... | collective-permute-start | bytes 3981320 | tf_op jit(solution)/shard_map/ppermute | solution.py:623
  299.0 27.3 %collective-permute-start.15 = (bf16[2,144,1152]{2,1,0:T(8,128)(2,1)S(1)}, bf16[2,144,1152]{2,1,0:T(8,128)(2,1)S(1)}, u32[]{:S(2)}, u32[]{:S(2)}) collective-permute-start(bf16[2,144,1152]{2,1,0:T(8,128)(2,1)S(1)} %pad_maximum_fusion.8), channel_id=1, source_target_pairs={{0,8},{4,12},{8,0},{12,4},{16,24},{20,28},{24,16},{28,20},{1,9},{5... | collective-permute-start | bytes 1990664 | tf_op jit(solution)/shard_map/ppermute | solution.py:623
  302.9 25.8 %collective-permute-start.16 = (bf16[2,144,1152]{2,1,0:T(8,128)(2,1)}, bf16[2,144,1152]{2,1,0:T(8,128)(2,1)S(1)}, u32[]{:S(2)}, u32[]{:S(2)}) collective-permute-start(bf16[2,144,1152]{2,1,0:T(8,128)(2,1)} %pad_maximum_fusion.9), channel_id=1, source_target_pairs={{0,16},{4,20},{8,24},{12,28},{16,0},{20,4},{24,8},{28,12},{1,17},{... | collective-permute-start | bytes 1990664 | tf_op jit(solution)/shard_map/ppermute | solution.py:623
  305.8 30.0 %collective-permute-start.13 = (bf16[1,144,1152]{2,1,0:T(8,128)(2,1)}, bf16[1,144,1152]{2,1,0:T(8,128)(2,1)S(1)}, u32[]{:S(2)}, u32[]{:S(2)}) collective-permute-start(bf16[1,144,1152]{2,1,0:T(8,128)(2,1)} %fusion.40), channel_id=1, source_target_pairs={{0,16},{4,20},{8,24},{12,28},{16,0},{20,4},{24,8},{28,12},{1,17},{... | collective-permute-start | bytes 995336 | tf_op jit(solution)/shard_map/ppermute | solution.py:623
  307.5 28.7 %collective-permute-start.12 = (bf16[1,144,1152]{2,1,0:T(8,128)(2,1)}, bf16[1,144,1152]{2,1,0:T(8,128)(2,1)S(1)}, u32[]{:S(2)}, u32[]{:S(2)}) collective-permute-start(bf16[1,144,1152]{2,1,0:T(8,128)(2,1)} %fusion.39), channel_id=1, source_target_pairs={{0,8},{4,12},{8,0},{12,4},{16,24},{20,28},{24,16},{28,20},{1,9},{5... | collective-permute-start | bytes 995336 | tf_op jit(solution)/shard_map/ppermute | solution.py:623
  330.0 30.8 %collective-permute-start.20 = (bf16[1,144,1152]{2,1,0:T(8,128)(2,1)S(1)}, bf16[1,144,1152]{2,1,0:T(8,128)(2,1)S(1)}, u32[]{:S(2)}, u32[]{:S(2)}) collective-permute-start(bf16[1,144,1152]{2,1,0:T(8,128)(2,1)S(1)} %fusion.42), channel_id=1, source_target_pairs={{0,16},{4,20},{8,24},{12,28},{16,0},{20,4},{24,8},{28,12},{1,17},{... | collective-permute-start | bytes 995336 | tf_op jit(solution)/shard_map/ppermute | solution.py:623
  332.0 30.2 %collective-permute-start.19 = (bf16[1,144,1152]{2,1,0:T(8,128)(2,1)S(1)}, bf16[1,144,1152]{2,1,0:T(8,128)(2,1)S(1)}, u32[]{:S(2)}, u32[]{:S(2)}) collective-permute-start(bf16[1,144,1152]{2,1,0:T(8,128)(2,1)S(1)} %fusion.41), channel_id=1, source_target_pairs={{0,8},{4,12},{8,0},{12,4},{16,24},{20,28},{24,16},{28,20},{1,9},{5... | collective-permute-start | bytes 995336 | tf_op jit(solution)/shard_map/ppermute | solution.py:623
  332.6 29.6 %collective-permute-start.22 = (bf16[1,576,1152]{2,1,0:T(8,128)(2,1)S(1)}, bf16[1,576,1152]{2,1,0:T(8,128)(2,1)S(1)}, u32[]{:S(2)}, u32[]{:S(2)}) collective-permute-start(bf16[1,576,1152]{2,1,0:T(8,128)(2,1)S(1)} %get-tuple-element.149), channel_id=1, source_target_pairs={{0,4},{4,0},{8,12},{12,8},{16,20},{20,16},{24,28},{28,24},{1,5},{5... | collective-permute-start | bytes 3981320 | tf_op jit(solution)/shard_map/ppermute | solution.py:623
  335.8 23.4 %collective-permute-start.21 = (bf16[2,144,1152]{2,1,0:T(8,128)(2,1)S(1)}, bf16[2,144,1152]{2,1,0:T(8,128)(2,1)S(1)}, u32[]{:S(2)}, u32[]{:S(2)}) collective-permute-start(bf16[2,144,1152]{2,1,0:T(8,128)(2,1)S(1)} %pad_maximum_fusion.10), channel_id=1, source_target_pairs={{0,8},{4,12},{8,0},{12,4},{16,24},{20,28},{24,16},{28,20},{1,9},{5... | collective-permute-start | bytes 1990664 | tf_op jit(solution)/shard_map/ppermute | solution.py:623
  353.2 24.5 %collective-permute-start.28 = (bf16[144,1152]{1,0:T(8,128)(2,1)S(1)}, bf16[144,1152]{1,0:T(8,128)(2,1)S(1)}, u32[]{:S(2)}, u32[]{:S(2)}) collective-permute-start(bf16[144,1152]{1,0:T(8,128)(2,1)S(1)} %fusion.14), channel_id=1, source_target_pairs={{0,3},{1,0},{2,1},{3,2},{4,7},{5,4},{6,5},{7,6},{8,11},{9,8},{10,9... | collective-permute-start | bytes 995336 | tf_op jit(solution)/shard_map/ppermute | solution.py:619
  359.2 38.3 %collective-permute-start.18 = (bf16[1,576,1152]{2,1,0:T(8,128)(2,1)}, bf16[1,576,1152]{2,1,0:T(8,128)(2,1)}, u32[]{:S(2)}, u32[]{:S(2)}) collective-permute-start(bf16[1,576,1152]{2,1,0:T(8,128)(2,1)} %get-tuple-element.141), channel_id=1, source_target_pairs={{0,4},{4,0},{8,12},{12,8},{16,20},{20,16},{24,28},{28,24},{1,5},{5... | collective-permute-start | bytes 3981320 | tf_op jit(solution)/shard_map/ppermute | solution.py:623
  360.8 24.1 %collective-permute-start.26 = (bf16[1,144,1152]{2,1,0:T(8,128)(2,1)}, bf16[1,144,1152]{2,1,0:T(8,128)(2,1)}, u32[]{:S(2)}, u32[]{:S(2)}) collective-permute-start(bf16[1,144,1152]{2,1,0:T(8,128)(2,1)} %fusion.44), channel_id=1, source_target_pairs={{0,16},{4,20},{8,24},{12,28},{16,0},{20,4},{24,8},{28,12},{1,17},{... | collective-permute-start | bytes 995336 | tf_op jit(solution)/shard_map/ppermute | solution.py:623
  382.9 37.4 %collective-permute-start.29 = (bf16[144,1152]{1,0:T(8,128)(2,1)}, bf16[144,1152]{1,0:T(8,128)(2,1)S(1)}, u32[]{:S(2)}, u32[]{:S(2)}) collective-permute-start(bf16[144,1152]{1,0:T(8,128)(2,1)} %fusion.10), channel_id=1, source_target_pairs={{0,3},{1,0},{2,1},{3,2},{4,7},{5,4},{6,5},{7,6},{8,11},{9,8},{10,9... | collective-permute-start | bytes 995336 | tf_op jit(solution)/shard_map/ppermute | solution.py:619
  386.3 34.1 %collective-permute-start.27 = (bf16[144,1152]{1,0:T(8,128)(2,1)S(1)}, bf16[144,1152]{1,0:T(8,128)(2,1)S(1)}, u32[]{:S(2)}, u32[]{:S(2)}) collective-permute-start(bf16[144,1152]{1,0:T(8,128)(2,1)S(1)} %fusion.17), channel_id=1, source_target_pairs={{0,3},{1,0},{2,1},{3,2},{4,7},{5,4},{6,5},{7,6},{8,11},{9,8},{10,9... | collective-permute-start | bytes 995336 | tf_op jit(solution)/shard_map/ppermute | solution.py:619
  398.8 21.6 %collective-permute-start.25 = (bf16[1,144,1152]{2,1,0:T(8,128)(2,1)S(1)}, bf16[1,144,1152]{2,1,0:T(8,128)(2,1)S(1)}, u32[]{:S(2)}, u32[]{:S(2)}) collective-permute-start(bf16[1,144,1152]{2,1,0:T(8,128)(2,1)S(1)} %fusion.43), channel_id=1, source_target_pairs={{0,8},{4,12},{8,0},{12,4},{16,24},{20,28},{24,16},{28,20},{1,9},{5... | collective-permute-start | bytes 995336 | tf_op jit(solution)/shard_map/ppermute | solution.py:623
  400.6 21.5 %collective-permute-start.23 = (bf16[2,144,1152]{2,1,0:T(8,128)(2,1)S(1)}, bf16[2,144,1152]{2,1,0:T(8,128)(2,1)S(1)}, u32[]{:S(2)}, u32[]{:S(2)}) collective-permute-start(bf16[2,144,1152]{2,1,0:T(8,128)(2,1)S(1)} %pad_maximum_fusion.11), channel_id=1, source_target_pairs={{0,8},{4,12},{8,0},{12,4},{16,24},{20,28},{24,16},{28,20},{1,9},{5... | collective-permute-start | bytes 1990664 | tf_op jit(solution)/shard_map/ppermute | solution.py:623
  402.7 39.6 %collective-permute-start.31 = (bf16[2,144,1152]{2,1,0:T(8,128)(2,1)S(1)}, bf16[2,144,1152]{2,1,0:T(8,128)(2,1)}, u32[]{:S(2)}, u32[]{:S(2)}) collective-permute-start(bf16[2,144,1152]{2,1,0:T(8,128)(2,1)S(1)} %pad_maximum_fusion.13), channel_id=1, source_target_pairs={{0,16},{4,20},{8,24},{12,28},{16,0},{20,4},{24,8},{28,12},{1,17},{... | collective-permute-start | bytes 1990664 | tf_op jit(solution)/shard_map/ppermute | solution.py:623
  443.7 17.8 %collective-permute-start.34 = (bf16[1,144,1152]{2,1,0:T(8,128)(2,1)S(1)}, bf16[1,144,1152]{2,1,0:T(8,128)(2,1)S(1)}, u32[]{:S(2)}, u32[]{:S(2)}) collective-permute-start(bf16[1,144,1152]{2,1,0:T(8,128)(2,1)S(1)} %fusion.45), channel_id=1, source_target_pairs={{0,16},{4,20},{8,24},{12,28},{16,0},{20,4},{24,8},{28,12},{1,17},{... | collective-permute-start | bytes 995336 | tf_op jit(solution)/shard_map/ppermute | solution.py:623
  445.8 17.5 %collective-permute-start.38 = (bf16[144,1152]{1,0:T(8,128)(2,1)S(1)}, bf16[144,1152]{1,0:T(8,128)(2,1)S(1)}, u32[]{:S(2)}, u32[]{:S(2)}) collective-permute-start(bf16[144,1152]{1,0:T(8,128)(2,1)S(1)} %fusion.6), channel_id=1, source_target_pairs={{0,3},{1,0},{2,1},{3,2},{4,7},{5,4},{6,5},{7,6},{8,11},{9,8},{10,9... | collective-permute-start | bytes 995336 | tf_op jit(solution)/shard_map/ppermute | solution.py:619
  (114 other events, 1536.8 us)
Sparse Core Ops, SparseCore 0:
  11.4 115.7 all-gather.3
  130.0 85.6 all-gather.5
  221.8 162.2 reduce-scatter.1

commit v5 on v4

--- a/solution.py
+++ b/solution.py
@@ -144,7 +144,7 @@
     def step(t, carry):
         return body(pl.ds(pl.multiple_of(t * STEP, STEP), STEP), carry)
 
-    return lax.fori_loop(0, total // STEP, step, carry, unroll=4)
+    return lax.fori_loop(0, total // STEP, step, carry, unroll=8)
 
 
 def norm_stats(rows):

time: 494 us -> 494 us (level)
  no operation moved by 1% of the time
where the time goes in v5:
time: 494 us; the launch traced here: 488 us
  Pallas kernels  220 us (45%)
  waiting for transfers between devices  128 us (26%)
  other arithmetic  45.4 us (9%)
  local copies, waits for them, and re-layouts  42.3 us (9%)
  starting transfers between devices  36.5 us (7%)
  between operations  16.2 us (3%)
    pallas_call x15, Pallas kernels, call(): pl.pallas_call(body, grid_spec=pltpu.PrefetchScalarGridSpec(num_scalar_pr...  220 us
    ppermute x31, waiting for transfers between devices, swap(): lax.ppermute(value, 'dp', [(i, i ^ offset) for i in range(lax.axis_size('...  82.3 us
    ppermute x9, waiting for transfers between devices, ring(): lax.ppermute(value, 'tensor', [(i, (i + by) % size) for i in range(size)])  26.6 us
    ppermute x31, starting transfers between devices, swap(): lax.ppermute(value, 'dp', [(i, i ^ offset) for i in range(lax.axis_size('...  21 us
    unnamed x201, local copies, waits for them, and re-layouts  16.7 us
    ppermute x9, starting transfers between devices, ring(): lax.ppermute(value, 'tensor', [(i, (i + by) % size) for i in range(size)])  15 us
    another operation x16, other arithmetic, send(): value = swap(jnp.stack([v for i in mine for v in outs[i]]), link)  10.8 us
    ppermute x2, waiting for transfers between devices, sum_all(): lax.ppermute(vector, 'tensor', [(i, i ^ offset) for i in range(size)])  10.4 us
  transfers between devices with their start and end apart: 45, of which 17 were waited for; matrix products, arithmetic and copies ran while one was open for 13% of the time, Pallas kernels for 45%

profile of v5, /device:TPU:0, one launch (start us, length us, event | category | flops | bytes accessed | tf_op | source)
XLA Modules:
  0.0 488.2 jit_solution(9531913758026581460)
XLA Ops:
  13.8 3.0 collective-permute-start
  23.8 4.3 collective-permute-done
  32.5 11.2 %collective-permute-done.3 = bf16[160,1152]{1,0:T(8,128)(2,1)S(1)} collective-permute-done((bf16[160,1152]{1,0:T(8,128)(2,1)}, bf16[160,1152]{1,0:T(8,128)(2,1)S(1)}, u32[]{:S(2)}, u32[]{:S(2)}) %collective-permute-start.3) | collective-permute-done | bytes 368672 | tf_op jit(solution)/shard_map/ppermute | solution.py:619
  43.7 3.1 norm_one.1
  49.3 11.1 %collective-permute-done.4 = bf16[160,1152]{1,0:T(8,128)(2,1)S(1)} collective-permute-done((bf16[160,1152]{1,0:T(8,128)(2,1)S(1)}, bf16[160,1152]{1,0:T(8,128)(2,1)S(1)}, u32[]{:S(2)}, u32[]{:S(2)}) %collective-permute-start.4) | collective-permute-done | bytes 368672 | tf_op jit(solution)/shard_map/ppermute | solution.py:619
  64.9 18.6 %collective-permute-done.5 = bf16[2,144,1152]{2,1,0:T(8,128)(2,1)S(1)} collective-permute-done((bf16[2,144,1152]{2,1,0:T(8,128)(2,1)S(1)}, bf16[2,144,1152]{2,1,0:T(8,128)(2,1)S(1)}, u32[]{:S(2)}, u32[]{:S(2)}) %collective-permute-start.5) | collective-permute-done | bytes 663584 | tf_op jit(solution)/shard_map/ppermute | solution.py:623
  86.3 32.4 %collective-permute-done.2.refs_2_.refs_4_.refs_10_.refs_16_.refs_22_ = bf16[2,2,144,1152]{3,2,1,0:T(8,128)(2,1)S(1)} collective-permute-done((bf16[2,2,144,1152]{3,2,1,0:T(8,128)(2,1)}, bf16[2,2,144,1152]{3,2,1,0:T(8,128)(2,1)S(1)}, u32[]{:S(2)}, u32[]{:S(2)}) %collective-permute-start.2) | collective-permute-done | bytes 1327136 | tf_op jit(solution)/shard_map/ppermute | solution.py:623
  118.7 8.5 %all-gather.4.cloned.1.call-done.refs_1_.refs_2_.refs_3_.refs_4_ = bf16[32,144,1152]{2,1,0:T(8,128)(2,1)} async-done(((bf16[1,144,1152]{2,1,0:T(8,128)(2,1)}), bf16[32,144,1152]{2,1,0:T(8,128)(2,1)}) %all-gather.4.cloned.1.call-update) | async-done | bytes 10616848 | tf_op jit(solution)/shard_map/all_gather | solution.py:637
  134.4 4.0 pad_maximum_fusion.1
  140.1 7.9 %attn_fwd.4 = (bf16[768,896]{1,0:T(8,128)(2,1)S(1)}, bf16[768,384]{1,0:T(8,128)(2,1)S(1)}, f32[8,768]{1,0:T(8,128)S(1)}) custom-call(s32[3]{0:T(128)S(1)} %copy-done.27, bf16[32,144,1152]{2,1,0:T(8,128)(2,1)S(1)} %copy-done.29, bf16[2,2,144,1152]{3,2,1,0:T(8,128)(2,1)S(1)} %collective-permute-done.2.refs_2_.refs_4_.refs_10_.refs_16_.refs_22_, ...), custom_call_target="tpu_custom_call" | custom-call | flops 9200000000 | bytes 800000 | tf_op jit(solution)/shard_map/attn_fwd/pallas_call | solution.py:63
  148.1 7.5 %attn_fwd.7 = (bf16[768,896]{1,0:T(8,128)(2,1)S(1)}, bf16[768,384]{1,0:T(8,128)(2,1)S(1)}, f32[8,768]{1,0:T(8,128)S(1)}) custom-call(s32[3]{0:T(128)S(1)} %copy-done.27, bf16[32,144,1152]{2,1,0:T(8,128)(2,1)S(1)} %copy-done.29, bf16[768,1152]{1,0:T(8,128)(2,1)S(1)} %copy-done.43, f32[1,896]{1,0:T(1,128)S(1)} %slice.620.refs_3_), custom_call_target="tpu_custom_call" | custom-call | flops 9200000000 | bytes 800000 | tf_op jit(solution)/shard_map/attn_fwd/pallas_call | solution.py:63
  155.6 7.6 %attn_fwd.6 = (bf16[768,896]{1,0:T(8,128)(2,1)S(1)}, bf16[768,384]{1,0:T(8,128)(2,1)S(1)}, f32[8,768]{1,0:T(8,128)S(1)}) custom-call(s32[3]{0:T(128)S(1)} %copy-done.27, bf16[32,144,1152]{2,1,0:T(8,128)(2,1)S(1)} %copy-done.29, bf16[768,1152]{1,0:T(8,128)(2,1)S(1)} %copy-done.43, f32[1,896]{1,0:T(1,128)S(1)} %slice.614.refs_3_), custom_call_target="tpu_custom_call" | custom-call | flops 9200000000 | bytes 800000 | tf_op jit(solution)/shard_map/attn_fwd/pallas_call | solution.py:63
  163.2 7.4 %attn_fwd.5 = (bf16[768,896]{1,0:T(8,128)(2,1)S(1)}, bf16[768,384]{1,0:T(8,128)(2,1)S(1)}, f32[8,768]{1,0:T(8,128)S(1)}) custom-call(s32[3]{0:T(128)S(1)} %copy-done.27, bf16[32,144,1152]{2,1,0:T(8,128)(2,1)S(1)} %copy-done.29, bf16[768,1152]{1,0:T(8,128)(2,1)S(1)} %copy-done.43, f32[1,896]{1,0:T(1,128)S(1)} %slice.608.refs_3_), custom_call_target="tpu_custom_call" | custom-call | flops 9200000000 | bytes 800000 | tf_op jit(solution)/shard_map/attn_fwd/pallas_call | solution.py:63
  170.7 10.0 %norm_two.1 = (f32[768,1152]{1,0:T(8,128)S(1)}, bf16[768,1152]{1,0:T(8,128)(2,1)S(1)}, bf16[1152,768]{1,0:T(8,128)(2,1)S(1)}) custom-call(s32[3]{0:T(128)S(1)} %copy-done.27, bf16[32,144,1152]{2,1,0:T(8,128)(2,1)} %all-gather.4.cloned.1.call-done.refs_1_.refs_2_.refs_3_.refs_4_, ...), custom_call_target="tpu_custom_call" | custom-call | flops 13799999488 | bytes 1200000 | tf_op jit(solution)/shard_map/norm_two/pallas_call | solution.py:63
  184.9 31.8 %ffn_one.1 = (bf16[4,768,1152]{2,1,0:T(8,128)(2,1)}, bf16[4,768,1152]{2,1,0:T(8,128)(2,1)}, bf16[8,4,144,1152]{3,2,1,0:T(8,128)(2,1)}) custom-call(s32[3]{0:T(128)} %copy-done.26, bf16[2,2,144,1152]{3,2,1,0:T(8,128)(2,1)} %get-tuple-element.219.refs_1_.refs_7_.refs_13_.refs_19_, ...), custom_call_target="tpu_custom_call" | custom-call | flops 34500001792 | bytes 3000000 | tf_op jit(solution)/shard_map/ffn_one/pallas_call | solution.py:63
  216.8 23.7 %ffn_two.2 = (bf16[2,576,1152]{2,1,0:T(8,128)(2,1)}, bf16[2,576,1152]{2,1,0:T(8,128)(2,1)}, f32[2,1,1152]{2,1,0:T(1,128)}, f32[768,1152]{1,0:T(8,128)}) custom-call(s32[3]{0:T(128)} %copy-done.26, bf16[2,2,144,1152]{3,2,1,0:T(8,128)(2,1)} %get-tuple-element.219.refs_1_.refs_7_.refs_13_.refs_19_, ...), custom_call_target="tpu_custom_call" | custom-call | flops 27599998976 | bytes 2400000 | tf_op jit(solution)/shard_map/ffn_two/pallas_call | solution.py:63
  240.8 29.8 %ffn_two.3 = (bf16[2,576,1152]{2,1,0:T(8,128)(2,1)}, bf16[2,576,1152]{2,1,0:T(8,128)(2,1)}, f32[2,1,1152]{2,1,0:T(1,128)}, f32[768,1152]{1,0:T(8,128)}, bf16[768...) custom-call(s32[3]{0:T(128)} %copy-done.26, ...), custom_call_target="tpu_custom_call" | custom-call | flops 34500001792 | bytes 3000000 | tf_op jit(solution)/shard_map/ffn_two/pallas_call | solution.py:63
  281.3 15.6 %attn_bwd.4 = (bf16[1,576,1152]{2,1,0:T(8,128)(2,1)S(1)}, bf16[1,576,1152]{2,1,0:T(8,128)(2,1)S(1)}, f32[1,896]{1,0:T(1,128)S(1)}, bf16[768,896]{1,0:T(8,128)(2,1)S(1)}) custom-call(s32[3]{0:T(128)S(1)} %copy-done.28, bf16[32,144,1152]{2,1,0:T(8,128)(2,1)} %all-gather.4.cloned.1.call-done.refs_1_.refs_2_.refs_3_.refs_4_, ...), custom_call_target="tpu_custom_call" | custom-call | flops 19549999104 | bytes 1700000 | tf_op jit(solution)/shard_map/attn_bwd/pallas_call | solution.py:63
  306.9 15.4 %attn_bwd.6 = (bf16[1,576,1152]{2,1,0:T(8,128)(2,1)S(1)}, bf16[1,576,1152]{2,1,0:T(8,128)(2,1)S(1)}, f32[1,896]{1,0:T(1,128)S(1)}, bf16[768,896]{1,0:T(8,128)(2,1)S(1)}) custom-call(s32[3]{0:T(128)S(1)} %copy-done.28, bf16[32,144,1152]{2,1,0:T(8,128)(2,1)} %all-gather.4.cloned.1.call-done.refs_1_.refs_2_.refs_3_.refs_4_, ...), custom_call_target="tpu_custom_call" | custom-call | flops 19549999104 | bytes 1700000 | tf_op jit(solution)/shard_map/attn_bwd/pallas_call | solution.py:63
  326.2 3.0 collective-permute-done.16.refs_5_
  332.6 3.7 collective-permute-done.13.refs_3_
  336.9 15.4 %attn_bwd.5 = (bf16[1,576,1152]{2,1,0:T(8,128)(2,1)S(1)}, bf16[1,576,1152]{2,1,0:T(8,128)(2,1)}, f32[1,896]{1,0:T(1,128)S(1)}, bf16[768,896]{1,0:T(8,128)(2,1)S(1)}) custom-call(s32[3]{0:T(128)S(1)} %copy-done.28, bf16[32,144,1152]{2,1,0:T(8,128)(2,1)} %all-gather.4.cloned.1.call-done.refs_1_.refs_2_.refs_3_.refs_4_, ...), custom_call_target="tpu_custom_call" | custom-call | flops 19549999104 | bytes 1700000 | tf_op jit(solution)/shard_map/attn_bwd/pallas_call | solution.py:63
  362.0 15.4 %attn_bwd.7 = (bf16[1,576,1152]{2,1,0:T(8,128)(2,1)S(1)}, bf16[1,576,1152]{2,1,0:T(8,128)(2,1)S(1)}, f32[1,896]{1,0:T(1,128)S(1)}, bf16[768,896]{1,0:T(8,128)(2,1)S(1)}) custom-call(s32[3]{0:T(128)S(1)} %copy-done.28, bf16[32,144,1152]{2,1,0:T(8,128)(2,1)} %all-gather.4.cloned.1.call-done.refs_1_.refs_2_.refs_3_.refs_4_, ...), custom_call_target="tpu_custom_call" | custom-call | flops 19549999104 | bytes 1700000 | tf_op jit(solution)/shard_map/attn_bwd/pallas_call | solution.py:63
  382.3 3.2 collective-permute-start.29
  387.5 8.9 %collective-permute-done.24.refs_6_ = bf16[2,144,1152]{2,1,0:T(8,128)(2,1)S(1)} collective-permute-done((bf16[2,144,1152]{2,1,0:T(8,128)(2,1)}, bf16[2,144,1152]{2,1,0:T(8,128)(2,1)S(1)}, u32[]{:S(2)}, u32[]{:S(2)}) %collective-permute-start.24) | collective-permute-done | bytes 663584 | tf_op jit(solution)/shard_map/ppermute | solution.py:623
  404.1 15.6 %norm_back.1 = (bf16[768,1152]{1,0:T(8,128)(2,1)S(1)}, f32[2,1152]{1,0:T(2,128)S(1)}) custom-call(s32[3]{0:T(128)S(1)} %copy-done.28, bf16[32,144,1152]{2,1,0:T(8,128)(2,1)} %all-gather.4.cloned.1.call-done.refs_1_.refs_2_.refs_3_.refs_4_, bf16[32,144,1152]{2,1,0:T(8,128)(2,1)} %all-gather.4.cloned.1.call-done.refs_1_.refs_2_.refs_3_.refs_4_, ...), custom_call_target="tpu_custom_call" | custom-call | flops 20700000256 | bytes 1800000 | tf_op jit(solution)/shard_map/norm_back/pallas_call | solution.py:63
  421.9 3.0 copy-done.31
  424.9 13.6 %mixed.1 = bf16[768,1152]{1,0:T(8,128)(2,1)S(1)} custom-call(s32[3]{0:T(128)S(1)} %copy-done.28, bf16[32,144,1152]{2,1,0:T(8,128)(2,1)} %bitcast.326, bf16[32,144,1152]{2,1,0:T(8,128)(2,1)} %bitcast.327, bf16[32,144,1152]{2,1,0:T(8,128)(2,1)} %bitcast.328, bf16[32,144,1152]{2,1,0:T(8,128)(2,1)} %bitcast.329, ...), custom_call_target="tpu_custom_call" | custom-call | flops 16099999744 | bytes 1400000 | tf_op jit(solution)/shard_map/mixed/pallas_call | solution.py:63
  445.2 3.2 collective-permute-start.38
  454.8 7.4 %collective-permute-done.33 = f32[15104]{0:T(1024)S(1)} collective-permute-done((f32[15104]{0:T(1024)S(1)}, f32[15104]{0:T(1024)S(1)}, u32[]{:S(2)}, u32[]{:S(2)}) %collective-permute-start.33) | collective-permute-done | bytes 60448 | tf_op jit(solution)/shard_map/ppermute | solution.py:623
  467.6 6.6 %collective-permute-done.37 = f32[15104]{0:T(1024)S(1)} collective-permute-done((f32[15104]{0:T(1024)S(1)}, f32[15104]{0:T(1024)S(1)}, u32[]{:S(2)}, u32[]{:S(2)}) %collective-permute-start.37) | collective-permute-done | bytes 60448 | tf_op jit(solution)/shard_map/ppermute | solution.py:808
  475.7 3.7 collective-permute-done.40
  (407 shorter events, 116.1 us)
Async XLA Ops:
  7.2 120.0 %all-gather.4.cloned.1.call-start = ((), (), s32[]{:S(2)}) async-start(), calls=%async_computation.1 | async-start | bytes 10948608 | tf_op jit(solution)/shard_map/all_gather | solution.py:637
  11.3 205.5 %all-gather.6.cloned.1.call-start = ((), (), s32[]{:S(2)}) async-start(), calls=%async_computation.3 | async-start | bytes 10948608 | tf_op jit(solution)/shard_map/all_gather | solution.py:637
  31.0 31.4 %collective-permute-start.1 = (bf16[2,144,1152]{2,1,0:T(8,128)(2,1)S(1)}, bf16[2,144,1152]{2,1,0:T(8,128)(2,1)S(1)}, u32[]{:S(2)}, u32[]{:S(2)}) collective-permute-start(bf16[2,144,1152]{2,1,0:T(8,128)(2,1)S(1)} %get-tuple-element.245), channel_id=1, source_target_pairs={{0,8},{4,12},{8,0},{12,4},{16,24},{20,28},{24,16},{28,20},{1,9},{5... | collective-permute-start | bytes 1990664 | tf_op jit(solution)/shard_map/ppermute | solution.py:623
  61.2 22.3 %collective-permute-start.5 = (bf16[2,144,1152]{2,1,0:T(8,128)(2,1)S(1)}, bf16[2,144,1152]{2,1,0:T(8,128)(2,1)S(1)}, u32[]{:S(2)}, u32[]{:S(2)}) collective-permute-start(bf16[2,144,1152]{2,1,0:T(8,128)(2,1)S(1)} %get-tuple-element.243), channel_id=1, source_target_pairs={{0,16},{4,20},{8,24},{12,28},{16,0},{20,4},{24,8},{28,12},{1,17},{... | collective-permute-start | bytes 1990664 | tf_op jit(solution)/shard_map/ppermute | solution.py:623
  64.1 54.6 %collective-permute-start.2 = (bf16[2,2,144,1152]{3,2,1,0:T(8,128)(2,1)}, bf16[2,2,144,1152]{3,2,1,0:T(8,128)(2,1)S(1)}, u32[]{:S(2)}, u32[]{:S(2)}) collective-permute-start(bf16[2,2,144,1152]{3,2,1,0:T(8,128)(2,1)} %get-tuple-element.219.refs_1_.refs_7_.refs_13_.refs_19_), channel_id=1, source_target_pairs={{0,16},{4,20},{8,24},{12,28},{16,0},{20,4},{24,8},{28,12},{1,17},{... | collective-permute-start | bytes 3981320 | tf_op jit(solution)/shard_map/ppermute | solution.py:623
  85.2 33.5 %collective-permute-start.6 = (bf16[2,2,144,1152]{3,2,1,0:T(8,128)(2,1)}, bf16[2,2,144,1152]{3,2,1,0:T(8,128)(2,1)}, u32[]{:S(2)}, u32[]{:S(2)}) collective-permute-start(bf16[2,2,144,1152]{3,2,1,0:T(8,128)(2,1)} %get-tuple-element.221.refs_2_.refs_8_.refs_14_.refs_20_), channel_id=1, source_target_pairs={{0,8},{4,12},{8,0},{12,4},{16,24},{20,28},{24,16},{28,20},{1,9},{5... | collective-permute-start | bytes 3981320 | tf_op jit(solution)/shard_map/ppermute | solution.py:623
  127.2 314.8 %reduce-scatter.2.cloned.1.call-start = ((), (), s32[]{:S(2)}) async-start(), calls=%async_computation.2 | async-start | bytes 10948608 | tf_op jit(solution)/shard_map/reduce_scatter | solution.py:707
  134.1 50.9 %collective-permute-start.7 = (bf16[2,2,2,144,1152]{4,3,2,1,0:T(8,128)(2,1)S(1)}, bf16[2,2,2,144,1152]{4,3,2,1,0:T(8,128)(2,1)}, u32[]{:S(2)}, u32[]{:S(2)}) collective-permute-start(bf16[2,2,2,144,1152]{4,3,2,1,0:T(8,128)(2,1)S(1)} %pad_maximum_fusion), channel_id=1, source_target_pairs={{0,4},{4,0},{8,12},{12,8},{16,20},{20,16},{24,28},{28,24},{1,5},{5... | collective-permute-start | bytes 7962632 | tf_op jit(solution)/shard_map/ppermute | solution.py:623
  138.4 46.5 %collective-permute-start.8 = (bf16[2,2,2,144,1152]{4,3,2,1,0:T(8,128)(2,1)}, bf16[2,2,2,144,1152]{4,3,2,1,0:T(8,128)(2,1)}, u32[]{:S(2)}, u32[]{:S(2)}) collective-permute-start(bf16[2,2,2,144,1152]{4,3,2,1,0:T(8,128)(2,1)} %pad_maximum_fusion.1), channel_id=1, source_target_pairs={{0,4},{4,0},{8,12},{12,8},{16,20},{20,16},{24,28},{28,24},{1,5},{5... | collective-permute-start | bytes 7962632 | tf_op jit(solution)/shard_map/ppermute | solution.py:623
  240.5 34.8 %collective-permute-start.9 = (bf16[2,576,1152]{2,1,0:T(8,128)(2,1)}, bf16[2,576,1152]{2,1,0:T(8,128)(2,1)S(1)}, u32[]{:S(2)}, u32[]{:S(2)}) collective-permute-start(bf16[2,576,1152]{2,1,0:T(8,128)(2,1)} %get-tuple-element.119), channel_id=1, source_target_pairs={{0,4},{4,0},{8,12},{12,8},{16,20},{20,16},{24,28},{28,24},{1,5},{5... | collective-permute-start | bytes 7962632 | tf_op jit(solution)/shard_map/ppermute | solution.py:623
  271.3 26.1 %collective-permute-start.14 = (bf16[2,576,1152]{2,1,0:T(8,128)(2,1)}, bf16[2,576,1152]{2,1,0:T(8,128)(2,1)S(1)}, u32[]{:S(2)}, u32[]{:S(2)}) collective-permute-start(bf16[2,576,1152]{2,1,0:T(8,128)(2,1)} %get-tuple-element.134), channel_id=1, source_target_pairs={{0,4},{4,0},{8,12},{12,8},{16,20},{20,16},{24,28},{28,24},{1,5},{5... | collective-permute-start | bytes 7962632 | tf_op jit(solution)/shard_map/ppermute | solution.py:623
  276.8 25.6 %collective-permute-start.10 = (bf16[2,144,1152]{2,1,0:T(8,128)(2,1)}, bf16[2,144,1152]{2,1,0:T(8,128)(2,1)S(1)}, u32[]{:S(2)}, u32[]{:S(2)}) collective-permute-start(bf16[2,144,1152]{2,1,0:T(8,128)(2,1)} %pad_maximum_fusion.6), channel_id=1, source_target_pairs={{0,8},{4,12},{8,0},{12,4},{16,24},{20,28},{24,16},{28,20},{1,9},{5... | collective-permute-start | bytes 1990664 | tf_op jit(solution)/shard_map/ppermute | solution.py:623
  279.6 22.9 %collective-permute-start.11 = (bf16[2,144,1152]{2,1,0:T(8,128)(2,1)}, bf16[2,144,1152]{2,1,0:T(8,128)(2,1)S(1)}, u32[]{:S(2)}, u32[]{:S(2)}) collective-permute-start(bf16[2,144,1152]{2,1,0:T(8,128)(2,1)} %pad_maximum_fusion.7), channel_id=1, source_target_pairs={{0,16},{4,20},{8,24},{12,28},{16,0},{20,4},{24,8},{28,12},{1,17},{... | collective-permute-start | bytes 1990664 | tf_op jit(solution)/shard_map/ppermute | solution.py:623
  296.9 35.3 %collective-permute-start.17 = (bf16[1,576,1152]{2,1,0:T(8,128)(2,1)S(1)}, bf16[1,576,1152]{2,1,0:T(8,128)(2,1)S(1)}, u32[]{:S(2)}, u32[]{:S(2)}) collective-permute-start(bf16[1,576,1152]{2,1,0:T(8,128)(2,1)S(1)} %get-tuple-element.137), channel_id=1, source_target_pairs={{0,4},{4,0},{8,12},{12,8},{16,20},{20,16},{24,28},{28,24},{1,5},{5... | collective-permute-start | bytes 3981320 | tf_op jit(solution)/shard_map/ppermute | solution.py:623
  298.2 27.2 %collective-permute-start.15 = (bf16[2,144,1152]{2,1,0:T(8,128)(2,1)S(1)}, bf16[2,144,1152]{2,1,0:T(8,128)(2,1)S(1)}, u32[]{:S(2)}, u32[]{:S(2)}) collective-permute-start(bf16[2,144,1152]{2,1,0:T(8,128)(2,1)S(1)} %pad_maximum_fusion.8), channel_id=1, source_target_pairs={{0,8},{4,12},{8,0},{12,4},{16,24},{20,28},{24,16},{28,20},{1,9},{5... | collective-permute-start | bytes 1990664 | tf_op jit(solution)/shard_map/ppermute | solution.py:623
  302.0 27.3 %collective-permute-start.16 = (bf16[2,144,1152]{2,1,0:T(8,128)(2,1)}, bf16[2,144,1152]{2,1,0:T(8,128)(2,1)S(1)}, u32[]{:S(2)}, u32[]{:S(2)}) collective-permute-start(bf16[2,144,1152]{2,1,0:T(8,128)(2,1)} %pad_maximum_fusion.9), channel_id=1, source_target_pairs={{0,16},{4,20},{8,24},{12,28},{16,0},{20,4},{24,8},{28,12},{1,17},{... | collective-permute-start | bytes 1990664 | tf_op jit(solution)/shard_map/ppermute | solution.py:623
  305.0 31.3 %collective-permute-start.13 = (bf16[1,144,1152]{2,1,0:T(8,128)(2,1)}, bf16[1,144,1152]{2,1,0:T(8,128)(2,1)S(1)}, u32[]{:S(2)}, u32[]{:S(2)}) collective-permute-start(bf16[1,144,1152]{2,1,0:T(8,128)(2,1)} %fusion.40), channel_id=1, source_target_pairs={{0,16},{4,20},{8,24},{12,28},{16,0},{20,4},{24,8},{28,12},{1,17},{... | collective-permute-start | bytes 995336 | tf_op jit(solution)/shard_map/ppermute | solution.py:623
  306.6 30.3 %collective-permute-start.12 = (bf16[1,144,1152]{2,1,0:T(8,128)(2,1)}, bf16[1,144,1152]{2,1,0:T(8,128)(2,1)S(1)}, u32[]{:S(2)}, u32[]{:S(2)}) collective-permute-start(bf16[1,144,1152]{2,1,0:T(8,128)(2,1)} %fusion.39), channel_id=1, source_target_pairs={{0,8},{4,12},{8,0},{12,4},{16,24},{20,28},{24,16},{28,20},{1,9},{5... | collective-permute-start | bytes 995336 | tf_op jit(solution)/shard_map/ppermute | solution.py:623
  330.3 29.9 %collective-permute-start.20 = (bf16[1,144,1152]{2,1,0:T(8,128)(2,1)S(1)}, bf16[1,144,1152]{2,1,0:T(8,128)(2,1)S(1)}, u32[]{:S(2)}, u32[]{:S(2)}) collective-permute-start(bf16[1,144,1152]{2,1,0:T(8,128)(2,1)S(1)} %fusion.42), channel_id=1, source_target_pairs={{0,16},{4,20},{8,24},{12,28},{16,0},{20,4},{24,8},{28,12},{1,17},{... | collective-permute-start | bytes 995336 | tf_op jit(solution)/shard_map/ppermute | solution.py:623
  332.2 29.8 %collective-permute-start.19 = (bf16[1,144,1152]{2,1,0:T(8,128)(2,1)S(1)}, bf16[1,144,1152]{2,1,0:T(8,128)(2,1)S(1)}, u32[]{:S(2)}, u32[]{:S(2)}) collective-permute-start(bf16[1,144,1152]{2,1,0:T(8,128)(2,1)S(1)} %fusion.41), channel_id=1, source_target_pairs={{0,8},{4,12},{8,0},{12,4},{16,24},{20,28},{24,16},{28,20},{1,9},{5... | collective-permute-start | bytes 995336 | tf_op jit(solution)/shard_map/ppermute | solution.py:623
  332.3 29.8 %collective-permute-start.22 = (bf16[1,576,1152]{2,1,0:T(8,128)(2,1)S(1)}, bf16[1,576,1152]{2,1,0:T(8,128)(2,1)S(1)}, u32[]{:S(2)}, u32[]{:S(2)}) collective-permute-start(bf16[1,576,1152]{2,1,0:T(8,128)(2,1)S(1)} %get-tuple-element.149), channel_id=1, source_target_pairs={{0,4},{4,0},{8,12},{12,8},{16,20},{20,16},{24,28},{28,24},{1,5},{5... | collective-permute-start | bytes 3981320 | tf_op jit(solution)/shard_map/ppermute | solution.py:623
  336.3 22.3 %collective-permute-start.21 = (bf16[2,144,1152]{2,1,0:T(8,128)(2,1)S(1)}, bf16[2,144,1152]{2,1,0:T(8,128)(2,1)S(1)}, u32[]{:S(2)}, u32[]{:S(2)}) collective-permute-start(bf16[2,144,1152]{2,1,0:T(8,128)(2,1)S(1)} %pad_maximum_fusion.10), channel_id=1, source_target_pairs={{0,8},{4,12},{8,0},{12,4},{16,24},{20,28},{24,16},{28,20},{1,9},{5... | collective-permute-start | bytes 1990664 | tf_op jit(solution)/shard_map/ppermute | solution.py:623
  354.2 23.3 %collective-permute-start.28 = (bf16[144,1152]{1,0:T(8,128)(2,1)S(1)}, bf16[144,1152]{1,0:T(8,128)(2,1)S(1)}, u32[]{:S(2)}, u32[]{:S(2)}) collective-permute-start(bf16[144,1152]{1,0:T(8,128)(2,1)S(1)} %fusion.14), channel_id=1, source_target_pairs={{0,3},{1,0},{2,1},{3,2},{4,7},{5,4},{6,5},{7,6},{8,11},{9,8},{10,9... | collective-permute-start | bytes 995336 | tf_op jit(solution)/shard_map/ppermute | solution.py:619
  358.6 38.6 %collective-permute-start.18 = (bf16[1,576,1152]{2,1,0:T(8,128)(2,1)}, bf16[1,576,1152]{2,1,0:T(8,128)(2,1)}, u32[]{:S(2)}, u32[]{:S(2)}) collective-permute-start(bf16[1,576,1152]{2,1,0:T(8,128)(2,1)} %get-tuple-element.141), channel_id=1, source_target_pairs={{0,4},{4,0},{8,12},{12,8},{16,20},{20,16},{24,28},{28,24},{1,5},{5... | collective-permute-start | bytes 3981320 | tf_op jit(solution)/shard_map/ppermute | solution.py:623
  360.3 25.2 %collective-permute-start.26 = (bf16[1,144,1152]{2,1,0:T(8,128)(2,1)}, bf16[1,144,1152]{2,1,0:T(8,128)(2,1)}, u32[]{:S(2)}, u32[]{:S(2)}) collective-permute-start(bf16[1,144,1152]{2,1,0:T(8,128)(2,1)} %fusion.44), channel_id=1, source_target_pairs={{0,16},{4,20},{8,24},{12,28},{16,0},{20,4},{24,8},{28,12},{1,17},{... | collective-permute-start | bytes 995336 | tf_op jit(solution)/shard_map/ppermute | solution.py:623
  382.3 37.5 %collective-permute-start.29 = (bf16[144,1152]{1,0:T(8,128)(2,1)}, bf16[144,1152]{1,0:T(8,128)(2,1)S(1)}, u32[]{:S(2)}, u32[]{:S(2)}) collective-permute-start(bf16[144,1152]{1,0:T(8,128)(2,1)} %fusion.10), channel_id=1, source_target_pairs={{0,3},{1,0},{2,1},{3,2},{4,7},{5,4},{6,5},{7,6},{8,11},{9,8},{10,9... | collective-permute-start | bytes 995336 | tf_op jit(solution)/shard_map/ppermute | solution.py:619
  386.9 32.9 %collective-permute-start.27 = (bf16[144,1152]{1,0:T(8,128)(2,1)S(1)}, bf16[144,1152]{1,0:T(8,128)(2,1)S(1)}, u32[]{:S(2)}, u32[]{:S(2)}) collective-permute-start(bf16[144,1152]{1,0:T(8,128)(2,1)S(1)} %fusion.17), channel_id=1, source_target_pairs={{0,3},{1,0},{2,1},{3,2},{4,7},{5,4},{6,5},{7,6},{8,11},{9,8},{10,9... | collective-permute-start | bytes 995336 | tf_op jit(solution)/shard_map/ppermute | solution.py:619
  398.5 21.3 %collective-permute-start.25 = (bf16[1,144,1152]{2,1,0:T(8,128)(2,1)S(1)}, bf16[1,144,1152]{2,1,0:T(8,128)(2,1)S(1)}, u32[]{:S(2)}, u32[]{:S(2)}) collective-permute-start(bf16[1,144,1152]{2,1,0:T(8,128)(2,1)S(1)} %fusion.43), channel_id=1, source_target_pairs={{0,8},{4,12},{8,0},{12,4},{16,24},{20,28},{24,16},{28,20},{1,9},{5... | collective-permute-start | bytes 995336 | tf_op jit(solution)/shard_map/ppermute | solution.py:623
  400.3 21.6 %collective-permute-start.23 = (bf16[2,144,1152]{2,1,0:T(8,128)(2,1)S(1)}, bf16[2,144,1152]{2,1,0:T(8,128)(2,1)S(1)}, u32[]{:S(2)}, u32[]{:S(2)}) collective-permute-start(bf16[2,144,1152]{2,1,0:T(8,128)(2,1)S(1)} %pad_maximum_fusion.11), channel_id=1, source_target_pairs={{0,8},{4,12},{8,0},{12,4},{16,24},{20,28},{24,16},{28,20},{1,9},{5... | collective-permute-start | bytes 1990664 | tf_op jit(solution)/shard_map/ppermute | solution.py:623
  402.4 39.7 %collective-permute-start.31 = (bf16[2,144,1152]{2,1,0:T(8,128)(2,1)S(1)}, bf16[2,144,1152]{2,1,0:T(8,128)(2,1)}, u32[]{:S(2)}, u32[]{:S(2)}) collective-permute-start(bf16[2,144,1152]{2,1,0:T(8,128)(2,1)S(1)} %pad_maximum_fusion.13), channel_id=1, source_target_pairs={{0,16},{4,20},{8,24},{12,28},{16,0},{20,4},{24,8},{28,12},{1,17},{... | collective-permute-start | bytes 1990664 | tf_op jit(solution)/shard_map/ppermute | solution.py:623
  443.5 18.7 %collective-permute-start.34 = (bf16[1,144,1152]{2,1,0:T(8,128)(2,1)S(1)}, bf16[1,144,1152]{2,1,0:T(8,128)(2,1)S(1)}, u32[]{:S(2)}, u32[]{:S(2)}) collective-permute-start(bf16[1,144,1152]{2,1,0:T(8,128)(2,1)S(1)} %fusion.45), channel_id=1, source_target_pairs={{0,16},{4,20},{8,24},{12,28},{16,0},{20,4},{24,8},{28,12},{1,17},{... | collective-permute-start | bytes 995336 | tf_op jit(solution)/shard_map/ppermute | solution.py:623
  445.2 18.0 %collective-permute-start.38 = (bf16[144,1152]{1,0:T(8,128)(2,1)S(1)}, bf16[144,1152]{1,0:T(8,128)(2,1)S(1)}, u32[]{:S(2)}, u32[]{:S(2)}) collective-permute-start(bf16[144,1152]{1,0:T(8,128)(2,1)S(1)} %fusion.6), channel_id=1, source_target_pairs={{0,3},{1,0},{2,1},{3,2},{4,7},{5,4},{6,5},{7,6},{8,11},{9,8},{10,9... | collective-permute-start | bytes 995336 | tf_op jit(solution)/shard_map/ppermute | solution.py:619
  (114 other events, 1536.0 us)
Sparse Core Ops, SparseCore 0:
  11.4 115.7 all-gather.3
  130.0 85.7 all-gather.5
  221.9 163.6 reduce-scatter.1
